TPU v7x, 32 devices: a whole 2x2x4 slice. The times are simulated.
32 devices in a mesh: grp: 2 (over x), rows: 8 (over z, core), cols: 2 (over y).
Axes of the slice: x: 2, y: 2, z: 4, core: 2. Of those that a mesh axis runs over, the one named last changes fastest.
Arguments:
- band_vectors: float32 [49152, 1024], P('rows'), may hold values from -6 to 6
- coulomb: float32 [49152], P('rows'), may hold values from 0.1 to 10
- pair_weight: float32 [1536], replicated, may hold values from 0.25 to 4
- occ_index: int32 [1536], replicated, may hold values from 0 to 255
- vir_index: int32 [1536], replicated, may hold values from 256 to 1023
- freq_index: int32 [1024], replicated, may hold values from 0 to 15
- freq_table: float32 [16], replicated, may hold values from 0.3 to 3
Outputs:
- self_energy: float32 [1024, 1024], P(('rows', 'cols'), 'grp')
Inputs may be any that keep to these rules, and one draw needn't show every extreme that they name: `occ_index`: every pair's occupied band lies below 256. `vir_index`: every pair's empty band lies at 256 or above.
All inputs are finite; a program needn't handle non-finite values.
Results may differ from a plain program's by a relative error of at most 0.0001.
Values sent between devices are 32-bit elements; how exact they have to be, the bound alone decides.
No kernel may reach another device: no remote copies, remote signals or barrier semaphores. Data moves between devices by JAX's collectives and lax.ppermute only.
A program may use at most 192 MiB of HBM per device.

v0:
```python
import math

import jax
import jax.numpy as jnp
from jax import lax
from jax.sharding import PartitionSpec as P

NB = 49152
PANEL = 512


def per_device(band_vectors, coulomb, pair_weight, occ_index, vir_index, freq_index, freq_table):
    highest = lax.Precision.HIGHEST
    row_count = lax.axis_size("rows")
    col_count = lax.axis_size("cols")
    group_count = lax.axis_size("grp")
    column = lax.axis_index("cols")
    group = lax.axis_index("grp")
    basis_rows = band_vectors.shape[0]
    band_total = band_vectors.shape[1]
    pair_cols = (
        jnp.take(band_vectors, occ_index, axis=1)
        * jnp.take(band_vectors, vir_index, axis=1)
        * pair_weight[None, :]
    )
    table_size = freq_table.shape[0]
    matches = freq_index[:, None] == jnp.arange(table_size, dtype=jnp.int32)[None, :]
    band_weight = jnp.sum(jnp.where(matches, freq_table[None, :], 0.0), axis=1)
    quarter = PANEL // col_count
    panel_start = group * PANEL + column * quarter
    weighted = lax.dynamic_slice_in_dim(pair_cols, panel_start, quarter, 1) * coulomb[:, None]
    partial_response = lax.dot_general(
        pair_cols,
        weighted,
        (((0,), (0,)), ((), ())),
        precision=highest,
        preferred_element_type=jnp.float32,
    )
    response = lax.psum(partial_response, "rows") * (1.0 / NB)
    band_rows = band_total // (row_count * col_count)
    half_rows = band_rows // group_count
    shaped = band_vectors.reshape(basis_rows, row_count, col_count, group_count, half_rows)
    chosen = lax.dynamic_index_in_dim(shaped, column, 2, keepdims=False)
    chosen = lax.dynamic_index_in_dim(chosen, group, 2, keepdims=False).reshape(
        basis_rows, row_count * half_rows
    )
    shaped_weight = band_weight.reshape(row_count, col_count, group_count, half_rows)
    chosen_weight = lax.dynamic_index_in_dim(shaped_weight, column, 1, keepdims=False)
    chosen_weight = lax.dynamic_index_in_dim(chosen_weight, group, 1, keepdims=False).reshape(
        row_count * half_rows
    )
    band_cols = chosen * coulomb[:, None] * chosen_weight[None, :]
    own_half = lax.psum_scatter(
        lax.dot_general(
            band_cols,
            pair_cols,
            (((0,), (0,)), ((), ())),
            precision=highest,
            preferred_element_type=jnp.float32,
        ),
        "rows",
        scatter_dimension=0,
        tiled=True,
    ) * (1.0 / math.sqrt(NB))
    coupling = lax.all_gather(own_half, "grp", axis=0, tiled=True)
    panel_response = lax.all_gather(response, "cols", axis=1, tiled=True)
    mixed_rows = jnp.dot(
        coupling, panel_response, precision=highest, preferred_element_type=jnp.float32
    )
    own_panel = lax.dynamic_slice_in_dim(coupling, group * PANEL, PANEL, 1)
    partial_energy = lax.dot_general(
        mixed_rows,
        lax.all_gather(own_panel, ("rows", "cols"), axis=0, tiled=True),
        (((1,), (1,)), ((), ())),
        precision=highest,
        preferred_element_type=jnp.float32,
    )
    scale = 1.0 / math.sqrt(PANEL * group_count)
    return lax.psum_scatter(partial_energy * scale, "grp", scatter_dimension=1, tiled=True)


def solution(mesh):
    placed = (P("rows", None), P("rows"), P(), P(), P(), P(), P())
    return jax.shard_map(
        per_device,
        mesh=mesh,
        in_specs=placed,
        out_specs=P(("rows", "cols"), "grp"),
        check_vma=False,
    )
```

profile of v0, /device:TPU:8, one launch (start us, length us, event | category | flops | bytes accessed | tf_op | source)
XLA Modules:
  0.0 394.7 jit_solution(15016719837879977791)
XLA Ops:
  6.5 0.7 compare_select_fusion.1
  7.2 0.7 compare_select_fusion
  7.9 1.3 compare_and_fusion
  9.2 24.7 %copy.14 = f32[6144,1024]{0,1:T(8,128)} copy(f32[6144,1024]{1,0:T(8,128)} %param.9) | data formatting | bytes 50331648 | tf_op args[0]
  33.9 39.6 %gather_fusion = f32[1536,6144]{1,0:T(8,128)} fusion(f32[6144,1024]{0,1:T(8,128)} %copy.14, s32[2048]{0:T(1024)S(1)} %pad_clamp_fusion.1), kind=kCustom, calls=%fused_computation.clone | custom fusion | bytes 75503616 | tf_op jit(solution)/shard_map/jit(_take)/gather | solution.py:22
  73.5 39.5 %gather_fusion.1 = f32[1536,6144]{1,0:T(8,128)} fusion(f32[6144,1024]{0,1:T(8,128)} %copy.14, s32[2048]{0:T(1024)S(1)} %pad_clamp_fusion), kind=kCustom, calls=%fused_computation.1.clone | custom fusion | bytes 75503616 | tf_op jit(solution)/shard_map/jit(_take)/gather | solution.py:23
  113.1 37.6 %fusion = f32[6144,1536]{0,1:T(8,128)} fusion(f32[1536,6144]{1,0:T(8,128)} %gather_fusion.1, f32[1536,6144]{1,0:T(8,128)} %gather_fusion, f32[1536]{0:T(1024)S(1)} %copy-done.1, pred[1536]{0:T(1024)(128)(4,1)S(1)} %copy-done.2, pred[1536]{0:T(1024)(128)(4,1)S(1)} %copy-done.3), kind=kLoop, calls=%fused_computation.3 | loop fusion | flops 37748736 | bytes 113255424 | tf_op jit(solution)/shard_map/mul | solution.py:22
  150.7 35.4 %fusion.2 = f32[1536,256]{1,0:T(8,128)} fusion(f32[6144,1536]{0,1:T(8,128)} %fusion, s32[]{:T(128)S(6)} %select_n.38, f32[6144]{0:T(1024)S(1)} %copy-done), kind=kOutput, calls=%fused_computation.6 | convolution fusion | flops 28992602112 | bytes 45637636 | tf_op jit(solution)/shard_map/dot_general | solution.py:32
  186.3 0.1 select_reduce_fusion
  186.5 6.1 %constant_dynamic-slice_fusion.1 = f32[6144,8,1,1,32]{0,4,3,2,1:T(8,128)} fusion(f32[6144,8,2,2,32]{0,4,3,2,1:T(8,128)} %bitcast.18, s32[]{:T(128)S(6)} %select_n.34, s32[]{:T(128)S(6)} %select_n.36), kind=kLoop, calls=%fused_computation.24 | loop fusion | bytes 12582920 | tf_op jit(solution)/shard_map/jit(dynamic_index_in_dim)/dynamic_slice | solution.py:44
  192.7 3.6 fusion.1
  196.3 35.0 %fusion.7 = f32[256,1536]{1,0:T(8,128)} fusion(f32[6144,256]{0,1:T(8,128)S(1)} %fusion.1, f32[6144,1536]{0,1:T(8,128)} %fusion), kind=kOutput, calls=%fused_computation.25 | convolution fusion | flops 28991029248 | bytes 45613056 | tf_op jit(solution)/shard_map/dot_general | solution.py:54
  231.4 17.3 %all-reduce.2.cloned.1.call-done = f32[1536,256]{1,0:T(8,128)} async-done(((f32[1536,256]{1,0:T(8,128)}), f32[1536,256]{1,0:T(8,128)}) %all-reduce.2.cloned.1.call-update) | async-done | bytes 1572880 | tf_op jit(solution)/shard_map/psum | solution.py:39
  248.6 2.8 broadcast_multiply_fusion
  251.5 29.7 %reduce-scatter.3.cloned.1.call-done = f32[32,1536]{1,0:T(8,128)} async-done(((f32[256,1536]{1,0:T(8,128)}), f32[32,1536]{1,0:T(8,128)}) %reduce-scatter.3.cloned.1.call-update) | async-done | bytes 196624 | tf_op jit(solution)/shard_map/reduce_scatter | solution.py:53
  281.2 0.9 broadcast_multiply_fusion.1
  282.1 6.3 %all_gather.9 = f32[64,1536]{1,0:T(8,128)S(1)} all-gather(f32[32,1536]{1,0:T(8,128)S(1)} %broadcast_multiply_fusion.1), channel_id=1, replica_groups=mesh['grp'=2,'rows'=8,'cols'=2] {'grp'}, dimensions={0}, use_global_device_ids=true | all-gather | bytes 589824 | tf_op jit(solution)/shard_map/all_gather | solution.py:65
  288.4 0.7 constant_dynamic-slice_fusion
  289.1 0.3 reduce-scatter.5.cloned.1.call-start
  289.4 40.2 %all-gather.3.cloned.1.call-done = f32[1536,512]{1,0:T(8,128)} async-done(((f32[1536,256]{1,0:T(8,128)}), f32[1536,512]{1,0:T(8,128)}) %all-gather.3.cloned.1.call-update) | async-done | bytes 3145744 | tf_op jit(solution)/shard_map/all_gather | solution.py:66
  329.6 3.9 fusion.8
  333.5 38.6 %all-gather.5.cloned.1.call-done = f32[1024,512]{1,0:T(8,128)} async-done(((f32[64,512]{1,0:T(8,128)}), f32[1024,512]{1,0:T(8,128)}) %all-gather.5.cloned.1.call-update) | async-done | bytes 2097168 | tf_op jit(solution)/shard_map/all_gather | solution.py:73
  372.2 4.4 %convolution_multiply_fusion = f32[64,1024]{1,0:T(8,128)} fusion(f32[64,512]{1,0:T(8,128)S(1)} %fusion.8, f32[1024,512]{1,0:T(8,128)} %all-gather.5.cloned.1.call-done), kind=kOutput, calls=%fused_computation.10 | convolution fusion | flops 402718720 | bytes 2490368 | tf_op jit(solution)/shard_map/dot_general | solution.py:71
  376.6 11.5 %reduce-scatter.5.cloned.1.call-done = f32[64,512]{1,0:T(8,128)} async-done(((f32[64,1024]{1,0:T(8,128)}), f32[64,512]{1,0:T(8,128)}) %reduce-scatter.5.cloned.1.call-update) | async-done | bytes 131088 | tf_op jit(solution)/shard_map/reduce_scatter | solution.py:79
  (26 shorter events, 0.4 us)
Async XLA Ops:
  6.5 242.1 %all-reduce.2.cloned.1.call-start = ((), (), s32[]{:S(2)}) async-start(), calls=%async_computation.3 | async-start | bytes 3145728 | tf_op jit(solution)/shard_map/psum | solution.py:39
  73.5 39.5 %copy-start.1 = (f32[1536]{0:T(1024)S(1)}, f32[1536]{0:T(1024)}, u32[]{:S(2)}) copy-start(f32[1536]{0:T(1024)} %param.11) | copy-start | bytes 18436
  73.5 39.5 %copy-start.2 = (pred[1536]{0:T(1024)(128)(4,1)S(1)}, pred[1536]{0:T(1024)(128)(4,1)}, u32[]{:S(2)}) copy-start(pred[1536]{0:T(1024)(128)(4,1)} %get-tuple-element.6) | copy-start | bytes 4612
  73.5 39.5 %copy-start.3 = (pred[1536]{0:T(1024)(128)(4,1)S(1)}, pred[1536]{0:T(1024)(128)(4,1)}, u32[]{:S(2)}) copy-start(pred[1536]{0:T(1024)(128)(4,1)} %get-tuple-element.7) | copy-start | bytes 4612
  113.1 37.7 %copy-start = (f32[6144]{0:T(1024)S(1)}, f32[6144]{0:T(1024)}, u32[]{:S(2)}) copy-start(f32[6144]{0:T(1024)} %param.10) | copy-start | bytes 73732
  150.7 35.5 %copy-start.4 = (s32[1024]{0:T(1024)S(1)}, s32[1024]{0:T(1024)}, u32[]{:S(2)}) copy-start(s32[1024]{0:T(1024)} %param.14) | copy-start | bytes 12292
  150.7 35.6 %copy-start.5 = (f32[16]{0:T(128)S(1)}, f32[16]{0:T(128)}, u32[]{:S(2)}) copy-start(f32[16]{0:T(128)} %param.15) | copy-start | bytes 196
  186.2 94.9 %reduce-scatter.3.cloned.1.call-start = ((), (), s32[]{:S(2)}) async-start(), calls=%async_computation.2 | async-start | bytes 1769472 | tf_op jit(solution)/shard_map/reduce_scatter | solution.py:53
  231.3 98.3 %all-gather.3.cloned.1.call-start = ((), (), s32[]{:S(2)}) async-start(), calls=%async_computation.4 | async-start | bytes 4718592 | tf_op jit(solution)/shard_map/all_gather | solution.py:66
  251.4 120.7 %all-gather.5.cloned.1.call-start = ((), (), s32[]{:S(2)}) async-start(), calls=%async_computation.5 | async-start | bytes 2228224 | tf_op jit(solution)/shard_map/all_gather | solution.py:73
  289.1 99.0 %reduce-scatter.5.cloned.1.call-start = ((), (), s32[]{:S(2)}) async-start(), calls=%async_computation.6 | async-start | bytes 393216 | tf_op jit(solution)/shard_map/reduce_scatter | solution.py:79
Sparse Core Ops, SparseCore 0:
  186.3 62.2 all-reduce.1
  250.9 30.1 reduce-scatter.2
  282.7 46.8 all-gather.2
  331.7 40.4 all-gather.4
  376.7 11.3 reduce-scatter.4
where the time goes:
time: 397 us; the launch traced here: 395 us
  waiting for transfers between devices  137 us (35%)
  local copies, waits for them, and re-layouts  111 us (28%)
  matrix products  78.8 us (20%)
  other arithmetic  47.8 us (12%)
  between operations  13.2 us (3%)
  blocking collectives  6.35 us (2%)
    all_gather x1, waiting for transfers between devices, per_device(): panel_response = lax.all_gather(response, 'cols', axis=1, tiled=True)  40.2 us
    gather x1, local copies, waits for them, and re-layouts, per_device(): jnp.take(band_vectors, occ_index, axis=1)  39.6 us
    gather x1, local copies, waits for them, and re-layouts, per_device(): jnp.take(band_vectors, vir_index, axis=1)  39.5 us
    all_gather x1, waiting for transfers between devices, per_device(): lax.all_gather(own_panel, ('rows', 'cols'), axis=0, tiled=True)  38.6 us
    mul x1, other arithmetic, per_device(): jnp.take(band_vectors, occ_index, axis=1)  37.6 us
    dot_general x1, matrix products, per_device(): lax.dot_general(pair_cols, weighted, (((0,), (0,)), ((), ())), precision=...  35.4 us
    dot_general x1, matrix products, per_device(): lax.dot_general(band_cols, pair_cols, (((0,), (0,)), ((), ())), precision...  35 us
    reduce_scatter x1, waiting for transfers between devices, per_device(): lax.psum_scatter(lax.dot_general(band_cols, pair_cols, (((0,), (0,)), (()...  29.7 us
  transfers between devices with their start and end apart: 5, of which 5 were waited for; matrix products, arithmetic and copies ran while one was open for 13% of the time, Pallas kernels for 0%

commit v1 on v0

v1 whole, which is shorter than its diff:
```python
import math

import jax
import jax.numpy as jnp
from jax import lax
from jax.experimental import pallas as pl
from jax.experimental.pallas import tpu as pltpu
from jax.sharding import PartitionSpec as P

PANEL = 512
LANES = 128
PAIR_BLOCK = 256
GATHER_BLOCK = 128
VMEM_BYTES = 60 * 2**20


def split(value):
    high = value.astype(jnp.bfloat16)
    return high, (value - high.astype(jnp.float32)).astype(jnp.bfloat16)


def three_pass(left_high, left_low, right_high, right_low):
    def dot(left, right):
        return jnp.dot(left, right, preferred_element_type=jnp.float32)

    return dot(left_high, right_high) + (dot(left_low, right_high) + dot(left_high, right_low))


def coupling_kernel(
    block_ref, occ_ref, vir_ref, occ_own_ref, vir_own_ref, coulomb_ref, band_ref,
    high_ref, low_ref, coupling_ref, own_high_ref, own_low_ref,
    turned, products, band_high, band_low, incoming, arrived,
):
    step = pl.program_id(0)
    bands = band_ref.shape[1]
    basis_rows = band_ref.shape[0]
    groups = basis_rows // LANES
    stride = turned.shape[0] // bands
    piece = incoming.shape[1]
    width = band_high.shape[1]
    pieces = basis_rows // piece
    batch = products.shape[0] // stride

    def gather(occ, vir, first):
        @pl.loop(0, batch, unroll=4)
        def _(pair):
            left = occ[first + pair] * stride
            right = vir[first + pair] * stride
            products[pl.ds(pair * stride, groups), :] = (
                turned[pl.ds(left, groups), :] * turned[pl.ds(right, groups), :]
            )

    def weight(group):
        return coulomb_ref[group : group + 1, :]

    @pl.when(step == 0)
    def _():
        def fetch(index):
            return pltpu.make_async_copy(
                band_ref.at[pl.ds(index * piece, piece), :],
                incoming.at[index % 2],
                arrived.at[index % 2],
            )

        own_bands = pl.ds(pl.multiple_of(block_ref[0] * width, LANES), width)
        fetch(0).start()
        for index in range(pieces):
            if index + 1 < pieces:
                fetch(index + 1).start()
            fetch(index).wait()
            for part in range(piece // LANES):
                group = index * (piece // LANES) + part
                rows = pl.ds(part * LANES, LANES)
                turned[pl.ds(group, bands, stride=stride), :] = incoming[index % 2, rows, :].T
                column = jnp.broadcast_to(weight(group), (LANES, LANES)).T
                own = incoming[index % 2, rows, own_bands]
                own = own * jnp.concatenate([column] * (width // LANES), axis=1)
                here = pl.ds(group * LANES, LANES)
                band_high[here, :], band_low[here, :] = split(own)
        for first in range(0, own_high_ref.shape[1], batch):
            gather(occ_own_ref, vir_own_ref, first)
            for group in range(groups):
                own = products[pl.ds(group, batch, stride=stride), :] * weight(group)
                here = pl.ds(group * LANES, LANES)
                there = pl.ds(first, batch)
                own_high_ref[here, there], own_low_ref[here, there] = split(own.T)

    for first in range(0, high_ref.shape[0], batch):
        gather(occ_ref, vir_ref, step * high_ref.shape[0] + first)
        for group in range(groups):
            here = pl.ds(first, batch)
            there = pl.ds(group * LANES, LANES)
            high_ref[here, there], low_ref[here, there] = split(
                products[pl.ds(group, batch, stride=stride), :]
            )
    coupling_ref[...] = three_pass(high_ref[...], low_ref[...], band_high[...], band_low[...])


def pair_coupling(band_vectors, coulomb, occ, vir, occ_own, vir_own, block, width):
    basis_rows, bands = band_vectors.shape
    pairs = occ.shape[0]
    own = occ_own.shape[0]
    groups = basis_rows // LANES
    stride = groups + 1 - groups % 2
    piece = min(256, basis_rows)
    scalars = pl.BlockSpec(memory_space=pltpu.SMEM)
    whole = pl.BlockSpec((basis_rows, own), lambda i: (0, 0), pipeline_mode=pl.Buffered(1))
    rows = pl.BlockSpec((PAIR_BLOCK, basis_rows), lambda i: (i, 0))
    half = jnp.bfloat16
    return pl.pallas_call(
        coupling_kernel,
        grid=(pairs // PAIR_BLOCK,),
        in_specs=[scalars] * 5
        + [pl.BlockSpec((groups, LANES), lambda i: (0, 0)), pl.BlockSpec(memory_space=pl.ANY)],
        out_specs=[rows, rows, pl.BlockSpec((PAIR_BLOCK, width), lambda i: (i, 0)), whole, whole],
        out_shape=[
            jax.ShapeDtypeStruct((pairs, basis_rows), half),
            jax.ShapeDtypeStruct((pairs, basis_rows), half),
            jax.ShapeDtypeStruct((pairs, width), jnp.float32),
            jax.ShapeDtypeStruct((basis_rows, own), half),
            jax.ShapeDtypeStruct((basis_rows, own), half),
        ],
        scratch_shapes=[
            pltpu.VMEM((bands * stride, LANES), jnp.float32),
            pltpu.VMEM((GATHER_BLOCK * stride, LANES), jnp.float32),
            pltpu.VMEM((basis_rows, width), half),
            pltpu.VMEM((basis_rows, width), half),
            pltpu.VMEM((2, piece, bands), jnp.float32),
            pltpu.SemaphoreType.DMA((2,)),
        ],
        compiler_params=pltpu.CompilerParams(vmem_limit_bytes=VMEM_BYTES),
        cost_estimate=pl.CostEstimate(
            flops=6 * basis_rows * pairs * width,
            bytes_accessed=4 * basis_rows * (bands + pairs),
            transcendentals=0,
        ),
        name="coupling",
    )(
        block, occ, vir, occ_own, vir_own, coulomb.reshape(groups, LANES), band_vectors
    )


def response_kernel(high_ref, low_ref, own_high_ref, own_low_ref, response_ref):
    response_ref[...] = three_pass(
        high_ref[...], low_ref[...], own_high_ref[...], own_low_ref[...]
    )


def pair_response(high, low, own_high, own_low):
    pairs, basis_rows = high.shape
    own = own_high.shape[1]
    rows = pl.BlockSpec((PAIR_BLOCK, basis_rows), lambda i: (i, 0))
    whole = pl.BlockSpec((basis_rows, own), lambda i: (0, 0))
    return pl.pallas_call(
        response_kernel,
        grid=(pairs // PAIR_BLOCK,),
        in_specs=[rows, rows, whole, whole],
        out_specs=pl.BlockSpec((PAIR_BLOCK, own), lambda i: (i, 0)),
        out_shape=jax.ShapeDtypeStruct((pairs, own), jnp.float32),
        compiler_params=pltpu.CompilerParams(vmem_limit_bytes=VMEM_BYTES),
        cost_estimate=pl.CostEstimate(
            flops=6 * basis_rows * pairs * own,
            bytes_accessed=4 * basis_rows * (own + pairs),
            transcendentals=0,
        ),
        name="response",
    )(high, low, own_high, own_low)


def per_device(band_vectors, coulomb, pair_weight, occ_index, vir_index, freq_index, freq_table):
    row_count = lax.axis_size("rows")
    col_count = lax.axis_size("cols")
    group_count = lax.axis_size("grp")
    blocks = col_count * group_count
    lines = row_count // 2
    row = lax.axis_index("rows")
    core, line = lax.rem(row, 2), lax.div(row, 2)
    column = lax.axis_index("cols")
    group = lax.axis_index("grp")
    block = group * col_count + column
    basis_rows, bands = band_vectors.shape
    pairs = occ_index.shape[0]
    window = PANEL * group_count
    basis = basis_rows * row_count

    def ordered(values):
        def shares(part):
            return part.reshape(lines, 2, -1).swapaxes(0, 1)

        return jnp.concatenate([shares(values[:window]), shares(values[window:])], axis=2)

    def own_window(values):
        return lax.dynamic_index_in_dim(
            values[:window].reshape(row_count, blocks, -1), block, 1, keepdims=False
        ).reshape(-1)

    def pick(values, index, axis=0):
        return lax.dynamic_index_in_dim(values, index, axis, keepdims=False)

    other_core = [(i, i ^ 1) for i in range(row_count)]

    def shift(step):
        return [(i, (i // 2 + step) % lines * 2 + i % 2) for i in range(row_count)]

    def scatter_rows(values):
        received = lax.ppermute(pick(values, 1 - core), "rows", other_core)
        both = pick(values, core) + received
        total = pick(both, line)
        arrived = [
            lax.ppermute(pick(both, lax.rem(line + step, lines)), "rows", shift(step))
            for step in range(1, lines)
        ]
        for value in arrived:
            total = total + value
        return total

    def gather_blocks(values):
        across = [(i, i ^ 1) for i in range(col_count)]
        pair = jnp.stack([values, lax.ppermute(values, "cols", across)])
        pair = jnp.where(column == 0, pair, pair[::-1])
        across = [(i, i ^ 1) for i in range(group_count)]
        quad = jnp.stack([pair, lax.ppermute(pair, "grp", across)])
        quad = jnp.where(group == 0, quad, quad[::-1])
        return quad.reshape((blocks,) + values.shape)

    occ_own, vir_own = own_window(occ_index), own_window(vir_index)
    high, low, partial_coupling, own_high, own_low = pair_coupling(
        band_vectors, coulomb, ordered(occ_index).reshape(-1), ordered(vir_index).reshape(-1),
        occ_own, vir_own, block.reshape(1), bands // blocks,
    )
    partial_response = pair_response(high, low, own_high, own_low)

    share = pairs // row_count
    shaped = (2, lines, share, -1)
    weights = ordered(pair_weight)
    own_weights = pick(pick(weights, core), line)
    coupling = scatter_rows(partial_coupling.reshape(shaped))
    coupling = coupling * (own_weights[:, None] * (1.0 / math.sqrt(basis)))
    all_coupling = gather_blocks(coupling)
    all_coupling = all_coupling.swapaxes(0, 1).reshape(share, bands)
    sub = window // (row_count * blocks)
    part = lax.dynamic_slice_in_dim(all_coupling, block * sub, sub, 0)
    parts = [part] + [lax.ppermute(part, "rows", shift(step)) for step in range(1, lines)]
    parts = jnp.stack(parts)
    beside = lax.ppermute(parts, "rows", other_core)
    both = jnp.where(core == 0, jnp.stack([parts, beside], 1), jnp.stack([beside, parts], 1))
    both = jnp.roll(both[::-1], line + 1, axis=0)
    window_coupling = both.reshape(row_count * sub, bands)

    response = scatter_rows(partial_response.reshape(shaped))
    response = response * (
        own_weights[:, None] * own_window(pair_weight)[None, :] * (1.0 / basis)
    )
    matches = freq_index[:, None] == jnp.arange(freq_table.shape[0], dtype=jnp.int32)[None, :]
    band_weight = jnp.sum(jnp.where(matches, freq_table[None, :], 0.0), axis=1)
    mixed = lax.dot_general(
        all_coupling, response, (((0,), (0,)), ((), ())),
        precision=lax.Precision.HIGH, preferred_element_type=jnp.float32,
    )
    mixed = scatter_rows(mixed.reshape(lines, 2, bands // row_count, -1).swapaxes(0, 1))
    energy = lax.dot_general(
        mixed, window_coupling, (((1,), (0,)), ((), ())),
        precision=lax.Precision.HIGH, preferred_element_type=jnp.float32,
    )
    here = bands // row_count
    own_band_weight = lax.dynamic_slice_in_dim(band_weight, row * here, here, 0)
    energy = energy * (
        own_band_weight[:, None] * band_weight[None, :] * (1.0 / math.sqrt(window))
    )
    energy = energy.reshape(col_count, here // col_count, group_count, bands // group_count)
    across = [(i, i ^ 1) for i in range(col_count)]
    received = lax.ppermute(pick(energy, 1 - column), "cols", across)
    energy = pick(energy, column) + received
    across = [(i, i ^ 1) for i in range(group_count)]
    received = lax.ppermute(pick(energy, 1 - group, 1), "grp", across)
    return pick(energy, group, 1) + received


def solution(mesh):
    placed = (P("rows", None), P("rows"), P(), P(), P(), P(), P())
    return jax.shard_map(
        per_device,
        mesh=mesh,
        in_specs=placed,
        out_specs=P(("rows", "cols"), "grp"),
        check_vma=False,
    )
```

time: 397 us -> 188 us (0.47)
  local copies, waits for them, and re-layouts: 111 us -> 15.3 us
  Pallas kernels: 0 us -> 76.4 us
  matrix products: 78.8 us -> 3.66 us
  waiting for transfers between devices: 137 us -> 64.7 us
  other arithmetic: 47.8 us -> 5.8 us
  starting transfers between devices: 0.39 us -> 20.5 us
  between operations: 13.2 us -> 0.34 us
  blocking collectives: 6.35 us -> 0 us
    gather x2 -> x0, local copies, waits for them, and re-layouts: 79.1 us -> none  [the longest x1 39.6 us: per_device(): jnp.take(band_vectors, occ_index, axis=1)]
    all_gather x2 -> x0, waiting for transfers between devices: 78.9 us -> none  [the longest x1 40.2 us: per_device(): panel_response = lax.all_gather(response, 'cols', axis=1, tiled=True)]
    pallas_call x0 -> x2, Pallas kernels: none -> 76.4 us  [the longest x1 54.5 us: pair_coupling(): pl.pallas_call(coupling_kernel, grid=(pairs // PAIR_BLOCK,), in_specs=[sc...]
    dot_general x4 -> x2, matrix products: 78.8 us -> 3.66 us  [the longest x1 2.19 us: per_device(): lax.dot_general(all_coupling, response, (((0,), (0,)), ((), ())), precisi...]
    ppermute x0 -> x20, waiting for transfers between devices: none -> 64.7 us  [the longest x9 34.6 us: scatter_rows(): lax.ppermute(pick(both, lax.rem(line + step, lines)), 'rows', shift(step))]
    mul x4 -> x2, other arithmetic: 45 us -> 0.1 us  [per_device(): coupling = coupling * (own_weights[:, None] * (1.0 / math.sqrt(basis)))]
    reduce_scatter x2 -> x0, waiting for transfers between devices: 41.2 us -> none  [the longest x1 29.7 us: per_device(): lax.psum_scatter(lax.dot_general(band_cols, pair_cols, (((0,), (0,)), (()...]
    unnamed x13 -> x12, local copies, waits for them, and re-layouts: 24.7 us -> 0.22 us
  transfers between devices with their start and end apart: 5 -> 20, of which waited for: 5 -> 16; matrix products, arithmetic and copies ran while one was open for 13% -> 6% of each run, Pallas kernels for 0% -> 12%
where the time goes in v1:
time: 188 us; the launch traced here: 187 us
  Pallas kernels  76.4 us (41%)
  waiting for transfers between devices  64.7 us (34%)
  starting transfers between devices  20.5 us (11%)
  local copies, waits for them, and re-layouts  15.3 us (8%)
  other arithmetic  5.8 us (3%)
  matrix products  3.66 us (2%)
    pallas_call x1, Pallas kernels, pair_coupling(): pl.pallas_call(coupling_kernel, grid=(pairs // PAIR_BLOCK,), in_specs=[sc...  54.5 us
    ppermute x9, waiting for transfers between devices, scatter_rows(): lax.ppermute(pick(both, lax.rem(line + step, lines)), 'rows', shift(step))  34.6 us
    pallas_call x1, Pallas kernels, pair_response(): pl.pallas_call(response_kernel, grid=(pairs // PAIR_BLOCK,), in_specs=[ro...  21.9 us
    ppermute x3, waiting for transfers between devices, per_device(): lax.ppermute(part, 'rows', shift(step))  10.6 us
    ppermute x9, starting transfers between devices, scatter_rows(): lax.ppermute(pick(both, lax.rem(line + step, lines)), 'rows', shift(step))  10 us
    ppermute x1, waiting for transfers between devices, per_device(): received = lax.ppermute(pick(energy, 1 - column), 'cols', across)  6.72 us
    squeeze x7, local copies, waits for them, and re-layouts, pick(): return lax.dynamic_index_in_dim(values, index, axis, keepdims=False)  5.17 us
    ppermute x1, waiting for transfers between devices, gather_blocks(): pair = jnp.stack([values, lax.ppermute(values, 'cols', across)])  4.93 us
  transfers between devices with their start and end apart: 20, of which 16 were waited for; matrix products, arithmetic and copies ran while one was open for 6% of the time, Pallas kernels for 12%

profile of v1, /device:TPU:8, one launch (start us, length us, event | category | flops | bytes accessed | tf_op | source)
XLA Modules:
  0.0 186.7 jit_solution(8206094578867660983)
XLA Ops:
  5.8 54.5 %coupling.1 = (bf16[1536,6144]{1,0:T(8,128)(2,1)}, bf16[1536,6144]{1,0:T(8,128)(2,1)}, f32[1536,256]{1,0:T(8,128)}, bf16[6144,256]{1,0:T(8,128)(2,1)}, bf16[6144,256]{1,0:T(8,128)(2,1)}) custom-call(s32[1]{0:T(128)} %bitcast.block_ref, s32[1536]{0:T(1024)} %reshape.156.occ_ref, s32[1536]{0:T(1024)} %reshape.158.vir_ref, s32[256]{0:T(256)} %reshape.160.occ_own_ref, ...), custom_call_target="tpu_custom_call" | custom-call | flops 14495514624 | bytes 62914560 | tf_op jit(solution)/shard_map/coupling/pallas_call | solution.py:110
  61.6 21.9 %response.1 = f32[1536,256]{1,0:T(8,128)} custom-call(bf16[1536,6144]{1,0:T(8,128)(2,1)} %get-tuple-element.11.high_ref, bf16[1536,6144]{1,0:T(8,128)(2,1)} %get-tuple-element.12.low_ref, bf16[6144,256]{1,0:T(8,128)(2,1)} %get-tuple-element.13.own_high_ref, bf16[6144,256]{1,0:T(8,128)(2,1)} %get-tuple-element.14.own_low_ref), custom_call_target="tpu_custom_call" | custom-call | flops 14495514624 | bytes 44040192 | tf_op jit(solution)/shard_map/response/pallas_call | solution.py:154
  83.5 2.2 %dynamic-slice_bitcast_fusion = f32[4,192,256]{2,1,0:T(8,128)} fusion(f32[2,4,192,256]{3,2,1,0:T(8,128)} %bitcast.119, s32[]{:T(128)S(6)} %select_n.114), kind=kLoop, calls=%fused_computation.11 | loop fusion | bytes 1572868 | tf_op jit(solution)/shard_map/jit(dynamic_index_in_dim)/squeeze | solution.py:198
  86.5 1.6 collective-permute-start.1
  89.2 1.9 %collective-permute-start.3 = (f32[192,256]{1,0:T(8,128)S(1)}, f32[192,256]{1,0:T(8,128)S(1)}, u32[]{:S(2)}, u32[]{:S(2)}) collective-permute-start(f32[192,256]{1,0:T(8,128)S(1)} %get-tuple-element.19), channel_id=1, source_target_pairs={{0,12},{2,14},{4,0},{6,2},{8,4},{10,6},{12,8},{14,10},{1,13},{3,15... | collective-permute-start | bytes 589832 | tf_op jit(solution)/shard_map/ppermute | solution.py:210
  91.2 10.7 %collective-permute-done.1 = f32[192,256]{1,0:T(8,128)S(1)} collective-permute-done((f32[192,256]{1,0:T(8,128)S(1)}, f32[192,256]{1,0:T(8,128)S(1)}, u32[]{:S(2)}, u32[]{:S(2)}) %collective-permute-start.1) | collective-permute-done | bytes 196640 | tf_op jit(solution)/shard_map/ppermute | solution.py:210
  101.8 3.3 %collective-permute-done.2 = f32[192,256]{1,0:T(8,128)S(1)} collective-permute-done((f32[192,256]{1,0:T(8,128)S(1)}, f32[192,256]{1,0:T(8,128)S(1)}, u32[]{:S(2)}, u32[]{:S(2)}) %collective-permute-start.2) | collective-permute-done | bytes 196640 | tf_op jit(solution)/shard_map/ppermute | solution.py:210
  105.1 1.8 collective-permute-done.3
  109.0 4.9 %collective-permute-done.4 = f32[192,256]{1,0:T(8,128)S(1)} collective-permute-done((f32[192,256]{1,0:T(8,128)S(1)}, f32[192,256]{1,0:T(8,128)S(1)}, u32[]{:S(2)}, u32[]{:S(2)}) %collective-permute-start.4) | collective-permute-done | bytes 196640 | tf_op jit(solution)/shard_map/ppermute | solution.py:219
  120.7 2.0 %collective-permute-start.9 = (f32[192,256]{1,0:T(8,128)S(1)}, f32[192,256]{1,0:T(8,128)}, u32[]{:S(2)}, u32[]{:S(2)}) collective-permute-start(f32[192,256]{1,0:T(8,128)S(1)} %get-tuple-element.16), channel_id=1, source_target_pairs={{0,12},{2,14},{4,0},{6,2},{8,4},{10,6},{12,8},{14,10},{1,13},{3,15... | collective-permute-start | bytes 589832 | tf_op jit(solution)/shard_map/ppermute | solution.py:210
  123.1 3.4 %collective-permute-done.5 = f32[2,192,256]{2,0,1:T(2,128)S(1)} collective-permute-done((f32[2,192,256]{2,0,1:T(2,128)S(1)}, f32[2,192,256]{2,0,1:T(2,128)S(1)}, u32[]{:S(2)}, u32[]{:S(2)}) %collective-permute-start.5) | collective-permute-done | bytes 393248 | tf_op jit(solution)/shard_map/ppermute | solution.py:222
  128.8 5.0 %collective-permute-done.7 = f32[192,256]{1,0:T(8,128)} collective-permute-done((f32[192,256]{1,0:T(8,128)}, f32[192,256]{1,0:T(8,128)}, u32[]{:S(2)}, u32[]{:S(2)}) %collective-permute-start.7) | collective-permute-done | bytes 196640 | tf_op jit(solution)/shard_map/ppermute | solution.py:210
  133.9 2.5 %collective-permute-done.8 = f32[192,256]{1,0:T(8,128)} collective-permute-done((f32[192,256]{1,0:T(8,128)}, f32[192,256]{1,0:T(8,128)}, u32[]{:S(2)}, u32[]{:S(2)}) %collective-permute-start.8) | collective-permute-done | bytes 196640 | tf_op jit(solution)/shard_map/ppermute | solution.py:210
  137.3 2.2 %fusion.1 = f32[4,2,128,256]{3,2,1,0:T(8,128)S(1)} fusion(f32[4,2,128,192]{2,1,0,3:T(2,128)S(1)} %dot_general.11, f32[192,256]{1,0:T(8,128)} %collective-permute-done.9, f32[192,256]{1,0:T(8,128)} %collective-permute-done.8, f32[192,256]{1,0:T(8,128)} %collective-permute-done.7, f32[4,192,256]{2,1,0:T(8,128)S(1)} %bitcast_add_fusion, s32[]{:T(128)S(6)} %select_n.115, ...), kind=kOutput, calls=%fused_computation.9 | convolution fusion | flops 302284800 | bytes 2623492 | tf_op jit(solution)/shard_map/dot_general | solution.py:256
  140.5 2.5 %collective-permute-start.15 = (f32[32,1024]{1,0:T(8,128)S(1)}, f32[32,1024]{1,0:T(8,128)S(1)}, u32[]{:S(2)}, u32[]{:S(2)}) collective-permute-start(f32[32,1024]{1,0:T(8,128)S(1)} %constant_dynamic-slice_fusion.2), channel_id=1, source_target_pairs={{0,8},{2,10},{4,12},{6,14},{8,0},{10,2},{12,4},{14,6},{1,9},{3,11}... | collective-permute-start | bytes 393224 | tf_op jit(solution)/shard_map/ppermute | solution.py:243
  143.0 1.9 %collective-permute-start.16 = (f32[32,1024]{1,0:T(8,128)S(1)}, f32[32,1024]{1,0:T(8,128)S(1)}, u32[]{:S(2)}, u32[]{:S(2)}) collective-permute-start(f32[32,1024]{1,0:T(8,128)S(1)} %constant_dynamic-slice_fusion.2), channel_id=1, source_target_pairs={{0,12},{2,14},{4,0},{6,2},{8,4},{10,6},{12,8},{14,10},{1,13},{3,15... | collective-permute-start | bytes 393224 | tf_op jit(solution)/shard_map/ppermute | solution.py:243
  144.9 1.8 collective-permute-done.14
  146.7 5.8 %collective-permute-done.15 = f32[32,1024]{1,0:T(8,128)S(1)} collective-permute-done((f32[32,1024]{1,0:T(8,128)S(1)}, f32[32,1024]{1,0:T(8,128)S(1)}, u32[]{:S(2)}, u32[]{:S(2)}) %collective-permute-start.15) | collective-permute-done | bytes 131104 | tf_op jit(solution)/shard_map/ppermute | solution.py:243
  152.6 2.9 %collective-permute-done.16 = f32[32,1024]{1,0:T(8,128)S(1)} collective-permute-done((f32[32,1024]{1,0:T(8,128)S(1)}, f32[32,1024]{1,0:T(8,128)S(1)}, u32[]{:S(2)}, u32[]{:S(2)}) %collective-permute-start.16) | collective-permute-done | bytes 131104 | tf_op jit(solution)/shard_map/ppermute | solution.py:243
  160.2 3.3 %collective-permute-done.11 = f32[128,256]{1,0:T(8,128)} collective-permute-done((f32[128,256]{1,0:T(8,128)S(1)}, f32[128,256]{1,0:T(8,128)}, u32[]{:S(2)}, u32[]{:S(2)}) %collective-permute-start.11) | collective-permute-done | bytes 131104 | tf_op jit(solution)/shard_map/ppermute | solution.py:210
  163.5 5.7 %collective-permute-done.12 = f32[128,256]{1,0:T(8,128)} collective-permute-done((f32[128,256]{1,0:T(8,128)S(1)}, f32[128,256]{1,0:T(8,128)}, u32[]{:S(2)}, u32[]{:S(2)}) %collective-permute-start.12) | collective-permute-done | bytes 131104 | tf_op jit(solution)/shard_map/ppermute | solution.py:210
  172.6 1.6 collective-permute-start.18
  174.2 6.7 %collective-permute-done.18 = f32[64,2,512]{2,0,1:T(8,128)S(1)} collective-permute-done((f32[64,2,512]{2,0,1:T(8,128)S(1)}, f32[64,2,512]{2,0,1:T(8,128)S(1)}, u32[]{:S(2)}, u32[]{:S(2)}) %collective-permute-start.18) | collective-permute-done | bytes 262176 | tf_op jit(solution)/shard_map/ppermute | solution.py:272
  181.6 4.4 %collective-permute-done.19 = f32[64,512]{1,0:T(8,128)S(1)} collective-permute-done((f32[64,512]{1,0:T(8,128)S(1)}, f32[64,512]{1,0:T(8,128)S(1)}, u32[]{:S(2)}, u32[]{:S(2)}) %collective-permute-start.19) | collective-permute-done | bytes 131104 | tf_op jit(solution)/shard_map/ppermute | solution.py:275
  (92 shorter events, 31.5 us)
Async XLA Ops:
  61.5 24.8 %collective-permute-start = (f32[4,192,256]{2,1,0:T(8,128)S(1)}, f32[4,192,256]{2,1,0:T(8,128)S(1)}, u32[]{:S(2)}, u32[]{:S(2)}) collective-permute-start(f32[4,192,256]{2,1,0:T(8,128)S(1)} %dynamic-slice_bitcast_fusion.1), channel_id=1, source_target_pairs={{0,2},{2,0},{4,6},{6,4},{8,10},{10,8},{12,14},{14,12},{1,3},{3,1},... | collective-permute-start | bytes 2359304 | tf_op jit(solution)/shard_map/ppermute | solution.py:206
  61.6 24.6 %copy-start.2 = (f32[1536]{0:T(1024)S(1)}, f32[1536]{0:T(1024)}, u32[]{:S(2)}) copy-start(f32[1536]{0:T(1024)} %param.9) | copy-start | bytes 18436
  61.6 24.6 %slice-start = ((f32[1536]{0:T(1024)}), f32[512]{0:T(512)S(1)}, s32[]{:S(2)}) async-start(f32[1536]{0:T(1024)} %param.9), calls=%async_computation | async-start | bytes 4096 | tf_op jit(solution)/shard_map/slice | solution.py:190
  85.7 32.1 %collective-permute-start.6 = (f32[4,192,256]{2,1,0:T(8,128)}, f32[4,192,256]{2,1,0:T(8,128)}, u32[]{:S(2)}, u32[]{:S(2)}) collective-permute-start(f32[4,192,256]{2,1,0:T(8,128)} %dynamic-slice_bitcast_fusion), channel_id=1, source_target_pairs={{0,2},{2,0},{4,6},{6,4},{8,10},{10,8},{12,14},{14,12},{1,3},{3,1},... | collective-permute-start | bytes 2359304 | tf_op jit(solution)/shard_map/ppermute | solution.py:206
  86.5 15.3 %collective-permute-start.1 = (f32[192,256]{1,0:T(8,128)S(1)}, f32[192,256]{1,0:T(8,128)S(1)}, u32[]{:S(2)}, u32[]{:S(2)}) collective-permute-start(f32[192,256]{1,0:T(8,128)S(1)} %get-tuple-element.18), channel_id=1, source_target_pairs={{0,4},{2,6},{4,8},{6,10},{8,12},{10,14},{12,0},{14,2},{1,5},{3,7},... | collective-permute-start | bytes 589832 | tf_op jit(solution)/shard_map/ppermute | solution.py:210
  88.1 17.0 %collective-permute-start.2 = (f32[192,256]{1,0:T(8,128)S(1)}, f32[192,256]{1,0:T(8,128)S(1)}, u32[]{:S(2)}, u32[]{:S(2)}) collective-permute-start(f32[192,256]{1,0:T(8,128)S(1)} %get-tuple-element.20), channel_id=1, source_target_pairs={{0,8},{2,10},{4,12},{6,14},{8,0},{10,2},{12,4},{14,6},{1,9},{3,11}... | collective-permute-start | bytes 589832 | tf_op jit(solution)/shard_map/ppermute | solution.py:210
  89.2 17.7 %collective-permute-start.3 = (f32[192,256]{1,0:T(8,128)S(1)}, f32[192,256]{1,0:T(8,128)S(1)}, u32[]{:S(2)}, u32[]{:S(2)}) collective-permute-start(f32[192,256]{1,0:T(8,128)S(1)} %get-tuple-element.19), channel_id=1, source_target_pairs={{0,12},{2,14},{4,0},{6,2},{8,4},{10,6},{12,8},{14,10},{1,13},{3,15... | collective-permute-start | bytes 589832 | tf_op jit(solution)/shard_map/ppermute | solution.py:210
  91.2 26.7 %copy-start = (f32[1536,256]{1,0:T(8,128)S(1)}, f32[1536,256]{1,0:T(8,128)}, u32[]{:S(2)}) copy-start(f32[1536,256]{1,0:T(8,128)} %response.1) | copy-start | bytes 4718596
  107.0 6.9 %collective-permute-start.4 = (f32[192,256]{1,0:T(8,128)S(1)}, f32[192,256]{1,0:T(8,128)S(1)}, u32[]{:S(2)}, u32[]{:S(2)}) collective-permute-start(f32[192,256]{1,0:T(8,128)S(1)} %fusion.11), channel_id=1, source_target_pairs={{0,1},{1,0},{2,3},{3,2},{4,5},{5,4},{6,7},{7,6},{8,9},{9,8},{10,11... | collective-permute-start | bytes 589832 | tf_op jit(solution)/shard_map/ppermute | solution.py:219
  116.3 10.3 %collective-permute-start.5 = (f32[2,192,256]{2,0,1:T(2,128)S(1)}, f32[2,192,256]{2,0,1:T(2,128)S(1)}, u32[]{:S(2)}, u32[]{:S(2)}) collective-permute-start(f32[2,192,256]{2,0,1:T(2,128)S(1)} %broadcast_select_fusion), channel_id=1, source_target_pairs={{0,16},{16,0},{1,17},{17,1},{2,18},{18,2},{3,19},{19,3},{4,20},{20... | collective-permute-start | bytes 1179656 | tf_op jit(solution)/shard_map/ppermute | solution.py:222
  119.9 14.0 %collective-permute-start.7 = (f32[192,256]{1,0:T(8,128)}, f32[192,256]{1,0:T(8,128)}, u32[]{:S(2)}, u32[]{:S(2)}) collective-permute-start(f32[192,256]{1,0:T(8,128)} %get-tuple-element.15), channel_id=1, source_target_pairs={{0,4},{2,6},{4,8},{6,10},{8,12},{10,14},{12,0},{14,2},{1,5},{3,7},... | collective-permute-start | bytes 589832 | tf_op jit(solution)/shard_map/ppermute | solution.py:210
  119.9 16.5 %collective-permute-start.8 = (f32[192,256]{1,0:T(8,128)}, f32[192,256]{1,0:T(8,128)}, u32[]{:S(2)}, u32[]{:S(2)}) collective-permute-start(f32[192,256]{1,0:T(8,128)} %get-tuple-element.17), channel_id=1, source_target_pairs={{0,8},{2,10},{4,12},{6,14},{8,0},{10,2},{12,4},{14,6},{1,9},{3,11}... | collective-permute-start | bytes 589832 | tf_op jit(solution)/shard_map/ppermute | solution.py:210
  120.7 16.6 %collective-permute-start.9 = (f32[192,256]{1,0:T(8,128)S(1)}, f32[192,256]{1,0:T(8,128)}, u32[]{:S(2)}, u32[]{:S(2)}) collective-permute-start(f32[192,256]{1,0:T(8,128)S(1)} %get-tuple-element.16), channel_id=1, source_target_pairs={{0,12},{2,14},{4,0},{6,2},{8,4},{10,6},{12,8},{14,10},{1,13},{3,15... | collective-permute-start | bytes 589832 | tf_op jit(solution)/shard_map/ppermute | solution.py:210
  139.5 16.2 %copy-start.3 = (s32[1024]{0:T(1024)S(1)}, s32[1024]{0:T(1024)}, u32[]{:S(2)}) copy-start(s32[1024]{0:T(1024)} %param.12) | copy-start | bytes 12292
  140.4 15.5 %collective-permute-start.10 = (f32[4,128,256]{2,1,0:T(8,128)}, f32[4,128,256]{2,1,0:T(8,128)}, u32[]{:S(2)}, u32[]{:S(2)}) collective-permute-start(f32[4,128,256]{2,1,0:T(8,128)} %dynamic-slice_bitcast_fusion.2), channel_id=1, source_target_pairs={{0,2},{2,0},{4,6},{6,4},{8,10},{10,8},{12,14},{14,12},{1,3},{3,1},... | collective-permute-start | bytes 1572872 | tf_op jit(solution)/shard_map/ppermute | solution.py:206
  140.4 6.3 %collective-permute-start.14 = (f32[32,1024]{1,0:T(8,128)S(1)}, f32[32,1024]{1,0:T(8,128)S(1)}, u32[]{:S(2)}, u32[]{:S(2)}) collective-permute-start(f32[32,1024]{1,0:T(8,128)S(1)} %constant_dynamic-slice_fusion.2), channel_id=1, source_target_pairs={{0,4},{2,6},{4,8},{6,10},{8,12},{10,14},{12,0},{14,2},{1,5},{3,7},... | collective-permute-start | bytes 393224 | tf_op jit(solution)/shard_map/ppermute | solution.py:243
  140.5 12.1 %collective-permute-start.15 = (f32[32,1024]{1,0:T(8,128)S(1)}, f32[32,1024]{1,0:T(8,128)S(1)}, u32[]{:S(2)}, u32[]{:S(2)}) collective-permute-start(f32[32,1024]{1,0:T(8,128)S(1)} %constant_dynamic-slice_fusion.2), channel_id=1, source_target_pairs={{0,8},{2,10},{4,12},{6,14},{8,0},{10,2},{12,4},{14,6},{1,9},{3,11}... | collective-permute-start | bytes 393224 | tf_op jit(solution)/shard_map/ppermute | solution.py:243
  143.0 12.5 %collective-permute-start.16 = (f32[32,1024]{1,0:T(8,128)S(1)}, f32[32,1024]{1,0:T(8,128)S(1)}, u32[]{:S(2)}, u32[]{:S(2)}) collective-permute-start(f32[32,1024]{1,0:T(8,128)S(1)} %constant_dynamic-slice_fusion.2), channel_id=1, source_target_pairs={{0,12},{2,14},{4,0},{6,2},{8,4},{10,6},{12,8},{14,10},{1,13},{3,15... | collective-permute-start | bytes 393224 | tf_op jit(solution)/shard_map/ppermute | solution.py:243
  155.6 4.0 %collective-permute-start.17 = (f32[4,32,1024]{2,1,0:T(8,128)S(1)}, f32[4,32,1024]{2,1,0:T(8,128)S(1)}, u32[]{:S(2)}, u32[]{:S(2)}) collective-permute-start(f32[4,32,1024]{2,1,0:T(8,128)S(1)} %get-tuple-element.27), channel_id=1, source_target_pairs={{0,2},{2,0},{4,6},{6,4},{8,10},{10,8},{12,14},{14,12},{1,3},{3,1},... | collective-permute-start | bytes 1572872 | tf_op jit(solution)/shard_map/ppermute | solution.py:245
  157.1 6.5 %collective-permute-start.11 = (f32[128,256]{1,0:T(8,128)S(1)}, f32[128,256]{1,0:T(8,128)}, u32[]{:S(2)}, u32[]{:S(2)}) collective-permute-start(f32[128,256]{1,0:T(8,128)S(1)} %get-tuple-element.23), channel_id=1, source_target_pairs={{0,4},{2,6},{4,8},{6,10},{8,12},{10,14},{12,0},{14,2},{1,5},{3,7},... | collective-permute-start | bytes 393224 | tf_op jit(solution)/shard_map/ppermute | solution.py:210
  157.1 12.1 %collective-permute-start.12 = (f32[128,256]{1,0:T(8,128)S(1)}, f32[128,256]{1,0:T(8,128)}, u32[]{:S(2)}, u32[]{:S(2)}) collective-permute-start(f32[128,256]{1,0:T(8,128)S(1)} %get-tuple-element.25), channel_id=1, source_target_pairs={{0,8},{2,10},{4,12},{6,14},{8,0},{10,2},{12,4},{14,6},{1,9},{3,11}... | collective-permute-start | bytes 393224 | tf_op jit(solution)/shard_map/ppermute | solution.py:210
  158.2 12.4 %collective-permute-start.13 = (f32[128,256]{1,0:T(8,128)S(1)}, f32[128,256]{1,0:T(8,128)}, u32[]{:S(2)}, u32[]{:S(2)}) collective-permute-start(f32[128,256]{1,0:T(8,128)S(1)} %get-tuple-element.24), channel_id=1, source_target_pairs={{0,12},{2,14},{4,0},{6,2},{8,4},{10,6},{12,8},{14,10},{1,13},{3,15... | collective-permute-start | bytes 393224 | tf_op jit(solution)/shard_map/ppermute | solution.py:210
  172.6 8.3 %collective-permute-start.18 = (f32[64,2,512]{2,0,1:T(8,128)S(1)}, f32[64,2,512]{2,0,1:T(8,128)S(1)}, u32[]{:S(2)}, u32[]{:S(2)}) collective-permute-start(f32[64,2,512]{2,0,1:T(8,128)S(1)} %bitcast.126), channel_id=1, source_target_pairs={{0,1},{1,0},{2,3},{3,2},{4,5},{5,4},{6,7},{7,6},{8,9},{9,8},{10,11... | collective-permute-start | bytes 786440 | tf_op jit(solution)/shard_map/ppermute | solution.py:272
  181.0 5.0 %collective-permute-start.19 = (f32[64,512]{1,0:T(8,128)S(1)}, f32[64,512]{1,0:T(8,128)S(1)}, u32[]{:S(2)}, u32[]{:S(2)}) collective-permute-start(f32[64,512]{1,0:T(8,128)S(1)} %dynamic-slice_bitcast_fusion.9), channel_id=1, source_target_pairs={{0,16},{16,0},{1,17},{17,1},{2,18},{18,2},{3,19},{19,3},{4,20},{20... | collective-permute-start | bytes 393224 | tf_op jit(solution)/shard_map/ppermute | solution.py:275
  (2 other events, 19.0 us)

commit v2 on v1

v2 whole, which is shorter than its diff:
```python
import functools
import math

import jax
import jax.numpy as jnp
from jax import lax
from jax.experimental import pallas as pl
from jax.experimental.pallas import tpu as pltpu
from jax.sharding import PartitionSpec as P

PANEL = 512
LANES = 128
CHUNK = 1024
VMEM_BYTES = 60 * 2**20
PARTS = 2
SLICES = 4


def split(value):
    high = value.astype(jnp.bfloat16)
    return high, (value - high.astype(jnp.float32)).astype(jnp.bfloat16)


def three_pass(left_high, left_low, right_high, right_low):
    def dot(left, right):
        return jnp.dot(left, right, preferred_element_type=jnp.float32)

    return dot(left_high, right_high) + (dot(left_low, right_high) + dot(left_high, right_low))


def product_kernel(
    paired, occ_ref, vir_ref, occ_own_ref, vir_own_ref, coulomb_ref, band_ref, out_ref,
    incoming, arrived, turned_even, turned_odd, products,
    left_high_even, left_high_odd, left_low_even, left_low_odd,
    right_high_even, right_high_odd, right_low_even, right_low_odd,
):
    turned = turned_even, turned_odd
    left_high, left_low = (left_high_even, left_high_odd), (left_low_even, left_low_odd)
    right_high, right_low = (right_high_even, right_high_odd), (right_low_even, right_low_odd)
    chunk, bands = incoming.shape[1:]
    chunks = band_ref.shape[0] // chunk
    groups = chunk // LANES
    stride = turned_even.shape[0] // bands
    pairs = out_ref.shape[0] // PARTS
    own = out_ref.shape[1] // PARTS
    depth = chunk // PARTS

    def fetch(c):
        slot = lax.rem(c, 3)
        return pltpu.make_async_copy(
            band_ref.at[pl.ds(c * chunk, chunk), :], incoming.at[slot], arrived.at[slot]
        )

    def turn(c, k, parity, part):
        group = k * (groups // PARTS) + part
        rows = pl.ds(pl.multiple_of(group * LANES, LANES), LANES)
        turned[parity][pl.ds(group, bands, stride=stride), :] = (
            incoming[lax.rem(c, 3), rows, :].T
        )

    def gather(parity, occ, vir, first, count, place):
        for pair in range(count):
            left = turned[parity][pl.ds(occ[first + pair], groups), :]
            right = turned[parity][pl.ds(vir[first + pair], groups), :]
            products[pl.ds((place + pair) * stride, groups), :] = left * right

    def weight(c, group):
        return coulomb_ref[pl.ds(lax.rem(c, chunks) * groups + group, 1), :]

    def prepare_own(c, k, parity):
        gather(parity, occ_own_ref, vir_own_ref, k * own, own, pairs)
        for group in range(groups):
            value = products[pl.ds(pairs * stride + group, own, stride=stride), :]
            here = pl.ds(group * LANES, LANES)
            there = pl.ds(pl.multiple_of(k * own, own), own)
            right_high[parity][here, there], right_low[parity][here, there] = split(
                (value * weight(c, group)).T
            )

    def prepare_bands(c, k, parity, part):
        here = pl.ds(pl.multiple_of(k * depth + part * LANES, LANES), LANES)
        right_high[parity][here, :], right_low[parity][here, :] = split(
            incoming[lax.rem(c, 3), here, :]
        )

    def prepare(c, k, parity, first, count):
        gather(parity, occ_ref, vir_ref, k * pairs + first, count, first)
        for group in range(groups):
            value = products[pl.ds(first * stride + group, count, stride=stride), :]
            if not paired:
                value = value * weight(c, group)
            here = pl.ds(pl.multiple_of(k * pairs + first, 16), count)
            there = pl.ds(group * LANES, LANES)
            left_high[parity][here, there], left_low[parity][here, there] = split(value)

    def multiply(k, parity, rows, columns):
        here = pl.ds(pl.multiple_of(k * depth, depth), depth)
        out_ref[rows, columns] += three_pass(
            left_high[parity][rows, here], left_low[parity][rows, here],
            right_high[parity][here, columns], right_low[parity][here, columns],
        )

    def body(c, k, parity, first, second, third):
        turns = groups // PARTS if third else 0
        for part in range(max(SLICES, turns)):
            if first and part < SLICES:
                if paired:
                    height = out_ref.shape[0] // SLICES
                    multiply(k, parity, pl.ds(part * height, height), slice(None))
                else:
                    height = out_ref.shape[1] // SLICES
                    multiply(k, parity, slice(None), pl.ds(part * height, height))
            if part < turns:
                turn(c + 2, k, parity, part)
            if second:
                if paired and part == 0:
                    prepare_own(c + 1, k, 1 - parity)
                if not paired and part < depth // LANES:
                    prepare_bands(c + 1, k, 1 - parity, part)
                if part < SLICES:
                    count = pairs // SLICES
                    prepare(c + 1, k, 1 - parity, part * count, count)

    for c in range(min(3, chunks)):
        fetch(c).start()
    out_ref[...] = jnp.zeros_like(out_ref)
    fetch(0).wait()

    @pl.loop(0, PARTS)
    def _(k):
        body(-2, k, 0, False, False, True)

    if chunks > 1:
        fetch(1).wait()

    @pl.loop(0, PARTS)
    def _(k):
        body(-1, k, 1, False, True, True)

    def advance(c, parity):
        @pl.when(c + 2 < chunks)
        def _():
            fetch(c + 2).wait()

        @pl.when(c + 3 < chunks)
        def _():
            fetch(c + 3).start()

        @pl.loop(0, PARTS)
        def _(k):
            body(c, k, parity, True, True, True)

    @pl.loop(0, chunks // 2)
    def _(index):
        advance(2 * index, 0)
        advance(2 * index + 1, 1)

    if chunks % 2:
        advance(chunks - 1, 0)


def pair_product(band_vectors, coulomb, occ, vir, occ_own, vir_own, paired, name):
    basis_rows, bands = band_vectors.shape
    pairs = occ.shape[0]
    width = occ_own.shape[0] if paired else bands
    chunk = math.gcd(CHUNK, basis_rows)
    groups = chunk // LANES
    stride = groups + 1 - groups % 2
    half = jnp.bfloat16
    scalars = pl.BlockSpec(memory_space=pltpu.SMEM)
    whole = pl.BlockSpec(memory_space=pltpu.VMEM)
    batch = (pairs + (width if paired else 0)) // PARTS
    return pl.pallas_call(
        functools.partial(product_kernel, paired),
        in_specs=[scalars] * 4 + [whole, pl.BlockSpec(memory_space=pl.ANY)],
        out_specs=whole,
        out_shape=jax.ShapeDtypeStruct((pairs, width), jnp.float32),
        scratch_shapes=[
            pltpu.VMEM((3, chunk, bands), jnp.float32),
            pltpu.SemaphoreType.DMA((3,)),
            pltpu.VMEM((bands * stride, LANES), jnp.float32),
            pltpu.VMEM((bands * stride, LANES), jnp.float32),
            pltpu.VMEM((batch * stride, LANES), jnp.float32),
        ]
        + [pltpu.VMEM((pairs, chunk), half)] * 4
        + [pltpu.VMEM((chunk, width), half)] * 4,
        compiler_params=pltpu.CompilerParams(vmem_limit_bytes=VMEM_BYTES),
        cost_estimate=pl.CostEstimate(
            flops=6 * basis_rows * pairs * width,
            bytes_accessed=4 * basis_rows * bands,
            transcendentals=0,
        ),
        name=name,
    )(
        occ * stride, vir * stride, occ_own * stride, vir_own * stride,
        coulomb.reshape(basis_rows // LANES, LANES), band_vectors,
    )


def per_device(band_vectors, coulomb, pair_weight, occ_index, vir_index, freq_index, freq_table):
    row_count = lax.axis_size("rows")
    col_count = lax.axis_size("cols")
    group_count = lax.axis_size("grp")
    blocks = col_count * group_count
    lines = row_count // 2
    row = lax.axis_index("rows")
    core, line = lax.rem(row, 2), lax.div(row, 2)
    column = lax.axis_index("cols")
    group = lax.axis_index("grp")
    block = group * col_count + column
    basis_rows, bands = band_vectors.shape
    pairs = occ_index.shape[0]
    window = PANEL * group_count
    basis = basis_rows * row_count

    def ordered(values):
        def shares(part):
            return part.reshape(lines, 2, blocks, -1).swapaxes(0, 1)

        return jnp.concatenate([shares(values[:window]), shares(values[window:])], axis=3)

    def own_window(values):
        shaped = values[:window].reshape(row_count, blocks, -1)
        return pick(shaped, block, 1).reshape(-1)

    def pick(values, index, axis=0):
        return lax.dynamic_index_in_dim(values, index, axis, keepdims=False)

    other_core = [(i, i ^ 1) for i in range(row_count)]

    def shift(step):
        return [(i, (i // 2 + step) % lines * 2 + i % 2) for i in range(row_count)]

    def add_cores(values):
        received = lax.ppermute(pick(values, 1 - core), "rows", other_core)
        return pick(values, core) + received

    def scatter_lines(values):
        arrived = [
            lax.ppermute(pick(values, lax.rem(line + step, lines)), "rows", shift(step))
            for step in range(1, lines)
        ]
        total = pick(values, line)
        for value in arrived:
            total = total + value
        return total

    def gather_blocks(values):
        across = [(i, i ^ 1) for i in range(col_count)]
        pair = jnp.stack([values, lax.ppermute(values, "cols", across)])
        pair = jnp.where(column == 0, pair, pair[::-1])
        across = [(i, i ^ 1) for i in range(group_count)]
        quad = jnp.stack([pair, lax.ppermute(pair, "grp", across)])
        quad = jnp.where(group == 0, quad, quad[::-1])
        return quad.reshape((blocks,) + values.shape)

    occ_own, vir_own = own_window(occ_index), own_window(vir_index)
    occ, vir, weights = ordered(occ_index), ordered(vir_index), ordered(pair_weight)
    partial_coupling = pair_product(
        band_vectors, coulomb, pick(occ, block, 2).reshape(-1), pick(vir, block, 2).reshape(-1),
        occ_own, vir_own, False, "coupling",
    )
    share = pairs // row_count
    partial_coupling = add_cores(partial_coupling.reshape(2, lines, share // blocks, bands))
    partial_coupling, occ, vir = lax.optimization_barrier((partial_coupling, occ, vir))
    partial_response = pair_product(
        band_vectors, coulomb, occ.reshape(-1), vir.reshape(-1), occ_own, vir_own, True, "response"
    )

    partial_response = add_cores(partial_response.reshape(2, lines, share, window // blocks))
    own_weights = pick(pick(weights, core), line)
    coupling = scatter_lines(partial_coupling)
    partial_response, coupling = lax.optimization_barrier((partial_response, coupling))
    coupling = coupling * (pick(own_weights, block)[:, None] * (1.0 / math.sqrt(basis)))
    all_coupling = gather_blocks(coupling).reshape(share, bands)
    response = scatter_lines(partial_response)
    response = response * (
        own_weights.reshape(-1)[:, None] * own_window(pair_weight)[None, :] * (1.0 / basis)
    )
    sub = window // (row_count * blocks)
    response, part = lax.optimization_barrier((response, coupling[:sub]))
    parts = [part] + [lax.ppermute(part, "rows", shift(step)) for step in range(1, lines)]
    parts = jnp.stack(parts)
    beside = lax.ppermute(parts, "rows", other_core)
    both = jnp.where(core == 0, jnp.stack([parts, beside], 1), jnp.stack([beside, parts], 1))
    both = jnp.roll(both[::-1], line + 1, axis=0)
    window_coupling = both.reshape(row_count * sub, bands)

    matches = freq_index[:, None] == jnp.arange(freq_table.shape[0], dtype=jnp.int32)[None, :]
    band_weight = jnp.sum(jnp.where(matches, freq_table[None, :], 0.0), axis=1)
    mixed = lax.dot_general(
        all_coupling, response, (((0,), (0,)), ((), ())),
        precision=lax.Precision.HIGH, preferred_element_type=jnp.float32,
    )
    mixed = add_cores(mixed.reshape(lines, 2, bands // row_count, -1).swapaxes(0, 1))
    mixed = scatter_lines(mixed)
    energy = lax.dot_general(
        mixed, window_coupling, (((1,), (0,)), ((), ())),
        precision=lax.Precision.HIGH, preferred_element_type=jnp.float32,
    )
    here = bands // row_count
    own_band_weight = lax.dynamic_slice_in_dim(band_weight, row * here, here, 0)
    energy = energy * (
        own_band_weight[:, None] * band_weight[None, :] * (1.0 / math.sqrt(window))
    )
    energy = energy.reshape(col_count, here // col_count, group_count, bands // group_count)
    across = [(i, i ^ 1) for i in range(col_count)]
    received = lax.ppermute(pick(energy, 1 - column), "cols", across)
    energy = pick(energy, column) + received
    across = [(i, i ^ 1) for i in range(group_count)]
    received = lax.ppermute(pick(energy, 1 - group, 1), "grp", across)
    return pick(energy, group, 1) + received


def solution(mesh):
    placed = (P("rows", None), P("rows"), P(), P(), P(), P(), P())
    return jax.shard_map(
        per_device,
        mesh=mesh,
        in_specs=placed,
        out_specs=P(("rows", "cols"), "grp"),
        check_vma=False,
    )
```

time: 188 us -> 195 us (1.037)
  Pallas kernels: 76.4 us -> 85.6 us
  waiting for transfers between devices: 64.7 us -> 56.9 us
  local copies, waits for them, and re-layouts: 15.3 us -> 19.3 us
  other arithmetic: 5.8 us -> 8.72 us
  matrix products: 3.66 us -> 1.46 us
    pallas_call x2, Pallas kernels: 76.4 us -> 85.6 us  [pair_product(): pl.pallas_call(functools.partial(product_kernel, paired), in_specs=[scala...]
    mul x1 -> x10, local copies, waits for them, and re-layouts: 0.08 us -> 6.67 us  [the longest x2 2.66 us: per_device(): own_weights.reshape(-1)[:, None] * own_window(pair_weight)[None, :]]
    ppermute x1, waiting for transfers between devices: 4.93 us -> 1.43 us  [gather_blocks(): pair = jnp.stack([values, lax.ppermute(values, 'cols', across)])]
    ppermute x1, waiting for transfers between devices: 3.43 us -> 0.01 us  [gather_blocks(): quad = jnp.stack([pair, lax.ppermute(pair, 'grp', across)])]
    ppermute x12, starting transfers between devices: 10.6 us -> 12.9 us  [the longest x9 12.2 us: scatter_lines(): lax.ppermute(pick(values, lax.rem(line + step, lines)), 'rows', shift(step))]
  transfers between devices with their start and end apart: 20 -> 20, of which waited for: 16 -> 17; matrix products, arithmetic and copies ran while one was open for 6% -> 8% of each run, Pallas kernels for 12% -> 0%
where the time goes in v2:
time: 195 us; the launch traced here: 194 us
  Pallas kernels  85.6 us (44%)
  waiting for transfers between devices  56.9 us (29%)
  starting transfers between devices  22 us (11%)
  local copies, waits for them, and re-layouts  19.3 us (10%)
  other arithmetic  8.72 us (4%)
    pallas_call x2, Pallas kernels, pair_product(): pl.pallas_call(functools.partial(product_kernel, paired), in_specs=[scala...  85.6 us
    ppermute x9, waiting for transfers between devices, scatter_lines(): lax.ppermute(pick(values, lax.rem(line + step, lines)), 'rows', shift(step))  32.4 us
    ppermute x9, starting transfers between devices, scatter_lines(): lax.ppermute(pick(values, lax.rem(line + step, lines)), 'rows', shift(step))  12.2 us
    ppermute x3, waiting for transfers between devices, per_device(): lax.ppermute(part, 'rows', shift(step))  9.31 us
    ppermute x1, waiting for transfers between devices, per_device(): received = lax.ppermute(pick(energy, 1 - column), 'cols', across)  7.77 us
    squeeze x7, local copies, waits for them, and re-layouts, pick(): return lax.dynamic_index_in_dim(values, index, axis, keepdims=False)  5.13 us
  transfers between devices with their start and end apart: 20, of which 17 were waited for; matrix products, arithmetic and copies ran while one was open for 8% of the time, Pallas kernels for 0%

profile of v2, /device:TPU:8, one launch (start us, length us, event | category | flops | bytes accessed | tf_op | source)
XLA Modules:
  0.0 194.2 jit_solution(8248852095021388317)
XLA Ops:
  6.0 34.4 %coupling.1 = f32[384,1024]{1,0:T(8,128)} custom-call(s32[384]{0:T(512)} %mul.110.occ_ref, s32[384]{0:T(512)} %mul.112.vir_ref, s32[256]{0:T(256)} %mul.114.occ_own_ref, s32[256]{0:T(256)} %mul.116.vir_own_ref, f32[48,128]{1,0:T(8,128)} %bitcast.137, f32[6144,1024]{1,0:T(8,128)} %band_ref.3), custom_call_target="tpu_custom_call" | custom-call | flops 14495514624 | bytes 25165824 | tf_op jit(solution)/shard_map/coupling/pallas_call | solution.py:173
  42.0 2.2 %collective-permute-done = f32[4,48,1024]{2,1,0:T(8,128)S(1)} collective-permute-done((f32[4,48,1024]{2,1,0:T(8,128)S(1)}, f32[4,48,1024]{2,1,0:T(8,128)S(1)}, u32[]{:S(2)}, u32[]{:S(2)}) %collective-permute-start) | collective-permute-done | bytes 786464 | tf_op jit(solution)/shard_map/ppermute | solution.py:235
  45.7 51.1 %response.1 = f32[1536,256]{1,0:T(8,128)} custom-call(s32[1536]{0:T(1024)} %mul.118.occ_ref, s32[1536]{0:T(1024)} %mul.120.vir_ref, s32[256]{0:T(256)} %mul.114.occ_own_ref, s32[256]{0:T(256)} %mul.116.vir_own_ref, f32[48,128]{1,0:T(8,128)} %bitcast.138, f32[6144,1024]{1,0:T(8,128)} %band_ref.3), custom_call_target="tpu_custom_call" | custom-call | flops 14495514624 | bytes 25165824 | tf_op jit(solution)/shard_map/response/pallas_call | solution.py:173
  96.9 2.1 %dynamic-slice_bitcast_fusion = f32[4,192,256]{2,1,0:T(8,128)} fusion(f32[2,4,192,256]{3,2,1,0:T(8,128)} %bitcast.114, s32[]{:T(128)S(6)} %select_n.120), kind=kLoop, calls=%fused_computation.11 | loop fusion | bytes 1572868 | tf_op jit(solution)/shard_map/jit(dynamic_index_in_dim)/squeeze | solution.py:227
  101.3 1.6 collective-permute-start.2
  103.9 2.0 %collective-permute-start.4 = (f32[48,1024]{1,0:T(8,128)S(1)}, f32[48,1024]{1,0:T(8,128)}, u32[]{:S(2)}, u32[]{:S(2)}) collective-permute-start(f32[48,1024]{1,0:T(8,128)S(1)} %get-tuple-element.23), channel_id=1, source_target_pairs={{0,12},{2,14},{4,0},{6,2},{8,4},{10,6},{12,8},{14,10},{1,13},{3,15... | collective-permute-start | bytes 589832 | tf_op jit(solution)/shard_map/ppermute | solution.py:240
  112.0 4.7 %collective-permute-done.2 = f32[48,1024]{1,0:T(8,128)S(1)} collective-permute-done((f32[48,1024]{1,0:T(8,128)}, f32[48,1024]{1,0:T(8,128)S(1)}, u32[]{:S(2)}, u32[]{:S(2)}) %collective-permute-start.2) | collective-permute-done | bytes 196640 | tf_op jit(solution)/shard_map/ppermute | solution.py:240
  116.8 3.8 %collective-permute-done.3 = f32[48,1024]{1,0:T(8,128)} collective-permute-done((f32[48,1024]{1,0:T(8,128)}, f32[48,1024]{1,0:T(8,128)}, u32[]{:S(2)}, u32[]{:S(2)}) %collective-permute-start.3) | collective-permute-done | bytes 196640 | tf_op jit(solution)/shard_map/ppermute | solution.py:240
  120.6 1.8 collective-permute-done.4
  123.7 1.6 collective-permute-start.5
  125.4 1.7 collective-permute-start.8
  127.1 1.9 %collective-permute-start.9 = (f32[192,256]{1,0:T(8,128)S(1)}, f32[192,256]{1,0:T(8,128)S(1)}, u32[]{:S(2)}, u32[]{:S(2)}) collective-permute-start(f32[192,256]{1,0:T(8,128)S(1)} %get-tuple-element.20), channel_id=1, source_target_pairs={{0,12},{2,14},{4,0},{6,2},{8,4},{10,6},{12,8},{14,10},{1,13},{3,15... | collective-permute-start | bytes 589832 | tf_op jit(solution)/shard_map/ppermute | solution.py:240
  133.2 9.2 %collective-permute-done.8 = f32[192,256]{1,0:T(8,128)S(1)} collective-permute-done((f32[192,256]{1,0:T(8,128)S(1)}, f32[192,256]{1,0:T(8,128)S(1)}, u32[]{:S(2)}, u32[]{:S(2)}) %collective-permute-start.8) | collective-permute-done | bytes 196640 | tf_op jit(solution)/shard_map/ppermute | solution.py:240
  144.2 1.9 collective-permute-start.15
  146.0 1.9 %collective-permute-start.16 = (f32[32,1024]{1,0:T(8,128)S(1)}, f32[32,1024]{1,0:T(8,128)S(1)}, u32[]{:S(2)}, u32[]{:S(2)}) collective-permute-start(f32[32,1024]{1,0:T(8,128)S(1)} %slice.103), channel_id=1, source_target_pairs={{0,12},{2,14},{4,0},{6,2},{8,4},{10,6},{12,8},{14,10},{1,13},{3,15... | collective-permute-start | bytes 393224 | tf_op jit(solution)/shard_map/ppermute | solution.py:282
  148.0 2.5 %collective-permute-done.14 = f32[32,1024]{1,0:T(8,128)S(1)} collective-permute-done((f32[32,1024]{1,0:T(8,128)S(1)}, f32[32,1024]{1,0:T(8,128)S(1)}, u32[]{:S(2)}, u32[]{:S(2)}) %collective-permute-start.14) | collective-permute-done | bytes 131104 | tf_op jit(solution)/shard_map/ppermute | solution.py:282
  150.5 5.3 %collective-permute-done.15 = f32[32,1024]{1,0:T(8,128)S(1)} collective-permute-done((f32[32,1024]{1,0:T(8,128)S(1)}, f32[32,1024]{1,0:T(8,128)S(1)}, u32[]{:S(2)}, u32[]{:S(2)}) %collective-permute-start.15) | collective-permute-done | bytes 131104 | tf_op jit(solution)/shard_map/ppermute | solution.py:282
  164.8 1.9 collective-permute-start.12
  166.8 1.9 %collective-permute-start.13 = (f32[128,256]{1,0:T(8,128)S(1)}, f32[128,256]{1,0:T(8,128)S(1)}, u32[]{:S(2)}, u32[]{:S(2)}) collective-permute-start(f32[128,256]{1,0:T(8,128)S(1)} %get-tuple-element.28), channel_id=1, source_target_pairs={{0,12},{2,14},{4,0},{6,2},{8,4},{10,6},{12,8},{14,10},{1,13},{3,15... | collective-permute-start | bytes 393224 | tf_op jit(solution)/shard_map/ppermute | solution.py:240
  169.0 2.2 %collective-permute-done.11 = f32[128,256]{1,0:T(8,128)S(1)} collective-permute-done((f32[128,256]{1,0:T(8,128)S(1)}, f32[128,256]{1,0:T(8,128)S(1)}, u32[]{:S(2)}, u32[]{:S(2)}) %collective-permute-start.11) | collective-permute-done | bytes 131104 | tf_op jit(solution)/shard_map/ppermute | solution.py:240
  171.2 5.7 %collective-permute-done.12 = f32[128,256]{1,0:T(8,128)S(1)} collective-permute-done((f32[128,256]{1,0:T(8,128)S(1)}, f32[128,256]{1,0:T(8,128)S(1)}, u32[]{:S(2)}, u32[]{:S(2)}) %collective-permute-start.12) | collective-permute-done | bytes 131104 | tf_op jit(solution)/shard_map/ppermute | solution.py:240
  176.8 2.3 %collective-permute-done.13 = f32[128,256]{1,0:T(8,128)S(1)} collective-permute-done((f32[128,256]{1,0:T(8,128)S(1)}, f32[128,256]{1,0:T(8,128)S(1)}, u32[]{:S(2)}, u32[]{:S(2)}) %collective-permute-start.13) | collective-permute-done | bytes 131104 | tf_op jit(solution)/shard_map/ppermute | solution.py:240
  180.7 7.8 %collective-permute-done.18 = f32[64,2,512]{2,0,1:T(8,128)S(1)} collective-permute-done((f32[64,2,512]{2,0,1:T(8,128)S(1)}, f32[64,2,512]{2,0,1:T(8,128)S(1)}, u32[]{:S(2)}, u32[]{:S(2)}) %collective-permute-start.18) | collective-permute-done | bytes 262176 | tf_op jit(solution)/shard_map/ppermute | solution.py:308
  190.0 3.5 %collective-permute-done.19 = f32[64,512]{1,0:T(8,128)S(1)} collective-permute-done((f32[64,512]{1,0:T(8,128)S(1)}, f32[64,512]{1,0:T(8,128)S(1)}, u32[]{:S(2)}, u32[]{:S(2)}) %collective-permute-start.19) | collective-permute-done | bytes 131104 | tf_op jit(solution)/shard_map/ppermute | solution.py:311
  (106 shorter events, 38.7 us)
Async XLA Ops:
  40.5 3.7 %copy-start.2 = (f32[384,1024]{1,0:T(8,128)S(1)}, f32[384,1024]{1,0:T(8,128)}, u32[]{:S(2)}) copy-start(f32[384,1024]{1,0:T(8,128)} %coupling.1) | copy-start | bytes 4718596
  41.8 2.4 %collective-permute-start = (f32[4,48,1024]{2,1,0:T(8,128)S(1)}, f32[4,48,1024]{2,1,0:T(8,128)S(1)}, u32[]{:S(2)}, u32[]{:S(2)}) collective-permute-start(f32[4,48,1024]{2,1,0:T(8,128)S(1)} %dynamic-slice_bitcast_fusion.1), channel_id=1, source_target_pairs={{0,2},{2,0},{4,6},{6,4},{8,10},{10,8},{12,14},{14,12},{1,3},{3,1},... | collective-permute-start | bytes 2359304 | tf_op jit(solution)/shard_map/ppermute | solution.py:235
  98.9 24.5 %copy-start.1 = (f32[1536,256]{1,0:T(8,128)S(1)}, f32[1536,256]{1,0:T(8,128)}, u32[]{:S(2)}) copy-start(f32[1536,256]{1,0:T(8,128)} %response.1) | copy-start | bytes 4718596
  98.9 24.5 %collective-permute-start.1 = (f32[4,192,256]{2,1,0:T(8,128)}, f32[4,192,256]{2,1,0:T(8,128)S(1)}, u32[]{:S(2)}, u32[]{:S(2)}) collective-permute-start(f32[4,192,256]{2,1,0:T(8,128)} %dynamic-slice_bitcast_fusion), channel_id=1, source_target_pairs={{0,2},{2,0},{4,6},{6,4},{8,10},{10,8},{12,14},{14,12},{1,3},{3,1},... | collective-permute-start | bytes 2359304 | tf_op jit(solution)/shard_map/ppermute | solution.py:235
  101.3 15.4 %collective-permute-start.2 = (f32[48,1024]{1,0:T(8,128)}, f32[48,1024]{1,0:T(8,128)S(1)}, u32[]{:S(2)}, u32[]{:S(2)}) collective-permute-start(f32[48,1024]{1,0:T(8,128)} %get-tuple-element.22), channel_id=1, source_target_pairs={{0,4},{2,6},{4,8},{6,10},{8,12},{10,14},{12,0},{14,2},{1,5},{3,7},... | collective-permute-start | bytes 589832 | tf_op jit(solution)/shard_map/ppermute | solution.py:240
  102.9 17.6 %collective-permute-start.3 = (f32[48,1024]{1,0:T(8,128)}, f32[48,1024]{1,0:T(8,128)}, u32[]{:S(2)}, u32[]{:S(2)}) collective-permute-start(f32[48,1024]{1,0:T(8,128)} %get-tuple-element.24), channel_id=1, source_target_pairs={{0,8},{2,10},{4,12},{6,14},{8,0},{10,2},{12,4},{14,6},{1,9},{3,11}... | collective-permute-start | bytes 589832 | tf_op jit(solution)/shard_map/ppermute | solution.py:240
  103.9 18.4 %collective-permute-start.4 = (f32[48,1024]{1,0:T(8,128)S(1)}, f32[48,1024]{1,0:T(8,128)}, u32[]{:S(2)}, u32[]{:S(2)}) collective-permute-start(f32[48,1024]{1,0:T(8,128)S(1)} %get-tuple-element.23), channel_id=1, source_target_pairs={{0,12},{2,14},{4,0},{6,2},{8,4},{10,6},{12,8},{14,10},{1,13},{3,15... | collective-permute-start | bytes 589832 | tf_op jit(solution)/shard_map/ppermute | solution.py:240
  123.7 6.9 %collective-permute-start.5 = (f32[48,1024]{1,0:T(8,128)S(1)}, f32[48,1024]{1,0:T(8,128)S(1)}, u32[]{:S(2)}, u32[]{:S(2)}) collective-permute-start(f32[48,1024]{1,0:T(8,128)S(1)} %broadcast_multiply_fusion), channel_id=1, source_target_pairs={{0,1},{1,0},{2,3},{3,2},{4,5},{5,4},{6,7},{7,6},{8,9},{9,8},{10,11... | collective-permute-start | bytes 589832 | tf_op jit(solution)/shard_map/ppermute | solution.py:250
  125.3 18.7 %copy-start.4 = (f32[192]{0:T(256)S(1)}, f32[192]{0:T(256)}, u32[]{:S(2)}) copy-start(f32[192]{0:T(256)} %mul.126) | copy-start | bytes 2308
  125.3 18.7 %copy-start.5 = (f32[256]{0:T(256)S(1)}, f32[256]{0:T(256)}, u32[]{:S(2)}) copy-start(f32[256]{0:T(256)} %mul.128) | copy-start | bytes 3076
  125.4 7.9 %collective-permute-start.7 = (f32[192,256]{1,0:T(8,128)S(1)}, f32[192,256]{1,0:T(8,128)S(1)}, u32[]{:S(2)}, u32[]{:S(2)}) collective-permute-start(f32[192,256]{1,0:T(8,128)S(1)} %get-tuple-element.19), channel_id=1, source_target_pairs={{0,4},{2,6},{4,8},{6,10},{8,12},{10,14},{12,0},{14,2},{1,5},{3,7},... | collective-permute-start | bytes 589832 | tf_op jit(solution)/shard_map/ppermute | solution.py:240
  125.4 17.0 %collective-permute-start.8 = (f32[192,256]{1,0:T(8,128)S(1)}, f32[192,256]{1,0:T(8,128)S(1)}, u32[]{:S(2)}, u32[]{:S(2)}) collective-permute-start(f32[192,256]{1,0:T(8,128)S(1)} %get-tuple-element.21), channel_id=1, source_target_pairs={{0,8},{2,10},{4,12},{6,14},{8,0},{10,2},{12,4},{14,6},{1,9},{3,11}... | collective-permute-start | bytes 589832 | tf_op jit(solution)/shard_map/ppermute | solution.py:240
  127.1 16.9 %collective-permute-start.9 = (f32[192,256]{1,0:T(8,128)S(1)}, f32[192,256]{1,0:T(8,128)S(1)}, u32[]{:S(2)}, u32[]{:S(2)}) collective-permute-start(f32[192,256]{1,0:T(8,128)S(1)} %get-tuple-element.20), channel_id=1, source_target_pairs={{0,12},{2,14},{4,0},{6,2},{8,4},{10,6},{12,8},{14,10},{1,13},{3,15... | collective-permute-start | bytes 589832 | tf_op jit(solution)/shard_map/ppermute | solution.py:240
  130.6 27.9 %collective-permute-start.6 = (f32[2,48,1024]{2,1,0:T(8,128)S(1)}, f32[2,48,1024]{2,1,0:T(8,128)S(1)}, u32[]{:S(2)}, u32[]{:S(2)}) collective-permute-start(f32[2,48,1024]{2,1,0:T(8,128)S(1)} %reverse_select_fusion.1), channel_id=1, source_target_pairs={{0,16},{16,0},{1,17},{17,1},{2,18},{18,2},{3,19},{19,3},{4,20},{20... | collective-permute-start | bytes 1179656 | tf_op jit(solution)/shard_map/ppermute | solution.py:253
  144.1 6.4 %collective-permute-start.14 = (f32[32,1024]{1,0:T(8,128)S(1)}, f32[32,1024]{1,0:T(8,128)S(1)}, u32[]{:S(2)}, u32[]{:S(2)}) collective-permute-start(f32[32,1024]{1,0:T(8,128)S(1)} %slice.103), channel_id=1, source_target_pairs={{0,4},{2,6},{4,8},{6,10},{8,12},{10,14},{12,0},{14,2},{1,5},{3,7},... | collective-permute-start | bytes 393224 | tf_op jit(solution)/shard_map/ppermute | solution.py:282
  144.2 11.6 %collective-permute-start.15 = (f32[32,1024]{1,0:T(8,128)S(1)}, f32[32,1024]{1,0:T(8,128)S(1)}, u32[]{:S(2)}, u32[]{:S(2)}) collective-permute-start(f32[32,1024]{1,0:T(8,128)S(1)} %slice.103), channel_id=1, source_target_pairs={{0,8},{2,10},{4,12},{6,14},{8,0},{10,2},{12,4},{14,6},{1,9},{3,11}... | collective-permute-start | bytes 393224 | tf_op jit(solution)/shard_map/ppermute | solution.py:282
  146.0 11.3 %collective-permute-start.16 = (f32[32,1024]{1,0:T(8,128)S(1)}, f32[32,1024]{1,0:T(8,128)S(1)}, u32[]{:S(2)}, u32[]{:S(2)}) collective-permute-start(f32[32,1024]{1,0:T(8,128)S(1)} %slice.103), channel_id=1, source_target_pairs={{0,12},{2,14},{4,0},{6,2},{8,4},{10,6},{12,8},{14,10},{1,13},{3,15... | collective-permute-start | bytes 393224 | tf_op jit(solution)/shard_map/ppermute | solution.py:282
  158.5 3.4 %collective-permute-start.17 = (f32[4,32,1024]{2,1,0:T(8,128)}, f32[4,32,1024]{2,1,0:T(8,128)}, u32[]{:S(2)}, u32[]{:S(2)}) collective-permute-start(f32[4,32,1024]{2,1,0:T(8,128)} %get-tuple-element.31), channel_id=1, source_target_pairs={{0,2},{2,0},{4,6},{6,4},{8,10},{10,8},{12,14},{14,12},{1,3},{3,1},... | collective-permute-start | bytes 1572872 | tf_op jit(solution)/shard_map/ppermute | solution.py:284
  161.2 2.4 %collective-permute-start.10 = (f32[4,128,256]{2,1,0:T(8,128)}, f32[4,128,256]{2,1,0:T(8,128)}, u32[]{:S(2)}, u32[]{:S(2)}) collective-permute-start(f32[4,128,256]{2,1,0:T(8,128)} %dynamic-slice_bitcast_fusion.2), channel_id=1, source_target_pairs={{0,2},{2,0},{4,6},{6,4},{8,10},{10,8},{12,14},{14,12},{1,3},{3,1},... | collective-permute-start | bytes 1572872 | tf_op jit(solution)/shard_map/ppermute | solution.py:235
  164.8 6.4 %collective-permute-start.11 = (f32[128,256]{1,0:T(8,128)S(1)}, f32[128,256]{1,0:T(8,128)S(1)}, u32[]{:S(2)}, u32[]{:S(2)}) collective-permute-start(f32[128,256]{1,0:T(8,128)S(1)} %get-tuple-element.27), channel_id=1, source_target_pairs={{0,4},{2,6},{4,8},{6,10},{8,12},{10,14},{12,0},{14,2},{1,5},{3,7},... | collective-permute-start | bytes 393224 | tf_op jit(solution)/shard_map/ppermute | solution.py:240
  164.8 12.0 %collective-permute-start.12 = (f32[128,256]{1,0:T(8,128)S(1)}, f32[128,256]{1,0:T(8,128)S(1)}, u32[]{:S(2)}, u32[]{:S(2)}) collective-permute-start(f32[128,256]{1,0:T(8,128)S(1)} %get-tuple-element.29), channel_id=1, source_target_pairs={{0,8},{2,10},{4,12},{6,14},{8,0},{10,2},{12,4},{14,6},{1,9},{3,11}... | collective-permute-start | bytes 393224 | tf_op jit(solution)/shard_map/ppermute | solution.py:240
  166.8 12.4 %collective-permute-start.13 = (f32[128,256]{1,0:T(8,128)S(1)}, f32[128,256]{1,0:T(8,128)S(1)}, u32[]{:S(2)}, u32[]{:S(2)}) collective-permute-start(f32[128,256]{1,0:T(8,128)S(1)} %get-tuple-element.28), channel_id=1, source_target_pairs={{0,12},{2,14},{4,0},{6,2},{8,4},{10,6},{12,8},{14,10},{1,13},{3,15... | collective-permute-start | bytes 393224 | tf_op jit(solution)/shard_map/ppermute | solution.py:240
  180.1 8.3 %collective-permute-start.18 = (f32[64,2,512]{2,0,1:T(8,128)S(1)}, f32[64,2,512]{2,0,1:T(8,128)S(1)}, u32[]{:S(2)}, u32[]{:S(2)}) collective-permute-start(f32[64,2,512]{2,0,1:T(8,128)S(1)} %bitcast.120), channel_id=1, source_target_pairs={{0,1},{1,0},{2,3},{3,2},{4,5},{5,4},{6,7},{7,6},{8,9},{9,8},{10,11... | collective-permute-start | bytes 786440 | tf_op jit(solution)/shard_map/ppermute | solution.py:308
  188.5 5.0 %collective-permute-start.19 = (f32[64,512]{1,0:T(8,128)S(1)}, f32[64,512]{1,0:T(8,128)S(1)}, u32[]{:S(2)}, u32[]{:S(2)}) collective-permute-start(f32[64,512]{1,0:T(8,128)S(1)} %dynamic-slice_bitcast_fusion.9), channel_id=1, source_target_pairs={{0,16},{16,0},{1,17},{17,1},{2,18},{18,2},{3,19},{19,3},{4,20},{20... | collective-permute-start | bytes 393224 | tf_op jit(solution)/shard_map/ppermute | solution.py:311
  (5 other events, 12.6 us)

commit v3 on v2

v3 whole, which is shorter than its diff:
```python
import functools
import math

import jax
import jax.numpy as jnp
from jax import lax
from jax.experimental import pallas as pl
from jax.experimental.pallas import tpu as pltpu
from jax.sharding import PartitionSpec as P

PANEL = 512
LANES = 128
CHUNK = 1024
SLICES = 4
PAIR_SLICES = 8
VMEM_BYTES = 60 * 2**20


def split(value):
    high = value.astype(jnp.bfloat16)
    return high, (value - high.astype(jnp.float32)).astype(jnp.bfloat16)


def three_pass(left_high, left_low, right_high, right_low):
    def dot(left, right):
        return jnp.dot(left, right, preferred_element_type=jnp.float32)

    return dot(left_high, right_high) + (dot(left_low, right_high) + dot(left_high, right_low))


def pair_position(place, lines, blocks, window, pairs):
    inside, outside = window // (2 * lines * blocks), (pairs - window) // (2 * lines * blocks)
    rest, place = divmod(place, inside + outside)
    rest, block = divmod(rest, blocks)
    core, line = divmod(rest, lines)
    share = (line * 2 + core) * blocks + block
    if place < inside:
        return share * inside + place, inside
    return window + share * outside + place - inside, outside


def coupling_kernel(
    shape, block_ref, occ_ref, vir_ref, coulomb_ref, band_ref, out_ref, turned_ref,
    incoming, arrived, turned_even, turned_odd, handed, products,
    left_high_even, left_high_odd, left_low_even, left_low_odd, right_high, right_low,
):
    turned = turned_even, turned_odd
    left_high, left_low = (left_high_even, left_high_odd), (left_low_even, left_low_odd)
    chunk, bands = incoming.shape[1:]
    chunks = band_ref.shape[0] // chunk
    groups = chunk // LANES
    stride = products.shape[0] // out_ref.shape[0]
    pairs = out_ref.shape[0]
    lines, blocks, window = shape
    count = pairs // SLICES
    width = bands // SLICES
    block = block_ref[0]

    def fetch(c):
        slot = lax.rem(c, 3)
        return pltpu.make_async_copy(
            band_ref.at[pl.ds(c * chunk, chunk), :], incoming.at[slot], arrived.at[slot]
        )

    def hand_on(c, parity):
        return pltpu.make_async_copy(turned[parity], turned_ref.at[c], handed.at[parity])

    def turn(c, parity, part):
        flat = turned[parity].reshape(bands * groups, LANES)
        for group in range(part, groups, SLICES):
            rows = pl.ds(group * LANES, LANES)
            flat[pl.ds(group, bands, stride=groups), :] = incoming[lax.rem(c, 3), rows, :].T

    def prepare(c, parity, part):
        here = pl.ds(part * width, width)
        right_high[:, here], right_low[:, here] = split(incoming[lax.rem(c, 3), :, here])
        for pair in range(part * count, part * count + count):
            per_share = pairs // (2 * lines)
            share, place = divmod(pair, per_share)
            index, step = pair_position(
                share * per_share * blocks + place, lines, blocks, window, occ_ref.shape[0]
            )
            index = index + block * step
            products[pl.ds(pair * stride, groups), :] = (
                turned[parity][occ_ref[index]] * turned[parity][vir_ref[index]]
            )
        for group in range(groups):
            weight = coulomb_ref[pl.ds(lax.rem(c, chunks) * groups + group, 1), :]
            value = products[pl.ds(part * count * stride + group, count, stride=stride), :]
            here = pl.ds(part * count, count)
            there = pl.ds(group * LANES, LANES)
            left_high[parity][here, there], left_low[parity][here, there] = split(value * weight)

    def multiply(parity, part):
        here = pl.ds(part * width, width)
        out_ref[:, here] += three_pass(
            left_high[parity][...], left_low[parity][...], right_high[:, here], right_low[:, here]
        )

    for c in range(min(3, chunks)):
        fetch(c).start()
    out_ref[...] = jnp.zeros_like(out_ref)
    fetch(0).wait()
    for part in range(SLICES):
        turn(0, 0, part)
    hand_on(0, 0).start()
    if chunks > 1:
        fetch(1).wait()
    for part in range(SLICES):
        if chunks > 1:
            turn(1, 1, part)
        prepare(0, 0, part)
    if chunks > 1:
        hand_on(1, 1).start()

    def advance(c, parity):
        @pl.when(c + 2 < chunks)
        def _():
            fetch(c + 2).wait()

        @pl.when(c + 3 < chunks)
        def _():
            fetch(c + 3).start()

        hand_on(c, parity).wait()
        for part in range(SLICES):
            multiply(parity, part)
            turn(c + 2, parity, part)
            prepare(c + 1, 1 - parity, part)

        @pl.when(c + 2 < chunks)
        def _():
            hand_on(c + 2, parity).start()

    @pl.loop(0, chunks // 2)
    def _(index):
        advance(2 * index, 0)
        advance(2 * index + 1, 1)

    if chunks % 2:
        advance(chunks - 1, 0)


def pair_coupling(band_vectors, coulomb, occ, vir, block, shape):
    basis_rows, bands = band_vectors.shape
    lines, blocks, window = shape
    pairs = occ.shape[0] // blocks
    chunk = math.gcd(CHUNK, basis_rows)
    groups = chunk // LANES
    stride = groups + 1 - groups % 2
    half = jnp.bfloat16
    scalars = pl.BlockSpec(memory_space=pltpu.SMEM)
    whole = pl.BlockSpec(memory_space=pltpu.VMEM)
    outside = pl.BlockSpec(memory_space=pl.ANY)
    return pl.pallas_call(
        functools.partial(coupling_kernel, shape),
        in_specs=[scalars] * 3 + [whole, outside],
        out_specs=[whole, outside],
        out_shape=[
            jax.ShapeDtypeStruct((pairs, bands), jnp.float32),
            jax.ShapeDtypeStruct((basis_rows // chunk, bands, groups, LANES), jnp.float32),
        ],
        scratch_shapes=[
            pltpu.VMEM((3, chunk, bands), jnp.float32),
            pltpu.SemaphoreType.DMA((3,)),
            pltpu.VMEM((bands, groups, LANES), jnp.float32),
            pltpu.VMEM((bands, groups, LANES), jnp.float32),
            pltpu.SemaphoreType.DMA((2,)),
            pltpu.VMEM((pairs * stride, LANES), jnp.float32),
        ]
        + [pltpu.VMEM((pairs, chunk), half)] * 4
        + [pltpu.VMEM((chunk, bands), half)] * 2,
        compiler_params=pltpu.CompilerParams(vmem_limit_bytes=VMEM_BYTES),
        cost_estimate=pl.CostEstimate(
            flops=6 * basis_rows * pairs * bands,
            bytes_accessed=8 * basis_rows * bands,
            transcendentals=0,
        ),
        name="coupling",
    )(block, occ, vir, coulomb.reshape(basis_rows // LANES, LANES), band_vectors)


def response_kernel(
    shape, block_ref, occ_ref, vir_ref, coulomb_ref, turned_ref, out_ref,
    turned, arrived, products, left_high_even, left_high_odd, left_low_even, left_low_odd,
    right_high, right_low,
):
    left_high, left_low = (left_high_even, left_high_odd), (left_low_even, left_low_odd)
    chunks, bands, groups, _ = turned_ref.shape
    pairs, own = out_ref.shape
    lines, blocks, window = shape
    height = left_high_even.shape[0]
    slices = pairs // height
    every = chunks * groups
    block = block_ref[0]
    inside, outside = window // (2 * lines * blocks), (pairs - window) // (2 * lines * blocks)
    half_slices = slices // 2
    per_slice = lines // half_slices

    def fetch(c):
        here = pl.ds(pl.multiple_of(c * groups, groups), groups)
        return pltpu.make_async_copy(turned_ref.at[c], turned.at[:, here, :], arrived.at[c])

    def gather(index, place, here, stride):
        products[pl.ds(place * stride, here.size), :] = (
            turned[occ_ref[index], here, :] * turned[vir_ref[index], here, :]
        )

    def gather_slice(i, here, stride):
        first = (lax.rem(i, half_slices) * (per_slice * 2) + lax.div(i, half_slices)) * blocks
        for pair in range(height):
            share, place = divmod(pair, blocks * (inside + outside))
            part, place = divmod(place, inside + outside)
            index = share * 2 * blocks + part
            if place < inside:
                index = first * inside + (index * inside + place)
            else:
                index = first * outside + (window + index * outside + place - inside)
            gather(index, pair, here, stride)

    def split_slice(parity, base, count, stride):
        for group in range(count):
            there = pl.ds(base + group * LANES, LANES)
            left_high[parity][:, there], left_low[parity][:, there] = split(
                products[pl.ds(group, height, stride=stride), :]
            )

    def multiply(i, parity):
        here = pl.ds(pl.multiple_of(i * height, height), height)
        out_ref[here, :] = three_pass(
            left_high[parity][...], left_low[parity][...], right_high[...], right_low[...]
        )

    for c in range(chunks):
        fetch(c).start()

    @pl.loop(0, chunks)
    def _(c):
        fetch(c).wait()
        here = pl.ds(pl.multiple_of(c * groups, groups), groups)
        base = pl.multiple_of(c * (groups * LANES), LANES)
        stride = groups + 1 - groups % 2
        for pair in range(own):
            share, place = divmod(pair, inside)
            gather(block * inside + (share * blocks * inside + place), pair, here, stride)
        for group in range(groups):
            weight = coulomb_ref[pl.ds(c * groups + group, 1), :]
            value = products[pl.ds(group, own, stride=stride), :] * weight
            there = pl.ds(base + group * LANES, LANES)
            right_high[there, :], right_low[there, :] = split(value.T)
        gather_slice(0, here, stride)
        split_slice(0, base, groups, stride)

    stride = every + 1 - every % 2

    @pl.loop(0, slices // 2)
    def _(index):
        for parity in range(2):
            multiply(2 * index + parity, parity)
            after = jnp.minimum(2 * index + parity + 1, slices - 1)
            gather_slice(after, pl.ds(0, every), stride)
            split_slice(1 - parity, 0, every, stride)


def pair_response(turned, coulomb, occ, vir, block, shape):
    steps, bands, groups, _ = turned.shape
    lines, blocks, window = shape
    pairs = occ.shape[0]
    own = window // blocks
    every = steps * groups
    basis_rows = every * LANES
    height = pairs // PAIR_SLICES
    places = max(height * (every + 1 - every % 2), own * (groups + 1 - groups % 2))
    half = jnp.bfloat16
    scalars = pl.BlockSpec(memory_space=pltpu.SMEM)
    whole = pl.BlockSpec(memory_space=pltpu.VMEM)
    return pl.pallas_call(
        functools.partial(response_kernel, shape),
        in_specs=[scalars] * 3 + [whole, pl.BlockSpec(memory_space=pl.ANY)],
        out_specs=whole,
        out_shape=jax.ShapeDtypeStruct((pairs, own), jnp.float32),
        scratch_shapes=[
            pltpu.VMEM((bands, every, LANES), jnp.float32),
            pltpu.SemaphoreType.DMA((steps,)),
            pltpu.VMEM((places, LANES), jnp.float32),
        ]
        + [pltpu.VMEM((height, basis_rows), half)] * 4
        + [pltpu.VMEM((basis_rows, own), half)] * 2,
        compiler_params=pltpu.CompilerParams(vmem_limit_bytes=VMEM_BYTES),
        cost_estimate=pl.CostEstimate(
            flops=6 * basis_rows * pairs * own,
            bytes_accessed=4 * basis_rows * bands,
            transcendentals=0,
        ),
        name="response",
    )(block, occ, vir, coulomb.reshape(basis_rows // LANES, LANES), turned)


def per_device(band_vectors, coulomb, pair_weight, occ_index, vir_index, freq_index, freq_table):
    row_count = lax.axis_size("rows")
    col_count = lax.axis_size("cols")
    group_count = lax.axis_size("grp")
    blocks = col_count * group_count
    lines = row_count // 2
    row = lax.axis_index("rows")
    core, line = lax.rem(row, 2), lax.div(row, 2)
    column = lax.axis_index("cols")
    group = lax.axis_index("grp")
    block = group * col_count + column
    basis_rows, bands = band_vectors.shape
    pairs = occ_index.shape[0]
    window = PANEL * group_count
    basis = basis_rows * row_count

    def ordered(values):
        def shares(part):
            return part.reshape(lines, 2, blocks, -1).swapaxes(0, 1)

        return jnp.concatenate([shares(values[:window]), shares(values[window:])], axis=3)

    def own_window(values):
        shaped = values[:window].reshape(row_count, blocks, -1)
        return pick(shaped, block, 1).reshape(-1)

    def pick(values, index, axis=0):
        return lax.dynamic_index_in_dim(values, index, axis, keepdims=False)

    other_core = [(i, i ^ 1) for i in range(row_count)]

    def shift(step):
        return [(i, (i // 2 + step) % lines * 2 + i % 2) for i in range(row_count)]

    def add_cores(values):
        received = lax.ppermute(pick(values, 1 - core), "rows", other_core)
        return pick(values, core) + received

    def scatter_lines(values):
        arrived = [
            lax.ppermute(pick(values, lax.rem(line + step, lines)), "rows", shift(step))
            for step in range(1, lines)
        ]
        total = pick(values, line)
        for value in arrived:
            total = total + value
        return total

    def gather_blocks(values):
        across = [(i, i ^ 1) for i in range(col_count)]
        pair = jnp.stack([values, lax.ppermute(values, "cols", across)])
        pair = jnp.where(column == 0, pair, pair[::-1])
        across = [(i, i ^ 1) for i in range(group_count)]
        quad = jnp.stack([pair, lax.ppermute(pair, "grp", across)])
        quad = jnp.where(group == 0, quad, quad[::-1])
        return quad.reshape((blocks,) + values.shape)

    weights = ordered(pair_weight)
    shape = (lines, blocks, window)
    place = block.reshape(1)
    partial_coupling, turned = pair_coupling(
        band_vectors, coulomb, occ_index, vir_index, place, shape
    )
    share = pairs // row_count
    partial_coupling = add_cores(partial_coupling.reshape(2, lines, share // blocks, bands))
    partial_coupling, turned = lax.optimization_barrier((partial_coupling, turned))
    partial_response = pair_response(turned, coulomb, occ_index, vir_index, place, shape)
    coupling = scatter_lines(partial_coupling)
    partial_response, coupling = lax.optimization_barrier((partial_response, coupling))
    partial_response = add_cores(partial_response.reshape(2, lines, share, window // blocks))
    partial_response, coupling = lax.optimization_barrier((partial_response, coupling))
    own_weights = pick(pick(weights, core), line)
    coupling = coupling * (pick(own_weights, block)[:, None] * (1.0 / math.sqrt(basis)))
    all_coupling = gather_blocks(coupling).reshape(share, bands)
    response = scatter_lines(partial_response)
    response = response * (
        own_weights.reshape(-1)[:, None] * own_window(pair_weight)[None, :] * (1.0 / basis)
    )
    sub = window // (row_count * blocks)
    response, part = lax.optimization_barrier((response, coupling[:sub]))
    parts = [part] + [lax.ppermute(part, "rows", shift(step)) for step in range(1, lines)]
    parts = jnp.stack(parts)
    beside = lax.ppermute(parts, "rows", other_core)
    both = jnp.where(core == 0, jnp.stack([parts, beside], 1), jnp.stack([beside, parts], 1))
    both = jnp.roll(both[::-1], line + 1, axis=0)
    window_coupling = both.reshape(row_count * sub, bands)

    matches = freq_index[:, None] == jnp.arange(freq_table.shape[0], dtype=jnp.int32)[None, :]
    band_weight = jnp.sum(jnp.where(matches, freq_table[None, :], 0.0), axis=1)
    mixed = lax.dot_general(
        all_coupling, response, (((0,), (0,)), ((), ())),
        precision=lax.Precision.HIGH, preferred_element_type=jnp.float32,
    )
    mixed = add_cores(mixed.reshape(lines, 2, bands // row_count, -1).swapaxes(0, 1))
    mixed = scatter_lines(mixed)
    energy = lax.dot_general(
        mixed, window_coupling, (((1,), (0,)), ((), ())),
        precision=lax.Precision.HIGH, preferred_element_type=jnp.float32,
    )
    here = bands // row_count
    own_band_weight = lax.dynamic_slice_in_dim(band_weight, row * here, here, 0)
    energy = energy * (
        own_band_weight[:, None] * band_weight[None, :] * (1.0 / math.sqrt(window))
    )
    energy = energy.reshape(col_count, here // col_count, group_count, bands // group_count)
    across = [(i, i ^ 1) for i in range(col_count)]
    received = lax.ppermute(pick(energy, 1 - column), "cols", across)
    energy = pick(energy, column) + received
    across = [(i, i ^ 1) for i in range(group_count)]
    received = lax.ppermute(pick(energy, 1 - group, 1), "grp", across)
    return pick(energy, group, 1) + received


def solution(mesh):
    placed = (P("rows", None), P("rows"), P(), P(), P(), P(), P())
    return jax.shard_map(
        per_device,
        mesh=mesh,
        in_specs=placed,
        out_specs=P(("rows", "cols"), "grp"),
        check_vma=False,
    )
```

time: 195 us -> 158 us (0.81)
  Pallas kernels: 85.6 us -> 73.1 us
  local copies, waits for them, and re-layouts: 19.3 us -> 6.84 us
  waiting for transfers between devices: 56.9 us -> 48.9 us
  other arithmetic: 8.72 us -> 5.55 us
    pallas_call x2, Pallas kernels: 85.6 us -> 73.1 us  [the longest x1 41.4 us: pair_response(): pl.pallas_call(functools.partial(response_kernel, shape), in_specs=[scala...]
    ppermute x9, waiting for transfers between devices: 32.4 us -> 23.8 us  [scatter_lines(): lax.ppermute(pick(values, lax.rem(line + step, lines)), 'rows', shift(step))]
    mul x8 -> x0, local copies, waits for them, and re-layouts: 4.01 us -> none  [the longest x3 1.36 us: pair_product(): occ * stride]
    mul x2, local copies, waits for them, and re-layouts: 2.66 us -> 0.16 us  [per_device(): own_weights.reshape(-1)[:, None] * own_window(pair_weight)[None, :]]
  transfers between devices with their start and end apart: 20 -> 20, of which waited for: 17 -> 15; matrix products, arithmetic and copies ran while one was open for 8% -> 5% of each run, Pallas kernels for 0% -> 26%
where the time goes in v3:
time: 158 us
  Pallas kernels  73.1 us (46%)
  waiting for transfers between devices  48.9 us (31%)
  starting transfers between devices  21.4 us (14%)
  local copies, waits for them, and re-layouts  6.84 us (4%)
  other arithmetic  5.55 us (4%)
    pallas_call x1, Pallas kernels, pair_response(): pl.pallas_call(functools.partial(response_kernel, shape), in_specs=[scala...  41.4 us
    pallas_call x1, Pallas kernels, pair_coupling(): pl.pallas_call(functools.partial(coupling_kernel, shape), in_specs=[scala...  31.7 us
    ppermute x9, waiting for transfers between devices, scatter_lines(): lax.ppermute(pick(values, lax.rem(line + step, lines)), 'rows', shift(step))  23.8 us
    ppermute x9, starting transfers between devices, scatter_lines(): lax.ppermute(pick(values, lax.rem(line + step, lines)), 'rows', shift(step))  13.4 us
    ppermute x3, waiting for transfers between devices, per_device(): lax.ppermute(part, 'rows', shift(step))  9.55 us
    ppermute x1, waiting for transfers between devices, per_device(): received = lax.ppermute(pick(energy, 1 - column), 'cols', across)  7.77 us
    squeeze x7, local copies, waits for them, and re-layouts, pick(): return lax.dynamic_index_in_dim(values, index, axis, keepdims=False)  3.62 us
    ppermute x1, waiting for transfers between devices, per_device(): received = lax.ppermute(pick(energy, 1 - group, 1), 'grp', across)  3.5 us
  transfers between devices with their start and end apart: 20, of which 15 were waited for; matrix products, arithmetic and copies ran while one was open for 5% of the time, Pallas kernels for 26%

profile of v3, /device:TPU:8, one launch (start us, length us, event | category | flops | bytes accessed | tf_op | source)
XLA Modules:
  0.0 157.6 jit_solution(10251467237298249436)
XLA Ops:
  0.0 31.7 %coupling.1 = (f32[384,1024]{1,0:T(8,128)}, f32[6,1024,8,128]{3,2,1,0:T(8,128)}) custom-call(s32[1]{0:T(128)} %bitcast.block_ref, s32[1536]{0:T(1024)} %occ_ref.3, s32[1536]{0:T(1024)} %vir_ref.3, f32[48,128]{1,0:T(8,128)} %bitcast.114, f32[6144,1024]{1,0:T(8,128)} %band_ref.1), custom_call_target="tpu_custom_call" | custom-call | flops 14495514624 | bytes 50331648 | tf_op jit(solution)/shard_map/coupling/pallas_call | solution.py:155
  31.8 1.3 dynamic-slice_bitcast_fusion.1
  33.2 2.2 %collective-permute-done = f32[4,48,1024]{2,1,0:T(8,128)S(1)} collective-permute-done((f32[4,48,1024]{2,1,0:T(8,128)S(1)}, f32[4,48,1024]{2,1,0:T(8,128)S(1)}, u32[]{:S(2)}, u32[]{:S(2)}) %collective-permute-start) | collective-permute-done | bytes 786464 | tf_op jit(solution)/shard_map/ppermute | solution.py:334
  35.6 1.6 %collective-permute-start.1 = (f32[48,1024]{1,0:T(8,128)S(1)}, f32[48,1024]{1,0:T(8,128)S(1)}, u32[]{:S(2)}, u32[]{:S(2)}) collective-permute-start(f32[48,1024]{1,0:T(8,128)S(1)} %get-tuple-element.28), channel_id=1, source_target_pairs={{0,4},{2,6},{4,8},{6,10},{8,12},{10,14},{12,0},{14,2},{1,5},{3,7},... | collective-permute-start | bytes 589832 | tf_op jit(solution)/shard_map/ppermute | solution.py:339
  38.3 1.9 %collective-permute-start.3 = (f32[48,1024]{1,0:T(8,128)S(1)}, f32[48,1024]{1,0:T(8,128)S(1)}, u32[]{:S(2)}, u32[]{:S(2)}) collective-permute-start(f32[48,1024]{1,0:T(8,128)S(1)} %get-tuple-element.29), channel_id=1, source_target_pairs={{0,12},{2,14},{4,0},{6,2},{8,4},{10,6},{12,8},{14,10},{1,13},{3,15... | collective-permute-start | bytes 589832 | tf_op jit(solution)/shard_map/ppermute | solution.py:339
  40.3 41.4 %response.1 = f32[1536,256]{1,0:T(8,128)} custom-call(s32[1]{0:T(128)} %bitcast.block_ref, s32[1536]{0:T(1024)} %occ_ref.3, s32[1536]{0:T(1024)} %vir_ref.3, f32[48,128]{1,0:T(8,128)} %bitcast.115, f32[6,1024,8,128]{3,2,1,0:T(8,128)} %get-tuple-element.17.turned_ref), custom_call_target="tpu_custom_call" | custom-call | flops 14495514624 | bytes 25165824 | tf_op jit(solution)/shard_map/response/pallas_call | solution.py:277
  81.8 1.3 dynamic-slice_bitcast_fusion
  85.6 1.6 %collective-permute-start.5 = (f32[48,1024]{1,0:T(8,128)S(1)}, f32[48,1024]{1,0:T(8,128)S(1)}, u32[]{:S(2)}, u32[]{:S(2)}) collective-permute-start(f32[48,1024]{1,0:T(8,128)S(1)} %broadcast_multiply_fusion), channel_id=1, source_target_pairs={{0,1},{1,0},{2,3},{3,2},{4,5},{5,4},{6,7},{7,6},{8,9},{9,8},{10,11... | collective-permute-start | bytes 589832 | tf_op jit(solution)/shard_map/ppermute | solution.py:349
  87.5 3.5 %collective-permute-start.8 = (f32[192,256]{1,0:T(8,128)S(1)}, f32[192,256]{1,0:T(8,128)S(1)}, u32[]{:S(2)}, u32[]{:S(2)}) collective-permute-start(f32[192,256]{1,0:T(8,128)S(1)} %get-tuple-element.27), channel_id=1, source_target_pairs={{0,8},{2,10},{4,12},{6,14},{8,0},{10,2},{12,4},{14,6},{1,9},{3,11}... | collective-permute-start | bytes 589832 | tf_op jit(solution)/shard_map/ppermute | solution.py:339
  91.1 1.6 collective-permute-done.5
  92.7 1.6 collective-permute-start.6
  95.1 9.4 %collective-permute-done.8 = f32[192,256]{1,0:T(8,128)S(1)} collective-permute-done((f32[192,256]{1,0:T(8,128)S(1)}, f32[192,256]{1,0:T(8,128)S(1)}, u32[]{:S(2)}, u32[]{:S(2)}) %collective-permute-start.8) | collective-permute-done | bytes 196640 | tf_op jit(solution)/shard_map/ppermute | solution.py:339
  104.5 3.4 %collective-permute-done.9 = f32[192,256]{1,0:T(8,128)S(1)} collective-permute-done((f32[192,256]{1,0:T(8,128)S(1)}, f32[192,256]{1,0:T(8,128)S(1)}, u32[]{:S(2)}, u32[]{:S(2)}) %collective-permute-start.9) | collective-permute-done | bytes 196640 | tf_op jit(solution)/shard_map/ppermute | solution.py:339
  108.3 1.8 %collective-permute-start.16 = (f32[32,1024]{1,0:T(8,128)S(1)}, f32[32,1024]{1,0:T(8,128)S(1)}, u32[]{:S(2)}, u32[]{:S(2)}) collective-permute-start(f32[32,1024]{1,0:T(8,128)S(1)} %slice.37), channel_id=1, source_target_pairs={{0,12},{2,14},{4,0},{6,2},{8,4},{10,6},{12,8},{14,10},{1,13},{3,15... | collective-permute-start | bytes 393224 | tf_op jit(solution)/shard_map/ppermute | solution.py:379
  110.1 4.4 %collective-permute-done.14 = f32[32,1024]{1,0:T(8,128)S(1)} collective-permute-done((f32[32,1024]{1,0:T(8,128)S(1)}, f32[32,1024]{1,0:T(8,128)S(1)}, u32[]{:S(2)}, u32[]{:S(2)}) %collective-permute-start.14) | collective-permute-done | bytes 131104 | tf_op jit(solution)/shard_map/ppermute | solution.py:379
  114.5 4.7 %collective-permute-done.15 = f32[32,1024]{1,0:T(8,128)S(1)} collective-permute-done((f32[32,1024]{1,0:T(8,128)S(1)}, f32[32,1024]{1,0:T(8,128)S(1)}, u32[]{:S(2)}, u32[]{:S(2)}) %collective-permute-start.15) | collective-permute-done | bytes 131104 | tf_op jit(solution)/shard_map/ppermute | solution.py:379
  124.2 1.3 maximum_select_fusion
  127.6 2.5 %collective-permute-start.12 = (f32[128,256]{1,0:T(8,128)S(1)}, f32[128,256]{1,0:T(8,128)S(1)}, u32[]{:S(2)}, u32[]{:S(2)}) collective-permute-start(f32[128,256]{1,0:T(8,128)S(1)} %get-tuple-element.35), channel_id=1, source_target_pairs={{0,8},{2,10},{4,12},{6,14},{8,0},{10,2},{12,4},{14,6},{1,9},{3,11}... | collective-permute-start | bytes 393224 | tf_op jit(solution)/shard_map/ppermute | solution.py:339
  130.1 1.9 %collective-permute-start.13 = (f32[128,256]{1,0:T(8,128)S(1)}, f32[128,256]{1,0:T(8,128)S(1)}, u32[]{:S(2)}, u32[]{:S(2)}) collective-permute-start(f32[128,256]{1,0:T(8,128)S(1)} %get-tuple-element.34), channel_id=1, source_target_pairs={{0,12},{2,14},{4,0},{6,2},{8,4},{10,6},{12,8},{14,10},{1,13},{3,15... | collective-permute-start | bytes 393224 | tf_op jit(solution)/shard_map/ppermute | solution.py:339
  133.1 6.2 %collective-permute-done.12 = f32[128,256]{1,0:T(8,128)S(1)} collective-permute-done((f32[128,256]{1,0:T(8,128)S(1)}, f32[128,256]{1,0:T(8,128)S(1)}, u32[]{:S(2)}, u32[]{:S(2)}) %collective-permute-start.12) | collective-permute-done | bytes 131104 | tf_op jit(solution)/shard_map/ppermute | solution.py:339
  139.3 3.2 %collective-permute-done.13 = f32[128,256]{1,0:T(8,128)S(1)} collective-permute-done((f32[128,256]{1,0:T(8,128)S(1)}, f32[128,256]{1,0:T(8,128)S(1)}, u32[]{:S(2)}, u32[]{:S(2)}) %collective-permute-start.13) | collective-permute-done | bytes 131104 | tf_op jit(solution)/shard_map/ppermute | solution.py:339
  144.0 7.8 %collective-permute-done.18 = f32[64,2,512]{2,0,1:T(8,128)S(1)} collective-permute-done((f32[64,2,512]{2,0,1:T(8,128)S(1)}, f32[64,2,512]{2,0,1:T(8,128)S(1)}, u32[]{:S(2)}, u32[]{:S(2)}) %collective-permute-start.18) | collective-permute-done | bytes 262176 | tf_op jit(solution)/shard_map/ppermute | solution.py:405
  151.9 1.5 collective-permute-start.19
  153.4 3.5 %collective-permute-done.19 = f32[64,512]{1,0:T(8,128)S(1)} collective-permute-done((f32[64,512]{1,0:T(8,128)S(1)}, f32[64,512]{1,0:T(8,128)S(1)}, u32[]{:S(2)}, u32[]{:S(2)}) %collective-permute-start.19) | collective-permute-done | bytes 131104 | tf_op jit(solution)/shard_map/ppermute | solution.py:408
  (72 shorter events, 15.9 us)
Async XLA Ops:
  31.7 3.7 %copy-start.1 = (f32[384,1024]{1,0:T(8,128)S(1)}, f32[384,1024]{1,0:T(8,128)}, u32[]{:S(2)}) copy-start(f32[384,1024]{1,0:T(8,128)} %get-tuple-element.15) | copy-start | bytes 4718596
  33.1 2.4 %collective-permute-start = (f32[4,48,1024]{2,1,0:T(8,128)S(1)}, f32[4,48,1024]{2,1,0:T(8,128)S(1)}, u32[]{:S(2)}, u32[]{:S(2)}) collective-permute-start(f32[4,48,1024]{2,1,0:T(8,128)S(1)} %dynamic-slice_bitcast_fusion.1), channel_id=1, source_target_pairs={{0,2},{2,0},{4,6},{6,4},{8,10},{10,8},{12,14},{14,12},{1,3},{3,1},... | collective-permute-start | bytes 2359304 | tf_op jit(solution)/shard_map/ppermute | solution.py:334
  35.6 46.0 %collective-permute-start.1 = (f32[48,1024]{1,0:T(8,128)S(1)}, f32[48,1024]{1,0:T(8,128)S(1)}, u32[]{:S(2)}, u32[]{:S(2)}) collective-permute-start(f32[48,1024]{1,0:T(8,128)S(1)} %get-tuple-element.28), channel_id=1, source_target_pairs={{0,4},{2,6},{4,8},{6,10},{8,12},{10,14},{12,0},{14,2},{1,5},{3,7},... | collective-permute-start | bytes 589832 | tf_op jit(solution)/shard_map/ppermute | solution.py:339
  37.3 44.4 %collective-permute-start.2 = (f32[48,1024]{1,0:T(8,128)S(1)}, f32[48,1024]{1,0:T(8,128)S(1)}, u32[]{:S(2)}, u32[]{:S(2)}) collective-permute-start(f32[48,1024]{1,0:T(8,128)S(1)} %get-tuple-element.30), channel_id=1, source_target_pairs={{0,8},{2,10},{4,12},{6,14},{8,0},{10,2},{12,4},{14,6},{1,9},{3,11}... | collective-permute-start | bytes 589832 | tf_op jit(solution)/shard_map/ppermute | solution.py:339
  38.3 43.3 %collective-permute-start.3 = (f32[48,1024]{1,0:T(8,128)S(1)}, f32[48,1024]{1,0:T(8,128)S(1)}, u32[]{:S(2)}, u32[]{:S(2)}) collective-permute-start(f32[48,1024]{1,0:T(8,128)S(1)} %get-tuple-element.29), channel_id=1, source_target_pairs={{0,12},{2,14},{4,0},{6,2},{8,4},{10,6},{12,8},{14,10},{1,13},{3,15... | collective-permute-start | bytes 589832 | tf_op jit(solution)/shard_map/ppermute | solution.py:339
  81.7 3.7 %copy-start.2 = (f32[1536,256]{1,0:T(8,128)S(1)}, f32[1536,256]{1,0:T(8,128)}, u32[]{:S(2)}) copy-start(f32[1536,256]{1,0:T(8,128)} %response.1) | copy-start | bytes 4718596
  83.1 2.4 %collective-permute-start.4 = (f32[4,192,256]{2,1,0:T(8,128)S(1)}, f32[4,192,256]{2,1,0:T(8,128)S(1)}, u32[]{:S(2)}, u32[]{:S(2)}) collective-permute-start(f32[4,192,256]{2,1,0:T(8,128)S(1)} %dynamic-slice_bitcast_fusion), channel_id=1, source_target_pairs={{0,2},{2,0},{4,6},{6,4},{8,10},{10,8},{12,14},{14,12},{1,3},{3,1},... | collective-permute-start | bytes 2359304 | tf_op jit(solution)/shard_map/ppermute | solution.py:334
  85.6 7.1 %collective-permute-start.5 = (f32[48,1024]{1,0:T(8,128)S(1)}, f32[48,1024]{1,0:T(8,128)S(1)}, u32[]{:S(2)}, u32[]{:S(2)}) collective-permute-start(f32[48,1024]{1,0:T(8,128)S(1)} %broadcast_multiply_fusion), channel_id=1, source_target_pairs={{0,1},{1,0},{2,3},{3,2},{4,5},{5,4},{6,7},{7,6},{8,9},{9,8},{10,11... | collective-permute-start | bytes 589832 | tf_op jit(solution)/shard_map/ppermute | solution.py:349
  87.3 7.8 %collective-permute-start.7 = (f32[192,256]{1,0:T(8,128)S(1)}, f32[192,256]{1,0:T(8,128)S(1)}, u32[]{:S(2)}, u32[]{:S(2)}) collective-permute-start(f32[192,256]{1,0:T(8,128)S(1)} %get-tuple-element.25), channel_id=1, source_target_pairs={{0,4},{2,6},{4,8},{6,10},{8,12},{10,14},{12,0},{14,2},{1,5},{3,7},... | collective-permute-start | bytes 589832 | tf_op jit(solution)/shard_map/ppermute | solution.py:339
  87.5 17.0 %collective-permute-start.8 = (f32[192,256]{1,0:T(8,128)S(1)}, f32[192,256]{1,0:T(8,128)S(1)}, u32[]{:S(2)}, u32[]{:S(2)}) collective-permute-start(f32[192,256]{1,0:T(8,128)S(1)} %get-tuple-element.27), channel_id=1, source_target_pairs={{0,8},{2,10},{4,12},{6,14},{8,0},{10,2},{12,4},{14,6},{1,9},{3,11}... | collective-permute-start | bytes 589832 | tf_op jit(solution)/shard_map/ppermute | solution.py:339
  91.0 16.9 %collective-permute-start.9 = (f32[192,256]{1,0:T(8,128)S(1)}, f32[192,256]{1,0:T(8,128)S(1)}, u32[]{:S(2)}, u32[]{:S(2)}) collective-permute-start(f32[192,256]{1,0:T(8,128)S(1)} %get-tuple-element.26), channel_id=1, source_target_pairs={{0,12},{2,14},{4,0},{6,2},{8,4},{10,6},{12,8},{14,10},{1,13},{3,15... | collective-permute-start | bytes 589832 | tf_op jit(solution)/shard_map/ppermute | solution.py:339
  92.7 28.1 %collective-permute-start.6 = (f32[2,48,1024]{2,1,0:T(8,128)S(1)}, f32[2,48,1024]{2,1,0:T(8,128)S(1)}, u32[]{:S(2)}, u32[]{:S(2)}) collective-permute-start(f32[2,48,1024]{2,1,0:T(8,128)S(1)} %reverse_select_fusion.1), channel_id=1, source_target_pairs={{0,16},{16,0},{1,17},{17,1},{2,18},{18,2},{3,19},{19,3},{4,20},{20... | collective-permute-start | bytes 1179656 | tf_op jit(solution)/shard_map/ppermute | solution.py:352
  108.0 6.5 %collective-permute-start.14 = (f32[32,1024]{1,0:T(8,128)S(1)}, f32[32,1024]{1,0:T(8,128)S(1)}, u32[]{:S(2)}, u32[]{:S(2)}) collective-permute-start(f32[32,1024]{1,0:T(8,128)S(1)} %slice.37), channel_id=1, source_target_pairs={{0,4},{2,6},{4,8},{6,10},{8,12},{10,14},{12,0},{14,2},{1,5},{3,7},... | collective-permute-start | bytes 393224 | tf_op jit(solution)/shard_map/ppermute | solution.py:379
  108.1 11.1 %collective-permute-start.15 = (f32[32,1024]{1,0:T(8,128)S(1)}, f32[32,1024]{1,0:T(8,128)S(1)}, u32[]{:S(2)}, u32[]{:S(2)}) collective-permute-start(f32[32,1024]{1,0:T(8,128)S(1)} %slice.37), channel_id=1, source_target_pairs={{0,8},{2,10},{4,12},{6,14},{8,0},{10,2},{12,4},{14,6},{1,9},{3,11}... | collective-permute-start | bytes 393224 | tf_op jit(solution)/shard_map/ppermute | solution.py:379
  108.3 11.4 %collective-permute-start.16 = (f32[32,1024]{1,0:T(8,128)S(1)}, f32[32,1024]{1,0:T(8,128)S(1)}, u32[]{:S(2)}, u32[]{:S(2)}) collective-permute-start(f32[32,1024]{1,0:T(8,128)S(1)} %slice.37), channel_id=1, source_target_pairs={{0,12},{2,14},{4,0},{6,2},{8,4},{10,6},{12,8},{14,10},{1,13},{3,15... | collective-permute-start | bytes 393224 | tf_op jit(solution)/shard_map/ppermute | solution.py:379
  120.8 3.4 %collective-permute-start.17 = (f32[4,32,1024]{2,1,0:T(8,128)}, f32[4,32,1024]{2,1,0:T(8,128)}, u32[]{:S(2)}, u32[]{:S(2)}) collective-permute-start(f32[4,32,1024]{2,1,0:T(8,128)} %get-tuple-element.37), channel_id=1, source_target_pairs={{0,2},{2,0},{4,6},{6,4},{8,10},{10,8},{12,14},{14,12},{1,3},{3,1},... | collective-permute-start | bytes 1572872 | tf_op jit(solution)/shard_map/ppermute | solution.py:381
  121.6 2.4 %copy-start.3 = (s32[1024]{0:T(1024)S(1)}, s32[1024]{0:T(1024)}, u32[]{:S(2)}) copy-start(s32[1024]{0:T(1024)} %param.12) | copy-start | bytes 12292
  121.7 2.6 %copy-start = (f32[4,1,32,1024]{3,2,1,0:T(8,128)S(1)}, f32[4,1,32,1024]{3,2,1,0:T(8,128)}, u32[]{:S(2)}) copy-start(f32[4,1,32,1024]{3,2,1,0:T(8,128)} %get-tuple-element.36) | copy-start | bytes 1572868
  123.6 2.4 %collective-permute-start.10 = (f32[4,128,256]{2,1,0:T(8,128)}, f32[4,128,256]{2,1,0:T(8,128)}, u32[]{:S(2)}, u32[]{:S(2)}) collective-permute-start(f32[4,128,256]{2,1,0:T(8,128)} %dynamic-slice_bitcast_fusion.2), channel_id=1, source_target_pairs={{0,2},{2,0},{4,6},{6,4},{8,10},{10,8},{12,14},{14,12},{1,3},{3,1},... | collective-permute-start | bytes 1572872 | tf_op jit(solution)/shard_map/ppermute | solution.py:334
  127.1 6.0 %collective-permute-start.11 = (f32[128,256]{1,0:T(8,128)S(1)}, f32[128,256]{1,0:T(8,128)S(1)}, u32[]{:S(2)}, u32[]{:S(2)}) collective-permute-start(f32[128,256]{1,0:T(8,128)S(1)} %get-tuple-element.33), channel_id=1, source_target_pairs={{0,4},{2,6},{4,8},{6,10},{8,12},{10,14},{12,0},{14,2},{1,5},{3,7},... | collective-permute-start | bytes 393224 | tf_op jit(solution)/shard_map/ppermute | solution.py:339
  127.6 11.7 %collective-permute-start.12 = (f32[128,256]{1,0:T(8,128)S(1)}, f32[128,256]{1,0:T(8,128)S(1)}, u32[]{:S(2)}, u32[]{:S(2)}) collective-permute-start(f32[128,256]{1,0:T(8,128)S(1)} %get-tuple-element.35), channel_id=1, source_target_pairs={{0,8},{2,10},{4,12},{6,14},{8,0},{10,2},{12,4},{14,6},{1,9},{3,11}... | collective-permute-start | bytes 393224 | tf_op jit(solution)/shard_map/ppermute | solution.py:339
  130.1 12.4 %collective-permute-start.13 = (f32[128,256]{1,0:T(8,128)S(1)}, f32[128,256]{1,0:T(8,128)S(1)}, u32[]{:S(2)}, u32[]{:S(2)}) collective-permute-start(f32[128,256]{1,0:T(8,128)S(1)} %get-tuple-element.34), channel_id=1, source_target_pairs={{0,12},{2,14},{4,0},{6,2},{8,4},{10,6},{12,8},{14,10},{1,13},{3,15... | collective-permute-start | bytes 393224 | tf_op jit(solution)/shard_map/ppermute | solution.py:339
  143.5 8.3 %collective-permute-start.18 = (f32[64,2,512]{2,0,1:T(8,128)S(1)}, f32[64,2,512]{2,0,1:T(8,128)S(1)}, u32[]{:S(2)}, u32[]{:S(2)}) collective-permute-start(f32[64,2,512]{2,0,1:T(8,128)S(1)} %bitcast.105), channel_id=1, source_target_pairs={{0,1},{1,0},{2,3},{3,2},{4,5},{5,4},{6,7},{7,6},{8,9},{9,8},{10,11... | collective-permute-start | bytes 786440 | tf_op jit(solution)/shard_map/ppermute | solution.py:405
  151.9 5.0 %collective-permute-start.19 = (f32[64,512]{1,0:T(8,128)S(1)}, f32[64,512]{1,0:T(8,128)S(1)}, u32[]{:S(2)}, u32[]{:S(2)}) collective-permute-start(f32[64,512]{1,0:T(8,128)S(1)} %dynamic-slice_bitcast_fusion.9), channel_id=1, source_target_pairs={{0,16},{16,0},{1,17},{17,1},{2,18},{18,2},{3,19},{19,3},{4,20},{20... | collective-permute-start | bytes 393224 | tf_op jit(solution)/shard_map/ppermute | solution.py:408
  (1 other events, 2.4 us)

commit v4 on v3

--- a/solution.py
+++ b/solution.py
@@ -180,22 +180,21 @@
     )(block, occ, vir, coulomb.reshape(basis_rows // LANES, LANES), band_vectors)
 
 
-def response_kernel(
-    shape, block_ref, occ_ref, vir_ref, coulomb_ref, turned_ref, out_ref,
-    turned, arrived, products, left_high_even, left_high_odd, left_low_even, left_low_odd,
-    right_high, right_low,
+def gather_kernel(
+    shape, block_ref, occ_ref, vir_ref, coulomb_ref, turned_ref,
+    high_ref, low_ref, own_high_ref, own_low_ref, turned, arrived, products,
 ):
-    left_high, left_low = (left_high_even, left_high_odd), (left_low_even, left_low_odd)
+    step = pl.program_id(0)
     chunks, bands, groups, _ = turned_ref.shape
-    pairs, own = out_ref.shape
+    height = high_ref.shape[0]
+    own = own_high_ref.shape[1]
     lines, blocks, window = shape
-    height = left_high_even.shape[0]
-    slices = pairs // height
     every = chunks * groups
     block = block_ref[0]
-    inside, outside = window // (2 * lines * blocks), (pairs - window) // (2 * lines * blocks)
-    half_slices = slices // 2
-    per_slice = lines // half_slices
+    inside, outside = window // (2 * lines * blocks), occ_ref.shape[0] - window
+    outside = outside // (2 * lines * blocks)
+    half, core = lax.div(step, 4), lax.rem(lax.div(step, 2), 2)
+    first = (lax.rem(step, 2) * lines + core) * blocks + half * (blocks // 2)
 
     def fetch(c):
         here = pl.ds(pl.multiple_of(c * groups, groups), groups)
@@ -206,63 +205,54 @@
             turned[occ_ref[index], here, :] * turned[vir_ref[index], here, :]
         )
 
-    def gather_slice(i, here, stride):
-        first = (lax.rem(i, half_slices) * (per_slice * 2) + lax.div(i, half_slices)) * blocks
+    def gather_slice(here, stride):
         for pair in range(height):
-            share, place = divmod(pair, blocks * (inside + outside))
+            line, place = divmod(pair, blocks // 2 * (inside + outside))
             part, place = divmod(place, inside + outside)
-            index = share * 2 * blocks + part
+            index = line * 2 * blocks + part
             if place < inside:
                 index = first * inside + (index * inside + place)
             else:
                 index = first * outside + (window + index * outside + place - inside)
             gather(index, pair, here, stride)
 
-    def split_slice(parity, base, count, stride):
+    def split_slice(base, count, stride):
         for group in range(count):
             there = pl.ds(base + group * LANES, LANES)
-            left_high[parity][:, there], left_low[parity][:, there] = split(
+            high_ref[:, there], low_ref[:, there] = split(
                 products[pl.ds(group, height, stride=stride), :]
             )
 
-    def multiply(i, parity):
-        here = pl.ds(pl.multiple_of(i * height, height), height)
-        out_ref[here, :] = three_pass(
-            left_high[parity][...], left_low[parity][...], right_high[...], right_low[...]
-        )
-
-    for c in range(chunks):
-        fetch(c).start()
-
-    @pl.loop(0, chunks)
-    def _(c):
-        fetch(c).wait()
-        here = pl.ds(pl.multiple_of(c * groups, groups), groups)
-        base = pl.multiple_of(c * (groups * LANES), LANES)
-        stride = groups + 1 - groups % 2
-        for pair in range(own):
-            share, place = divmod(pair, inside)
-            gather(block * inside + (share * blocks * inside + place), pair, here, stride)
-        for group in range(groups):
-            weight = coulomb_ref[pl.ds(c * groups + group, 1), :]
-            value = products[pl.ds(group, own, stride=stride), :] * weight
-            there = pl.ds(base + group * LANES, LANES)
-            right_high[there, :], right_low[there, :] = split(value.T)
-        gather_slice(0, here, stride)
-        split_slice(0, base, groups, stride)
-
-    stride = every + 1 - every % 2
-
-    @pl.loop(0, slices // 2)
-    def _(index):
-        for parity in range(2):
-            multiply(2 * index + parity, parity)
-            after = jnp.minimum(2 * index + parity + 1, slices - 1)
-            gather_slice(after, pl.ds(0, every), stride)
-            split_slice(1 - parity, 0, every, stride)
-
-
-def pair_response(turned, coulomb, occ, vir, block, shape):
+    @pl.when(step == 0)
+    def _():
+        for c in range(chunks):
+            fetch(c).start()
+
+        @pl.loop(0, chunks)
+        def _(c):
+            fetch(c).wait()
+            here = pl.ds(pl.multiple_of(c * groups, groups), groups)
+            base = pl.multiple_of(c * (groups * LANES), LANES)
+            stride = groups + 1 - groups % 2
+            for pair in range(own):
+                share, place = divmod(pair, inside)
+                gather(block * inside + (share * blocks * inside + place), pair, here, stride)
+            for group in range(groups):
+                weight = coulomb_ref[pl.ds(c * groups + group, 1), :]
+                value = products[pl.ds(group, own, stride=stride), :] * weight
+                there = pl.ds(base + group * LANES, LANES)
+                own_high_ref[there, :], own_low_ref[there, :] = split(value.T)
+            gather_slice(here, stride)
+            split_slice(base, groups, stride)
+
+    @pl.when(step > 0)
+    def _():
+        stride = every + 1 - every % 2
+        gather_slice(pl.ds(0, every), stride)
+        split_slice(0, every, stride)
+
+
+def pair_products(turned, coulomb, occ, vir, block, shape):
     steps, bands, groups, _ = turned.shape
     lines, blocks, window = shape
     pairs = occ.shape[0]
@@ -271,29 +261,57 @@
     basis_rows = every * LANES
     height = pairs // PAIR_SLICES
     places = max(height * (every + 1 - every % 2), own * (groups + 1 - groups % 2))
-    half = jnp.bfloat16
     scalars = pl.BlockSpec(memory_space=pltpu.SMEM)
-    whole = pl.BlockSpec(memory_space=pltpu.VMEM)
+    rows = pl.BlockSpec((height, basis_rows), lambda i: (i, 0))
+    whole = pl.BlockSpec((basis_rows, own), lambda i: (0, 0), pipeline_mode=pl.Buffered(1))
     return pl.pallas_call(
-        functools.partial(response_kernel, shape),
-        in_specs=[scalars] * 3 + [whole, pl.BlockSpec(memory_space=pl.ANY)],
-        out_specs=whole,
-        out_shape=jax.ShapeDtypeStruct((pairs, own), jnp.float32),
+        functools.partial(gather_kernel, shape),
+        grid=(PAIR_SLICES,),
+        in_specs=[scalars] * 3
+        + [pl.BlockSpec((every, LANES), lambda i: (0, 0)), pl.BlockSpec(memory_space=pl.ANY)],
+        out_specs=[rows, rows, whole, whole],
+        out_shape=[jax.ShapeDtypeStruct((pairs, basis_rows), jnp.bfloat16)] * 2
+        + [jax.ShapeDtypeStruct((basis_rows, own), jnp.bfloat16)] * 2,
         scratch_shapes=[
             pltpu.VMEM((bands, every, LANES), jnp.float32),
             pltpu.SemaphoreType.DMA((steps,)),
             pltpu.VMEM((places, LANES), jnp.float32),
-        ]
-        + [pltpu.VMEM((height, basis_rows), half)] * 4
-        + [pltpu.VMEM((basis_rows, own), half)] * 2,
+        ],
         compiler_params=pltpu.CompilerParams(vmem_limit_bytes=VMEM_BYTES),
         cost_estimate=pl.CostEstimate(
-            flops=6 * basis_rows * pairs * own,
-            bytes_accessed=4 * basis_rows * bands,
+            flops=0,
+            bytes_accessed=4 * basis_rows * (bands + pairs + own),
             transcendentals=0,
         ),
-        name="response",
-    )(block, occ, vir, coulomb.reshape(basis_rows // LANES, LANES), turned)
+        name="products",
+    )(block, occ, vir, coulomb.reshape(every, LANES), turned)
+
+
+def response_kernel(high_ref, low_ref, own_high_ref, own_low_ref, out_ref):
+    out_ref[...] = three_pass(high_ref[...], low_ref[...], own_high_ref[...], own_low_ref[...])
+
+
+def pair_response(high, low, own_high, own_low, half):
+    pairs, basis_rows = high.shape
+    own = own_high.shape[1]
+    height = pairs // PAIR_SLICES
+    steps = PAIR_SLICES // 2
+    rows = pl.BlockSpec((height, basis_rows), lambda i: (i + half * steps, 0))
+    whole = pl.BlockSpec((basis_rows, own), lambda i: (0, 0), pipeline_mode=pl.Buffered(1))
+    return pl.pallas_call(
+        response_kernel,
+        grid=(steps,),
+        in_specs=[rows, rows, whole, whole],
+        out_specs=pl.BlockSpec((height, own), lambda i: (i, 0)),
+        out_shape=jax.ShapeDtypeStruct((pairs // 2, own), jnp.float32),
+        compiler_params=pltpu.CompilerParams(vmem_limit_bytes=VMEM_BYTES),
+        cost_estimate=pl.CostEstimate(
+            flops=3 * basis_rows * pairs * own,
+            bytes_accessed=2 * basis_rows * (pairs + 2 * own),
+            transcendentals=0,
+        ),
+        name=f"response_{half}",
+    )(high, low, own_high, own_low)
 
 
 def per_device(band_vectors, coulomb, pair_weight, occ_index, vir_index, freq_index, freq_table):
@@ -362,27 +380,39 @@
     share = pairs // row_count
     partial_coupling = add_cores(partial_coupling.reshape(2, lines, share // blocks, bands))
     partial_coupling, turned = lax.optimization_barrier((partial_coupling, turned))
-    partial_response = pair_response(turned, coulomb, occ_index, vir_index, place, shape)
+    high, low, own_high, own_low = pair_products(
+        turned, coulomb, occ_index, vir_index, place, shape
+    )
     coupling = scatter_lines(partial_coupling)
-    partial_response, coupling = lax.optimization_barrier((partial_response, coupling))
-    partial_response = add_cores(partial_response.reshape(2, lines, share, window // blocks))
-    partial_response, coupling = lax.optimization_barrier((partial_response, coupling))
+    high, low, coupling = lax.optimization_barrier((high, low, coupling))
+
     own_weights = pick(pick(weights, core), line)
     coupling = coupling * (pick(own_weights, block)[:, None] * (1.0 / math.sqrt(basis)))
     all_coupling = gather_blocks(coupling).reshape(share, bands)
-    response = scatter_lines(partial_response)
-    response = response * (
+    sub = window // (row_count * blocks)
+    part = coupling[:sub]
+    parts = [part] + [lax.ppermute(part, "rows", shift(step)) for step in range(1, lines)]
+
+    def sum_cores(values):
+        return add_cores(values.reshape(2, lines, share // 2, window // blocks))
+
+    first = pair_response(high, low, own_high, own_low, 0)
+    first, all_coupling, *parts = lax.optimization_barrier((first, all_coupling, *parts))
+    first = sum_cores(first)
+    first, high = lax.optimization_barrier((first, high))
+    second = pair_response(high, low, own_high, own_low, 1)
+    first = scatter_lines(first)
+    second, first = lax.optimization_barrier((second, first))
+    second = scatter_lines(sum_cores(second))
+    response = jnp.concatenate([first, second]) * (
         own_weights.reshape(-1)[:, None] * own_window(pair_weight)[None, :] * (1.0 / basis)
     )
-    sub = window // (row_count * blocks)
-    response, part = lax.optimization_barrier((response, coupling[:sub]))
-    parts = [part] + [lax.ppermute(part, "rows", shift(step)) for step in range(1, lines)]
+
     parts = jnp.stack(parts)
     beside = lax.ppermute(parts, "rows", other_core)
     both = jnp.where(core == 0, jnp.stack([parts, beside], 1), jnp.stack([beside, parts], 1))
     both = jnp.roll(both[::-1], line + 1, axis=0)
     window_coupling = both.reshape(row_count * sub, bands)
-
     matches = freq_index[:, None] == jnp.arange(freq_table.shape[0], dtype=jnp.int32)[None, :]
     band_weight = jnp.sum(jnp.where(matches, freq_table[None, :], 0.0), axis=1)
     mixed = lax.dot_general(
@@ -401,12 +431,23 @@
         own_band_weight[:, None] * band_weight[None, :] * (1.0 / math.sqrt(window))
     )
     energy = energy.reshape(col_count, here // col_count, group_count, bands // group_count)
-    across = [(i, i ^ 1) for i in range(col_count)]
-    received = lax.ppermute(pick(energy, 1 - column), "cols", across)
-    energy = pick(energy, column) + received
-    across = [(i, i ^ 1) for i in range(group_count)]
-    received = lax.ppermute(pick(energy, 1 - group, 1), "grp", across)
-    return pick(energy, group, 1) + received
+    total = pick(pick(energy, column), group, 1)
+    for step in range(1, blocks):
+        there_group, there_column = divmod(step, col_count)
+        away_group = lax.rem(group + there_group, group_count)
+        away_column = lax.rem(column + there_column, col_count)
+        targets = [
+            (
+                i,
+                (i // col_count + there_group) % group_count * col_count
+                + (i % col_count + there_column) % col_count,
+            )
+            for i in range(blocks)
+        ]
+        total = total + lax.ppermute(
+            pick(pick(energy, away_column), away_group, 1), ("grp", "cols"), targets
+        )
+    return total
 
 
 def solution(mesh):

time: 158 us -> 162 us (1.025)
  waiting for transfers between devices: 48.9 us -> 30.4 us
  Pallas kernels: 73.1 us -> 88.3 us
  starting transfers between devices: 21.4 us -> 27.1 us
  other arithmetic: 5.55 us -> 7.72 us
    pallas_call x1 -> x3, Pallas kernels: 41.4 us -> 56.6 us  [the longest x1 29.6 us: pair_products(): pl.pallas_call(functools.partial(gather_kernel, shape), grid=(PAIR_SLICES...]
    ppermute x3, waiting for transfers between devices: 9.55 us -> 0.01 us  [per_device(): lax.ppermute(part, 'rows', shift(step))]
    ppermute x9 -> x12, waiting for transfers between devices: 23.8 us -> 18.3 us  [scatter_lines(): lax.ppermute(pick(values, lax.rem(line + step, lines)), 'rows', shift(step))]
    ppermute x2 -> x3, waiting for transfers between devices: 11.3 us -> 5.85 us  [per_device(): lax.ppermute(pick(pick(energy, away_column), away_group, 1), ('grp', 'col...]
    ppermute x9 -> x12, starting transfers between devices: 13.4 us -> 16.3 us  [scatter_lines(): lax.ppermute(pick(values, lax.rem(line + step, lines)), 'rows', shift(step))]
    ppermute x3 -> x4, waiting for transfers between devices: 2.76 us -> 5.54 us  [add_cores(): received = lax.ppermute(pick(values, 1 - core), 'rows', other_core)]
    add x3 -> x4, other arithmetic: 1.33 us -> 3.43 us  [add_cores(): return pick(values, core) + received]
    ppermute x3, starting transfers between devices: 2.07 us -> 3.76 us  [per_device(): lax.ppermute(part, 'rows', shift(step))]
  transfers between devices with their start and end apart: 20 -> 25, of which waited for: 15 -> 14; matrix products, arithmetic and copies ran while one was open for 5% -> 4% of each run, Pallas kernels for 26% -> 35%
where the time goes in v4:
time: 162 us; the launch traced here: 161 us
  Pallas kernels  88.3 us (55%)
  waiting for transfers between devices  30.4 us (19%)
  starting transfers between devices  27.1 us (17%)
  other arithmetic  7.72 us (5%)
  local copies, waits for them, and re-layouts  5.73 us (4%)
    pallas_call x1, Pallas kernels, pair_coupling(): pl.pallas_call(functools.partial(coupling_kernel, shape), in_specs=[scala...  31.7 us
    pallas_call x1, Pallas kernels, pair_products(): pl.pallas_call(functools.partial(gather_kernel, shape), grid=(PAIR_SLICES...  29.6 us
    pallas_call x2, Pallas kernels, pair_response(): pl.pallas_call(response_kernel, grid=(steps,), in_specs=[rows, rows, whol...  27 us
    ppermute x12, waiting for transfers between devices, scatter_lines(): lax.ppermute(pick(values, lax.rem(line + step, lines)), 'rows', shift(step))  18.3 us
    ppermute x12, starting transfers between devices, scatter_lines(): lax.ppermute(pick(values, lax.rem(line + step, lines)), 'rows', shift(step))  16.3 us
    ppermute x3, waiting for transfers between devices, per_device(): lax.ppermute(pick(pick(energy, away_column), away_group, 1), ('grp', 'col...  5.85 us
    ppermute x4, waiting for transfers between devices, add_cores(): received = lax.ppermute(pick(values, 1 - core), 'rows', other_core)  5.54 us
    ppermute x3, starting transfers between devices, per_device(): lax.ppermute(part, 'rows', shift(step))  3.76 us
  transfers between devices with their start and end apart: 25, of which 14 were waited for; matrix products, arithmetic and copies ran while one was open for 4% of the time, Pallas kernels for 35%

profile of v4, /device:TPU:8, one launch (start us, length us, event | category | flops | bytes accessed | tf_op | source)
XLA Modules:
  0.0 161.2 jit_solution(17924600588877827093)
XLA Ops:
  0.0 31.7 %coupling.1 = (f32[384,1024]{1,0:T(8,128)}, f32[6,1024,8,128]{3,2,1,0:T(8,128)}) custom-call(s32[1]{0:T(128)} %bitcast.block_ref, s32[1536]{0:T(1024)} %occ_ref.3, s32[1536]{0:T(1024)} %vir_ref.3, f32[48,128]{1,0:T(8,128)} %bitcast.132, f32[6144,1024]{1,0:T(8,128)} %band_ref.1), custom_call_target="tpu_custom_call" | custom-call | flops 14495514624 | bytes 50331648 | tf_op jit(solution)/shard_map/coupling/pallas_call | solution.py:155
  33.1 2.2 %collective-permute-done = f32[4,48,1024]{2,1,0:T(8,128)S(1)} collective-permute-done((f32[4,48,1024]{2,1,0:T(8,128)S(1)}, f32[4,48,1024]{2,1,0:T(8,128)S(1)}, u32[]{:S(2)}, u32[]{:S(2)}) %collective-permute-start) | collective-permute-done | bytes 786464 | tf_op jit(solution)/shard_map/ppermute | solution.py:352
  36.6 1.6 %collective-permute-start.1 = (f32[48,1024]{1,0:T(8,128)S(1)}, f32[48,1024]{1,0:T(8,128)S(1)}, u32[]{:S(2)}, u32[]{:S(2)}) collective-permute-start(f32[48,1024]{1,0:T(8,128)S(1)} %get-tuple-element.47), channel_id=1, source_target_pairs={{0,4},{2,6},{4,8},{6,10},{8,12},{10,14},{12,0},{14,2},{1,5},{3,7},... | collective-permute-start | bytes 589832 | tf_op jit(solution)/shard_map/ppermute | solution.py:357
  39.3 1.9 %collective-permute-start.3 = (f32[48,1024]{1,0:T(8,128)S(1)}, f32[48,1024]{1,0:T(8,128)S(1)}, u32[]{:S(2)}, u32[]{:S(2)}) collective-permute-start(f32[48,1024]{1,0:T(8,128)S(1)} %get-tuple-element.48), channel_id=1, source_target_pairs={{0,12},{2,14},{4,0},{6,2},{8,4},{10,6},{12,8},{14,10},{1,13},{3,15... | collective-permute-start | bytes 589832 | tf_op jit(solution)/shard_map/ppermute | solution.py:357
  41.5 29.6 %products.1 = (bf16[1536,6144]{1,0:T(8,128)(2,1)}, bf16[1536,6144]{1,0:T(8,128)(2,1)}, bf16[6144,256]{1,0:T(8,128)(2,1)}, bf16[6144,256]{1,0:T(8,128)(2,1)}) custom-call(s32[1]{0:T(128)} %bitcast.block_ref, s32[1536]{0:T(1024)} %occ_ref.3, s32[1536]{0:T(1024)} %vir_ref.3, f32[48,128]{1,0:T(8,128)} %bitcast.133, f32[6,1024,8,128]{3,2,1,0:T(8,128)} %get-tuple-element.28.turned_ref), custom_call_target="tpu_custom_call" | custom-call | bytes 69206016 | tf_op jit(solution)/shard_map/products/pallas_call | solution.py:267
  71.3 1.6 collective-permute-start.4
  73.2 3.5 %collective-permute-start.7 = (f32[32,1024]{1,0:T(8,128)S(1)}, f32[32,1024]{1,0:T(8,128)S(1)}, u32[]{:S(2)}, u32[]{:S(2)}) collective-permute-start(f32[32,1024]{1,0:T(8,128)S(1)} %slice.37), channel_id=1, source_target_pairs={{0,8},{2,10},{4,12},{6,14},{8,0},{10,2},{12,4},{14,6},{1,9},{3,11}... | collective-permute-start | bytes 393224 | tf_op jit(solution)/shard_map/ppermute | solution.py:394
  79.1 13.5 %response_0.1 = f32[768,256]{1,0:T(8,128)} custom-call(bf16[1536,6144]{1,0:T(8,128)(2,1)} %get-tuple-element.39.high_ref, bf16[1536,6144]{1,0:T(8,128)(2,1)} %get-tuple-element.33.low_ref, bf16[6144,256]{1,0:T(8,128)(2,1)} %get-tuple-element.34.own_high_ref, bf16[6144,256]{1,0:T(8,128)(2,1)} %get-tuple-element.35.own_low_ref), custom_call_target="tpu_custom_call" | custom-call | flops 7247757312 | bytes 25165824 | tf_op jit(solution)/shard_map/response_0/pallas_call | solution.py:301
  93.9 1.7 %collective-permute-done.9 = f32[4,96,256]{2,1,0:T(8,128)S(1)} collective-permute-done((f32[4,96,256]{2,1,0:T(8,128)S(1)}, f32[4,96,256]{2,1,0:T(8,128)S(1)}, u32[]{:S(2)}, u32[]{:S(2)}) %collective-permute-start.9) | collective-permute-done | bytes 393248 | tf_op jit(solution)/shard_map/ppermute | solution.py:352
  97.0 2.5 %collective-permute-start.11 = (f32[96,256]{1,0:T(8,128)S(1)}, f32[96,256]{1,0:T(8,128)S(1)}, u32[]{:S(2)}, u32[]{:S(2)}) collective-permute-start(f32[96,256]{1,0:T(8,128)S(1)} %get-tuple-element.64), channel_id=1, source_target_pairs={{0,8},{2,10},{4,12},{6,14},{8,0},{10,2},{12,4},{14,6},{1,9},{3,11}... | collective-permute-start | bytes 294920 | tf_op jit(solution)/shard_map/ppermute | solution.py:357
  99.4 13.5 %response_1.1 = f32[768,256]{1,0:T(8,128)} custom-call(bf16[1536,6144]{1,0:T(8,128)(2,1)} %get-tuple-element.39.high_ref, bf16[1536,6144]{1,0:T(8,128)(2,1)} %get-tuple-element.33.low_ref, bf16[6144,256]{1,0:T(8,128)(2,1)} %get-tuple-element.34.own_high_ref, bf16[6144,256]{1,0:T(8,128)(2,1)} %get-tuple-element.35.own_low_ref), custom_call_target="tpu_custom_call" | custom-call | flops 7247757312 | bytes 25165824 | tf_op jit(solution)/shard_map/response_1/pallas_call | solution.py:301
  116.9 2.1 %collective-permute-start.14 = (f32[96,256]{1,0:T(8,128)S(1)}, f32[96,256]{1,0:T(8,128)S(1)}, u32[]{:S(2)}, u32[]{:S(2)}) collective-permute-start(f32[96,256]{1,0:T(8,128)S(1)} %get-tuple-element.59), channel_id=1, source_target_pairs={{0,4},{2,6},{4,8},{6,10},{8,12},{10,14},{12,0},{14,2},{1,5},{3,7},... | collective-permute-start | bytes 294920 | tf_op jit(solution)/shard_map/ppermute | solution.py:357
  119.0 2.2 %collective-permute-start.15 = (f32[96,256]{1,0:T(8,128)S(1)}, f32[96,256]{1,0:T(8,128)S(1)}, u32[]{:S(2)}, u32[]{:S(2)}) collective-permute-start(f32[96,256]{1,0:T(8,128)S(1)} %get-tuple-element.61), channel_id=1, source_target_pairs={{0,8},{2,10},{4,12},{6,14},{8,0},{10,2},{12,4},{14,6},{1,9},{3,11}... | collective-permute-start | bytes 294920 | tf_op jit(solution)/shard_map/ppermute | solution.py:357
  122.1 4.0 %collective-permute-done.14 = f32[96,256]{1,0:T(8,128)S(1)} collective-permute-done((f32[96,256]{1,0:T(8,128)S(1)}, f32[96,256]{1,0:T(8,128)S(1)}, u32[]{:S(2)}, u32[]{:S(2)}) %collective-permute-start.14) | collective-permute-done | bytes 98336 | tf_op jit(solution)/shard_map/ppermute | solution.py:357
  127.7 1.9 %collective-permute-done.16 = f32[96,256]{1,0:T(8,128)S(1)} collective-permute-done((f32[96,256]{1,0:T(8,128)S(1)}, f32[96,256]{1,0:T(8,128)S(1)}, u32[]{:S(2)}, u32[]{:S(2)}) %collective-permute-start.16) | collective-permute-done | bytes 98336 | tf_op jit(solution)/shard_map/ppermute | solution.py:357
  131.7 1.7 %maximum_select_fusion = f32[4,2,32,1024]{3,2,1,0:T(8,128)S(1)} fusion(f32[4,1,32,1024]{3,2,1,0:T(8,128)} %bitcast.43, f32[4,1,32,1024]{3,2,1,0:T(8,128)} %get-tuple-element.57, pred[]{:T(512)S(6)} %eq.27), kind=kLoop, calls=%fused_computation.5 | loop fusion | flops 786432 | bytes 2097153 | tf_op jit(solution)/shard_map/jit(_where)/select_n | solution.py:413
  135.0 2.5 %collective-permute-start.19 = (f32[128,256]{1,0:T(8,128)S(1)}, f32[128,256]{1,0:T(8,128)S(1)}, u32[]{:S(2)}, u32[]{:S(2)}) collective-permute-start(f32[128,256]{1,0:T(8,128)S(1)} %get-tuple-element.56), channel_id=1, source_target_pairs={{0,8},{2,10},{4,12},{6,14},{8,0},{10,2},{12,4},{14,6},{1,9},{3,11}... | collective-permute-start | bytes 393224 | tf_op jit(solution)/shard_map/ppermute | solution.py:357
  138.7 2.6 %collective-permute-done.18 = f32[128,256]{1,0:T(8,128)S(1)} collective-permute-done((f32[128,256]{1,0:T(8,128)S(1)}, f32[128,256]{1,0:T(8,128)S(1)}, u32[]{:S(2)}, u32[]{:S(2)}) %collective-permute-start.18) | collective-permute-done | bytes 131104 | tf_op jit(solution)/shard_map/ppermute | solution.py:357
  141.3 5.6 %collective-permute-done.19 = f32[128,256]{1,0:T(8,128)S(1)} collective-permute-done((f32[128,256]{1,0:T(8,128)S(1)}, f32[128,256]{1,0:T(8,128)S(1)}, u32[]{:S(2)}, u32[]{:S(2)}) %collective-permute-start.19) | collective-permute-done | bytes 131104 | tf_op jit(solution)/shard_map/ppermute | solution.py:357
  146.9 2.7 %collective-permute-done.20 = f32[128,256]{1,0:T(8,128)S(1)} collective-permute-done((f32[128,256]{1,0:T(8,128)S(1)}, f32[128,256]{1,0:T(8,128)S(1)}, u32[]{:S(2)}, u32[]{:S(2)}) %collective-permute-start.20) | collective-permute-done | bytes 131104 | tf_op jit(solution)/shard_map/ppermute | solution.py:357
  152.8 1.9 %collective-permute-start.24 = (f32[64,512]{1,0:T(8,128)S(1)}, f32[64,512]{1,0:T(8,128)S(1)}, u32[]{:S(2)}, u32[]{:S(2)}) collective-permute-start(f32[64,512]{1,0:T(8,128)S(1)} %bitcast.131), channel_id=1, source_target_pairs={{0,17},{1,16},{16,1},{17,0},{2,19},{3,18},{18,3},{19,2},{4,21},{5,... | collective-permute-start | bytes 393224 | tf_op jit(solution)/shard_map/ppermute | solution.py:447
  154.7 1.8 %collective-permute-done.22 = f32[64,512]{1,0:T(8,128)S(1)} collective-permute-done((f32[64,512]{1,0:T(8,128)S(1)}, f32[64,512]{1,0:T(8,128)S(1)}, u32[]{:S(2)}, u32[]{:S(2)}) %collective-permute-start.22) | collective-permute-done | bytes 131104 | tf_op jit(solution)/shard_map/ppermute | solution.py:447
  156.5 2.1 %collective-permute-done.23 = f32[64,512]{1,0:T(8,128)S(1)} collective-permute-done((f32[64,512]{1,0:T(8,128)S(1)}, f32[64,512]{1,0:T(8,128)S(1)}, u32[]{:S(2)}, u32[]{:S(2)}) %collective-permute-start.23) | collective-permute-done | bytes 131104 | tf_op jit(solution)/shard_map/ppermute | solution.py:447
  158.6 1.9 %collective-permute-done.24 = f32[64,512]{1,0:T(8,128)S(1)} collective-permute-done((f32[64,512]{1,0:T(8,128)S(1)}, f32[64,512]{1,0:T(8,128)S(1)}, u32[]{:S(2)}, u32[]{:S(2)}) %collective-permute-start.24) | collective-permute-done | bytes 131104 | tf_op jit(solution)/shard_map/ppermute | solution.py:447
  (86 shorter events, 24.4 us)
Async XLA Ops:
  33.0 2.4 %collective-permute-start = (f32[4,48,1024]{2,1,0:T(8,128)S(1)}, f32[4,48,1024]{2,1,0:T(8,128)S(1)}, u32[]{:S(2)}, u32[]{:S(2)}) collective-permute-start(f32[4,48,1024]{2,1,0:T(8,128)S(1)} %dynamic-slice_bitcast_fusion), channel_id=1, source_target_pairs={{0,2},{2,0},{4,6},{6,4},{8,10},{10,8},{12,14},{14,12},{1,3},{3,1},... | collective-permute-start | bytes 2359304 | tf_op jit(solution)/shard_map/ppermute | solution.py:352
  36.6 34.5 %collective-permute-start.1 = (f32[48,1024]{1,0:T(8,128)S(1)}, f32[48,1024]{1,0:T(8,128)S(1)}, u32[]{:S(2)}, u32[]{:S(2)}) collective-permute-start(f32[48,1024]{1,0:T(8,128)S(1)} %get-tuple-element.47), channel_id=1, source_target_pairs={{0,4},{2,6},{4,8},{6,10},{8,12},{10,14},{12,0},{14,2},{1,5},{3,7},... | collective-permute-start | bytes 589832 | tf_op jit(solution)/shard_map/ppermute | solution.py:357
  38.2 32.9 %collective-permute-start.2 = (f32[48,1024]{1,0:T(8,128)S(1)}, f32[48,1024]{1,0:T(8,128)S(1)}, u32[]{:S(2)}, u32[]{:S(2)}) collective-permute-start(f32[48,1024]{1,0:T(8,128)S(1)} %get-tuple-element.49), channel_id=1, source_target_pairs={{0,8},{2,10},{4,12},{6,14},{8,0},{10,2},{12,4},{14,6},{1,9},{3,11}... | collective-permute-start | bytes 589832 | tf_op jit(solution)/shard_map/ppermute | solution.py:357
  39.3 31.9 %collective-permute-start.3 = (f32[48,1024]{1,0:T(8,128)S(1)}, f32[48,1024]{1,0:T(8,128)S(1)}, u32[]{:S(2)}, u32[]{:S(2)}) collective-permute-start(f32[48,1024]{1,0:T(8,128)S(1)} %get-tuple-element.48), channel_id=1, source_target_pairs={{0,12},{2,14},{4,0},{6,2},{8,4},{10,6},{12,8},{14,10},{1,13},{3,15... | collective-permute-start | bytes 589832 | tf_op jit(solution)/shard_map/ppermute | solution.py:357
  71.3 6.2 %collective-permute-start.4 = (f32[48,1024]{1,0:T(8,128)S(1)}, f32[48,1024]{1,0:T(8,128)S(1)}, u32[]{:S(2)}, u32[]{:S(2)}) collective-permute-start(f32[48,1024]{1,0:T(8,128)S(1)} %broadcast_multiply_fusion), channel_id=1, source_target_pairs={{0,1},{1,0},{2,3},{3,2},{4,5},{5,4},{6,7},{7,6},{8,9},{9,8},{10,11... | collective-permute-start | bytes 589832 | tf_op jit(solution)/shard_map/ppermute | solution.py:367
  72.9 19.9 %collective-permute-start.6 = (f32[32,1024]{1,0:T(8,128)S(1)}, f32[32,1024]{1,0:T(8,128)S(1)}, u32[]{:S(2)}, u32[]{:S(2)}) collective-permute-start(f32[32,1024]{1,0:T(8,128)S(1)} %slice.37), channel_id=1, source_target_pairs={{0,4},{2,6},{4,8},{6,10},{8,12},{10,14},{12,0},{14,2},{1,5},{3,7},... | collective-permute-start | bytes 393224 | tf_op jit(solution)/shard_map/ppermute | solution.py:394
  73.2 19.6 %collective-permute-start.7 = (f32[32,1024]{1,0:T(8,128)S(1)}, f32[32,1024]{1,0:T(8,128)S(1)}, u32[]{:S(2)}, u32[]{:S(2)}) collective-permute-start(f32[32,1024]{1,0:T(8,128)S(1)} %slice.37), channel_id=1, source_target_pairs={{0,8},{2,10},{4,12},{6,14},{8,0},{10,2},{12,4},{14,6},{1,9},{3,11}... | collective-permute-start | bytes 393224 | tf_op jit(solution)/shard_map/ppermute | solution.py:394
  76.7 16.2 %collective-permute-start.8 = (f32[32,1024]{1,0:T(8,128)S(1)}, f32[32,1024]{1,0:T(8,128)S(1)}, u32[]{:S(2)}, u32[]{:S(2)}) collective-permute-start(f32[32,1024]{1,0:T(8,128)S(1)} %slice.37), channel_id=1, source_target_pairs={{0,12},{2,14},{4,0},{6,2},{8,4},{10,6},{12,8},{14,10},{1,13},{3,15... | collective-permute-start | bytes 393224 | tf_op jit(solution)/shard_map/ppermute | solution.py:394
  77.6 15.1 %collective-permute-start.5 = (f32[2,48,1024]{2,1,0:T(8,128)S(1)}, f32[2,48,1024]{2,1,0:T(8,128)S(1)}, u32[]{:S(2)}, u32[]{:S(2)}) collective-permute-start(f32[2,48,1024]{2,1,0:T(8,128)S(1)} %reverse_select_fusion.1), channel_id=1, source_target_pairs={{0,16},{16,0},{1,17},{17,1},{2,18},{18,2},{3,19},{19,3},{4,20},{20... | collective-permute-start | bytes 1179656 | tf_op jit(solution)/shard_map/ppermute | solution.py:370
  95.7 17.3 %collective-permute-start.10 = (f32[96,256]{1,0:T(8,128)S(1)}, f32[96,256]{1,0:T(8,128)S(1)}, u32[]{:S(2)}, u32[]{:S(2)}) collective-permute-start(f32[96,256]{1,0:T(8,128)S(1)} %get-tuple-element.62), channel_id=1, source_target_pairs={{0,4},{2,6},{4,8},{6,10},{8,12},{10,14},{12,0},{14,2},{1,5},{3,7},... | collective-permute-start | bytes 294920 | tf_op jit(solution)/shard_map/ppermute | solution.py:357
  97.0 16.0 %collective-permute-start.11 = (f32[96,256]{1,0:T(8,128)S(1)}, f32[96,256]{1,0:T(8,128)S(1)}, u32[]{:S(2)}, u32[]{:S(2)}) collective-permute-start(f32[96,256]{1,0:T(8,128)S(1)} %get-tuple-element.64), channel_id=1, source_target_pairs={{0,8},{2,10},{4,12},{6,14},{8,0},{10,2},{12,4},{14,6},{1,9},{3,11}... | collective-permute-start | bytes 294920 | tf_op jit(solution)/shard_map/ppermute | solution.py:357
  99.4 13.5 %collective-permute-start.12 = (f32[96,256]{1,0:T(8,128)S(1)}, f32[96,256]{1,0:T(8,128)S(1)}, u32[]{:S(2)}, u32[]{:S(2)}) collective-permute-start(f32[96,256]{1,0:T(8,128)S(1)} %get-tuple-element.63), channel_id=1, source_target_pairs={{0,12},{2,14},{4,0},{6,2},{8,4},{10,6},{12,8},{14,10},{1,13},{3,15... | collective-permute-start | bytes 294920 | tf_op jit(solution)/shard_map/ppermute | solution.py:357
  114.0 1.8 %collective-permute-start.13 = (f32[4,96,256]{2,1,0:T(8,128)S(1)}, f32[4,96,256]{2,1,0:T(8,128)S(1)}, u32[]{:S(2)}, u32[]{:S(2)}) collective-permute-start(f32[4,96,256]{2,1,0:T(8,128)S(1)} %dynamic-slice_bitcast_fusion.2), channel_id=1, source_target_pairs={{0,2},{2,0},{4,6},{6,4},{8,10},{10,8},{12,14},{14,12},{1,3},{3,1},... | collective-permute-start | bytes 1179656 | tf_op jit(solution)/shard_map/ppermute | solution.py:352
  116.9 9.2 %collective-permute-start.14 = (f32[96,256]{1,0:T(8,128)S(1)}, f32[96,256]{1,0:T(8,128)S(1)}, u32[]{:S(2)}, u32[]{:S(2)}) collective-permute-start(f32[96,256]{1,0:T(8,128)S(1)} %get-tuple-element.59), channel_id=1, source_target_pairs={{0,4},{2,6},{4,8},{6,10},{8,12},{10,14},{12,0},{14,2},{1,5},{3,7},... | collective-permute-start | bytes 294920 | tf_op jit(solution)/shard_map/ppermute | solution.py:357
  119.0 8.7 %collective-permute-start.15 = (f32[96,256]{1,0:T(8,128)S(1)}, f32[96,256]{1,0:T(8,128)S(1)}, u32[]{:S(2)}, u32[]{:S(2)}) collective-permute-start(f32[96,256]{1,0:T(8,128)S(1)} %get-tuple-element.61), channel_id=1, source_target_pairs={{0,8},{2,10},{4,12},{6,14},{8,0},{10,2},{12,4},{14,6},{1,9},{3,11}... | collective-permute-start | bytes 294920 | tf_op jit(solution)/shard_map/ppermute | solution.py:357
  121.2 8.3 %collective-permute-start.16 = (f32[96,256]{1,0:T(8,128)S(1)}, f32[96,256]{1,0:T(8,128)S(1)}, u32[]{:S(2)}, u32[]{:S(2)}) collective-permute-start(f32[96,256]{1,0:T(8,128)S(1)} %get-tuple-element.60), channel_id=1, source_target_pairs={{0,12},{2,14},{4,0},{6,2},{8,4},{10,6},{12,8},{14,10},{1,13},{3,15... | collective-permute-start | bytes 294920 | tf_op jit(solution)/shard_map/ppermute | solution.py:357
  122.1 9.5 %collective-permute-start.21 = (f32[4,32,1024]{2,1,0:T(8,128)S(1)}, f32[4,32,1024]{2,1,0:T(8,128)}, u32[]{:S(2)}, u32[]{:S(2)}) collective-permute-start(f32[4,32,1024]{2,1,0:T(8,128)S(1)} %get-tuple-element.58), channel_id=1, source_target_pairs={{0,2},{2,0},{4,6},{6,4},{8,10},{10,8},{12,14},{14,12},{1,3},{3,1},... | collective-permute-start | bytes 1572872 | tf_op jit(solution)/shard_map/ppermute | solution.py:412
  131.5 2.3 %collective-permute-start.17 = (f32[4,128,256]{2,1,0:T(8,128)}, f32[4,128,256]{2,1,0:T(8,128)}, u32[]{:S(2)}, u32[]{:S(2)}) collective-permute-start(f32[4,128,256]{2,1,0:T(8,128)} %dynamic-slice_bitcast_fusion.1), channel_id=1, source_target_pairs={{0,2},{2,0},{4,6},{6,4},{8,10},{10,8},{12,14},{14,12},{1,3},{3,1},... | collective-permute-start | bytes 1572872 | tf_op jit(solution)/shard_map/ppermute | solution.py:352
  134.9 6.4 %collective-permute-start.18 = (f32[128,256]{1,0:T(8,128)S(1)}, f32[128,256]{1,0:T(8,128)S(1)}, u32[]{:S(2)}, u32[]{:S(2)}) collective-permute-start(f32[128,256]{1,0:T(8,128)S(1)} %get-tuple-element.54), channel_id=1, source_target_pairs={{0,4},{2,6},{4,8},{6,10},{8,12},{10,14},{12,0},{14,2},{1,5},{3,7},... | collective-permute-start | bytes 393224 | tf_op jit(solution)/shard_map/ppermute | solution.py:357
  135.0 11.9 %collective-permute-start.19 = (f32[128,256]{1,0:T(8,128)S(1)}, f32[128,256]{1,0:T(8,128)S(1)}, u32[]{:S(2)}, u32[]{:S(2)}) collective-permute-start(f32[128,256]{1,0:T(8,128)S(1)} %get-tuple-element.56), channel_id=1, source_target_pairs={{0,8},{2,10},{4,12},{6,14},{8,0},{10,2},{12,4},{14,6},{1,9},{3,11}... | collective-permute-start | bytes 393224 | tf_op jit(solution)/shard_map/ppermute | solution.py:357
  137.5 12.1 %collective-permute-start.20 = (f32[128,256]{1,0:T(8,128)S(1)}, f32[128,256]{1,0:T(8,128)S(1)}, u32[]{:S(2)}, u32[]{:S(2)}) collective-permute-start(f32[128,256]{1,0:T(8,128)S(1)} %get-tuple-element.55), channel_id=1, source_target_pairs={{0,12},{2,14},{4,0},{6,2},{8,4},{10,6},{12,8},{14,10},{1,13},{3,15... | collective-permute-start | bytes 393224 | tf_op jit(solution)/shard_map/ppermute | solution.py:357
  151.0 5.5 %collective-permute-start.22 = (f32[64,512]{1,0:T(8,128)S(1)}, f32[64,512]{1,0:T(8,128)S(1)}, u32[]{:S(2)}, u32[]{:S(2)}) collective-permute-start(f32[64,512]{1,0:T(8,128)S(1)} %bitcast.129), channel_id=1, source_target_pairs={{0,1},{1,0},{16,17},{17,16},{2,3},{3,2},{18,19},{19,18},{4,5},{5,4... | collective-permute-start | bytes 393224 | tf_op jit(solution)/shard_map/ppermute | solution.py:447
  152.1 6.5 %collective-permute-start.23 = (f32[64,512]{1,0:T(8,128)S(1)}, f32[64,512]{1,0:T(8,128)S(1)}, u32[]{:S(2)}, u32[]{:S(2)}) collective-permute-start(f32[64,512]{1,0:T(8,128)S(1)} %bitcast.130), channel_id=1, source_target_pairs={{0,16},{1,17},{16,0},{17,1},{2,18},{3,19},{18,2},{19,3},{4,20},{5,... | collective-permute-start | bytes 393224 | tf_op jit(solution)/shard_map/ppermute | solution.py:447
  152.8 7.7 %collective-permute-start.24 = (f32[64,512]{1,0:T(8,128)S(1)}, f32[64,512]{1,0:T(8,128)S(1)}, u32[]{:S(2)}, u32[]{:S(2)}) collective-permute-start(f32[64,512]{1,0:T(8,128)S(1)} %bitcast.131), channel_id=1, source_target_pairs={{0,17},{1,16},{16,1},{17,0},{2,19},{3,18},{18,3},{19,2},{4,21},{5,... | collective-permute-start | bytes 393224 | tf_op jit(solution)/shard_map/ppermute | solution.py:447
  (6 other events, 51.3 us)

commit v5 on v3

--- a/solution.py
+++ b/solution.py
@@ -233,6 +233,7 @@
 
     for c in range(chunks):
         fetch(c).start()
+    out_ref[pl.ds(0, height), :] = jnp.zeros((height, own), jnp.float32)
 
     @pl.loop(0, chunks)
     def _(c):
@@ -250,16 +251,27 @@
             right_high[there, :], right_low[there, :] = split(value.T)
         gather_slice(0, here, stride)
         split_slice(0, base, groups, stride)
+        along = pl.ds(base, groups * LANES)
+        out_ref[pl.ds(0, height), :] += three_pass(
+            left_high[0][:, along], left_low[0][:, along], right_high[along, :], right_low[along, :]
+        )
 
     stride = every + 1 - every % 2
 
-    @pl.loop(0, slices // 2)
+    def gather_whole(i, parity):
+        gather_slice(i, pl.ds(0, every), stride)
+        split_slice(parity, 0, every, stride)
+
+    gather_whole(1, 1)
+
+    @pl.loop(0, slices // 2 - 1)
     def _(index):
-        for parity in range(2):
-            multiply(2 * index + parity, parity)
-            after = jnp.minimum(2 * index + parity + 1, slices - 1)
-            gather_slice(after, pl.ds(0, every), stride)
-            split_slice(1 - parity, 0, every, stride)
+        for parity in (1, 0):
+            i = 2 * index + 2 - parity
+            multiply(i, parity)
+            gather_whole(i + 1, 1 - parity)
+
+    multiply(slices - 1, 1)
 
 
 def pair_response(turned, coulomb, occ, vir, block, shape):
@@ -375,22 +387,23 @@
         own_weights.reshape(-1)[:, None] * own_window(pair_weight)[None, :] * (1.0 / basis)
     )
     sub = window // (row_count * blocks)
-    response, part = lax.optimization_barrier((response, coupling[:sub]))
+    response, all_coupling, part = lax.optimization_barrier(
+        (response, all_coupling, coupling[:sub])
+    )
     parts = [part] + [lax.ppermute(part, "rows", shift(step)) for step in range(1, lines)]
-    parts = jnp.stack(parts)
-    beside = lax.ppermute(parts, "rows", other_core)
-    both = jnp.where(core == 0, jnp.stack([parts, beside], 1), jnp.stack([beside, parts], 1))
-    both = jnp.roll(both[::-1], line + 1, axis=0)
-    window_coupling = both.reshape(row_count * sub, bands)
-
-    matches = freq_index[:, None] == jnp.arange(freq_table.shape[0], dtype=jnp.int32)[None, :]
-    band_weight = jnp.sum(jnp.where(matches, freq_table[None, :], 0.0), axis=1)
     mixed = lax.dot_general(
         all_coupling, response, (((0,), (0,)), ((), ())),
         precision=lax.Precision.HIGH, preferred_element_type=jnp.float32,
     )
     mixed = add_cores(mixed.reshape(lines, 2, bands // row_count, -1).swapaxes(0, 1))
     mixed = scatter_lines(mixed)
+    order = lax.rem(line - jnp.arange(lines) + lines, lines)
+    parts = jnp.stack(parts)[order]
+    beside = lax.ppermute(parts, "rows", other_core)
+    pairs_of = jnp.where(core == 0, jnp.stack([parts, beside], 1), jnp.stack([beside, parts], 1))
+    window_coupling = pairs_of.reshape(row_count * sub, bands)
+    matches = freq_index[:, None] == jnp.arange(freq_table.shape[0], dtype=jnp.int32)[None, :]
+    band_weight = jnp.sum(jnp.where(matches, freq_table[None, :], 0.0), axis=1)
     energy = lax.dot_general(
         mixed, window_coupling, (((1,), (0,)), ((), ())),
         precision=lax.Precision.HIGH, preferred_element_type=jnp.float32,
@@ -401,12 +414,23 @@
         own_band_weight[:, None] * band_weight[None, :] * (1.0 / math.sqrt(window))
     )
     energy = energy.reshape(col_count, here // col_count, group_count, bands // group_count)
-    across = [(i, i ^ 1) for i in range(col_count)]
-    received = lax.ppermute(pick(energy, 1 - column), "cols", across)
-    energy = pick(energy, column) + received
-    across = [(i, i ^ 1) for i in range(group_count)]
-    received = lax.ppermute(pick(energy, 1 - group, 1), "grp", across)
-    return pick(energy, group, 1) + received
+    total = pick(pick(energy, column), group, 1)
+    for step in range(1, blocks):
+        there_group, there_column = divmod(step, col_count)
+        away_group = lax.rem(group + there_group, group_count)
+        away_column = lax.rem(column + there_column, col_count)
+        targets = [
+            (
+                i,
+                (i // col_count + there_group) % group_count * col_count
+                + (i % col_count + there_column) % col_count,
+            )
+            for i in range(blocks)
+        ]
+        total = total + lax.ppermute(
+            pick(pick(energy, away_column), away_group, 1), ("grp", "cols"), targets
+        )
+    return total
 
 
 def solution(mesh):

time: 158 us -> 151 us (0.956)
  other arithmetic: 5.55 us -> 1.94 us
  waiting for transfers between devices: 48.9 us -> 45.6 us
  local copies, waits for them, and re-layouts: 6.84 us -> 4.85 us
    ppermute x2 -> x3, waiting for transfers between devices: 11.3 us -> 5.89 us  [per_device(): lax.ppermute(pick(pick(energy, away_column), away_group, 1), ('grp', 'col...]
    ppermute x2 -> x3, starting transfers between devices: 2.1 us -> 3.68 us  [per_device(): lax.ppermute(pick(pick(energy, away_column), away_group, 1), ('grp', 'col...]
    squeeze x7 -> x6, local copies, waits for them, and re-layouts: 3.62 us -> 2.78 us  [pick(): return lax.dynamic_index_in_dim(values, index, axis, keepdims=False)]
  transfers between devices with their start and end apart: 20 -> 21, of which waited for: 15 -> 15; matrix products, arithmetic and copies ran while one was open for 5% -> 1% of each run, Pallas kernels for 26% -> 28%
where the time goes in v5:
time: 151 us; the launch traced here: 150 us
  Pallas kernels  73.4 us (49%)
  waiting for transfers between devices  45.6 us (30%)
  starting transfers between devices  22.7 us (15%)
  local copies, waits for them, and re-layouts  4.85 us (3%)
  other arithmetic  1.94 us (1%)
    pallas_call x1, Pallas kernels, pair_response(): pl.pallas_call(functools.partial(response_kernel, shape), in_specs=[scala...  41.7 us
    pallas_call x1, Pallas kernels, pair_coupling(): pl.pallas_call(functools.partial(coupling_kernel, shape), in_specs=[scala...  31.7 us
    ppermute x9, waiting for transfers between devices, scatter_lines(): lax.ppermute(pick(values, lax.rem(line + step, lines)), 'rows', shift(step))  23.9 us
    ppermute x9, starting transfers between devices, scatter_lines(): lax.ppermute(pick(values, lax.rem(line + step, lines)), 'rows', shift(step))  13.4 us
    ppermute x3, waiting for transfers between devices, per_device(): lax.ppermute(part, 'rows', shift(step))  10.5 us
    ppermute x3, waiting for transfers between devices, per_device(): lax.ppermute(pick(pick(energy, away_column), away_group, 1), ('grp', 'col...  5.89 us
    ppermute x3, waiting for transfers between devices, add_cores(): received = lax.ppermute(pick(values, 1 - core), 'rows', other_core)  3.84 us
    ppermute x3, starting transfers between devices, per_device(): lax.ppermute(pick(pick(energy, away_column), away_group, 1), ('grp', 'col...  3.68 us
  transfers between devices with their start and end apart: 21, of which 15 were waited for; matrix products, arithmetic and copies ran while one was open for 1% of the time, Pallas kernels for 28%

profile of v5, /device:TPU:8, one launch (start us, length us, event | category | flops | bytes accessed | tf_op | source)
XLA Modules:
  0.0 150.5 jit_solution(10440272337922036355)
XLA Ops:
  0.0 31.7 %coupling.1 = (f32[384,1024]{1,0:T(8,128)}, f32[6,1024,8,128]{3,2,1,0:T(8,128)}) custom-call(s32[1]{0:T(128)} %bitcast.block_ref, s32[1536]{0:T(1024)} %occ_ref.3, s32[1536]{0:T(1024)} %vir_ref.3, f32[48,128]{1,0:T(8,128)} %bitcast.119, f32[6144,1024]{1,0:T(8,128)} %band_ref.1), custom_call_target="tpu_custom_call" | custom-call | flops 14495514624 | bytes 50331648 | tf_op jit(solution)/shard_map/coupling/pallas_call | solution.py:155
  31.8 1.3 dynamic-slice_bitcast_fusion.1
  33.2 2.2 %collective-permute-done = f32[4,48,1024]{2,1,0:T(8,128)S(1)} collective-permute-done((f32[4,48,1024]{2,1,0:T(8,128)S(1)}, f32[4,48,1024]{2,1,0:T(8,128)S(1)}, u32[]{:S(2)}, u32[]{:S(2)}) %collective-permute-start) | collective-permute-done | bytes 786464 | tf_op jit(solution)/shard_map/ppermute | solution.py:346
  35.6 1.6 %collective-permute-start.1 = (f32[48,1024]{1,0:T(8,128)S(1)}, f32[48,1024]{1,0:T(8,128)S(1)}, u32[]{:S(2)}, u32[]{:S(2)}) collective-permute-start(f32[48,1024]{1,0:T(8,128)S(1)} %get-tuple-element.30), channel_id=1, source_target_pairs={{0,4},{2,6},{4,8},{6,10},{8,12},{10,14},{12,0},{14,2},{1,5},{3,7},... | collective-permute-start | bytes 589832 | tf_op jit(solution)/shard_map/ppermute | solution.py:351
  38.3 1.9 %collective-permute-start.3 = (f32[48,1024]{1,0:T(8,128)S(1)}, f32[48,1024]{1,0:T(8,128)S(1)}, u32[]{:S(2)}, u32[]{:S(2)}) collective-permute-start(f32[48,1024]{1,0:T(8,128)S(1)} %get-tuple-element.31), channel_id=1, source_target_pairs={{0,12},{2,14},{4,0},{6,2},{8,4},{10,6},{12,8},{14,10},{1,13},{3,15... | collective-permute-start | bytes 589832 | tf_op jit(solution)/shard_map/ppermute | solution.py:351
  40.3 41.7 %response.1 = f32[1536,256]{1,0:T(8,128)} custom-call(s32[1]{0:T(128)} %bitcast.block_ref, s32[1536]{0:T(1024)} %occ_ref.3, s32[1536]{0:T(1024)} %vir_ref.3, f32[48,128]{1,0:T(8,128)} %bitcast.120, f32[6,1024,8,128]{3,2,1,0:T(8,128)} %get-tuple-element.18.turned_ref), custom_call_target="tpu_custom_call" | custom-call | flops 14495514624 | bytes 25165824 | tf_op jit(solution)/shard_map/response/pallas_call | solution.py:289
  84.1 1.6 %collective-permute-done.4 = f32[4,192,256]{2,1,0:T(8,128)S(1)} collective-permute-done((f32[4,192,256]{2,1,0:T(8,128)S(1)}, f32[4,192,256]{2,1,0:T(8,128)S(1)}, u32[]{:S(2)}, u32[]{:S(2)}) %collective-permute-start.4) | collective-permute-done | bytes 786464 | tf_op jit(solution)/shard_map/ppermute | solution.py:346
  85.9 1.6 %collective-permute-start.8 = (f32[48,1024]{1,0:T(8,128)S(1)}, f32[48,1024]{1,0:T(8,128)S(1)}, u32[]{:S(2)}, u32[]{:S(2)}) collective-permute-start(f32[48,1024]{1,0:T(8,128)S(1)} %broadcast_multiply_fusion), channel_id=1, source_target_pairs={{0,1},{1,0},{2,3},{3,2},{4,5},{5,4},{6,7},{7,6},{8,9},{9,8},{10,11... | collective-permute-start | bytes 589832 | tf_op jit(solution)/shard_map/ppermute | solution.py:361
  87.8 3.5 %collective-permute-start.6 = (f32[192,256]{1,0:T(8,128)S(1)}, f32[192,256]{1,0:T(8,128)S(1)}, u32[]{:S(2)}, u32[]{:S(2)}) collective-permute-start(f32[192,256]{1,0:T(8,128)S(1)} %get-tuple-element.29), channel_id=1, source_target_pairs={{0,8},{2,10},{4,12},{6,14},{8,0},{10,2},{12,4},{14,6},{1,9},{3,11}... | collective-permute-start | bytes 589832 | tf_op jit(solution)/shard_map/ppermute | solution.py:351
  91.4 1.5 collective-permute-done.8
  93.0 1.6 %collective-permute-start.9 = (f32[2,48,1024]{2,1,0:T(8,128)S(1)}, f32[2,48,1024]{2,1,0:T(8,128)S(1)}, u32[]{:S(2)}, u32[]{:S(2)}) collective-permute-start(f32[2,48,1024]{2,1,0:T(8,128)S(1)} %reverse_select_fusion.1), channel_id=1, source_target_pairs={{0,16},{16,0},{1,17},{17,1},{2,18},{18,2},{3,19},{19,3},{4,20},{20... | collective-permute-start | bytes 1179656 | tf_op jit(solution)/shard_map/ppermute | solution.py:364
  95.4 9.3 %collective-permute-done.6 = f32[192,256]{1,0:T(8,128)S(1)} collective-permute-done((f32[192,256]{1,0:T(8,128)S(1)}, f32[192,256]{1,0:T(8,128)S(1)}, u32[]{:S(2)}, u32[]{:S(2)}) %collective-permute-start.6) | collective-permute-done | bytes 196640 | tf_op jit(solution)/shard_map/ppermute | solution.py:351
  104.7 3.4 %collective-permute-done.7 = f32[192,256]{1,0:T(8,128)S(1)} collective-permute-done((f32[192,256]{1,0:T(8,128)S(1)}, f32[192,256]{1,0:T(8,128)S(1)}, u32[]{:S(2)}, u32[]{:S(2)}) %collective-permute-start.7) | collective-permute-done | bytes 196640 | tf_op jit(solution)/shard_map/ppermute | solution.py:351
  109.9 1.8 %collective-permute-start.16 = (f32[32,1024]{1,0:T(8,128)S(1)}, f32[32,1024]{1,0:T(8,128)S(1)}, u32[]{:S(2)}, u32[]{:S(2)}) collective-permute-start(f32[32,1024]{1,0:T(8,128)S(1)} %slice.39), channel_id=1, source_target_pairs={{0,12},{2,14},{4,0},{6,2},{8,4},{10,6},{12,8},{14,10},{1,13},{3,15... | collective-permute-start | bytes 393224 | tf_op jit(solution)/shard_map/ppermute | solution.py:393
  111.7 4.2 %collective-permute-done.14 = f32[32,1024]{1,0:T(8,128)S(1)} collective-permute-done((f32[32,1024]{1,0:T(8,128)S(1)}, f32[32,1024]{1,0:T(8,128)S(1)}, u32[]{:S(2)}, u32[]{:S(2)}) %collective-permute-start.14) | collective-permute-done | bytes 131104 | tf_op jit(solution)/shard_map/ppermute | solution.py:393
  115.9 5.8 %collective-permute-done.15 = f32[32,1024]{1,0:T(8,128)S(1)} collective-permute-done((f32[32,1024]{1,0:T(8,128)S(1)}, f32[32,1024]{1,0:T(8,128)S(1)}, u32[]{:S(2)}, u32[]{:S(2)}) %collective-permute-start.15) | collective-permute-done | bytes 131104 | tf_op jit(solution)/shard_map/ppermute | solution.py:393
  123.3 3.0 %collective-permute-start.12 = (f32[128,256]{1,0:T(8,128)S(1)}, f32[128,256]{1,0:T(8,128)S(1)}, u32[]{:S(2)}, u32[]{:S(2)}) collective-permute-start(f32[128,256]{1,0:T(8,128)S(1)} %get-tuple-element.39), channel_id=1, source_target_pairs={{0,8},{2,10},{4,12},{6,14},{8,0},{10,2},{12,4},{14,6},{1,9},{3,11}... | collective-permute-start | bytes 393224 | tf_op jit(solution)/shard_map/ppermute | solution.py:351
  126.3 1.9 %collective-permute-start.13 = (f32[128,256]{1,0:T(8,128)S(1)}, f32[128,256]{1,0:T(8,128)S(1)}, u32[]{:S(2)}, u32[]{:S(2)}) collective-permute-start(f32[128,256]{1,0:T(8,128)S(1)} %get-tuple-element.38), channel_id=1, source_target_pairs={{0,12},{2,14},{4,0},{6,2},{8,4},{10,6},{12,8},{14,10},{1,13},{3,15... | collective-permute-start | bytes 393224 | tf_op jit(solution)/shard_map/ppermute | solution.py:351
  129.2 6.2 %collective-permute-done.12 = f32[128,256]{1,0:T(8,128)S(1)} collective-permute-done((f32[128,256]{1,0:T(8,128)S(1)}, f32[128,256]{1,0:T(8,128)S(1)}, u32[]{:S(2)}, u32[]{:S(2)}) %collective-permute-start.12) | collective-permute-done | bytes 131104 | tf_op jit(solution)/shard_map/ppermute | solution.py:351
  135.4 3.4 %collective-permute-done.13 = f32[128,256]{1,0:T(8,128)S(1)} collective-permute-done((f32[128,256]{1,0:T(8,128)S(1)}, f32[128,256]{1,0:T(8,128)S(1)}, u32[]{:S(2)}, u32[]{:S(2)}) %collective-permute-start.13) | collective-permute-done | bytes 131104 | tf_op jit(solution)/shard_map/ppermute | solution.py:351
  140.8 1.6 %collective-permute-start.19 = (f32[64,512]{1,0:T(8,128)S(1)}, f32[64,512]{1,0:T(8,128)S(1)}, u32[]{:S(2)}, u32[]{:S(2)}) collective-permute-start(f32[64,512]{1,0:T(8,128)S(1)} %bitcast.114), channel_id=1, source_target_pairs={{0,16},{1,17},{16,0},{17,1},{2,18},{3,19},{18,2},{19,3},{4,20},{5,... | collective-permute-start | bytes 393224 | tf_op jit(solution)/shard_map/ppermute | solution.py:430
  142.3 1.6 %collective-permute-start.20 = (f32[64,512]{1,0:T(8,128)S(1)}, f32[64,512]{1,0:T(8,128)S(1)}, u32[]{:S(2)}, u32[]{:S(2)}) collective-permute-start(f32[64,512]{1,0:T(8,128)S(1)} %bitcast.115), channel_id=1, source_target_pairs={{0,17},{1,16},{16,1},{17,0},{2,19},{3,18},{18,3},{19,2},{4,21},{5,... | collective-permute-start | bytes 393224 | tf_op jit(solution)/shard_map/ppermute | solution.py:430
  143.9 1.8 %collective-permute-done.18 = f32[64,512]{1,0:T(8,128)S(1)} collective-permute-done((f32[64,512]{1,0:T(8,128)S(1)}, f32[64,512]{1,0:T(8,128)S(1)}, u32[]{:S(2)}, u32[]{:S(2)}) %collective-permute-start.18) | collective-permute-done | bytes 131104 | tf_op jit(solution)/shard_map/ppermute | solution.py:430
  146.6 3.2 %collective-permute-done.20 = f32[64,512]{1,0:T(8,128)S(1)} collective-permute-done((f32[64,512]{1,0:T(8,128)S(1)}, f32[64,512]{1,0:T(8,128)S(1)}, u32[]{:S(2)}, u32[]{:S(2)}) %collective-permute-start.20) | collective-permute-done | bytes 131104 | tf_op jit(solution)/shard_map/ppermute | solution.py:430
  (74 shorter events, 12.5 us)
Async XLA Ops:
  33.1 2.4 %collective-permute-start = (f32[4,48,1024]{2,1,0:T(8,128)S(1)}, f32[4,48,1024]{2,1,0:T(8,128)S(1)}, u32[]{:S(2)}, u32[]{:S(2)}) collective-permute-start(f32[4,48,1024]{2,1,0:T(8,128)S(1)} %dynamic-slice_bitcast_fusion.1), channel_id=1, source_target_pairs={{0,2},{2,0},{4,6},{6,4},{8,10},{10,8},{12,14},{14,12},{1,3},{3,1},... | collective-permute-start | bytes 2359304 | tf_op jit(solution)/shard_map/ppermute | solution.py:346
  35.6 46.3 %collective-permute-start.1 = (f32[48,1024]{1,0:T(8,128)S(1)}, f32[48,1024]{1,0:T(8,128)S(1)}, u32[]{:S(2)}, u32[]{:S(2)}) collective-permute-start(f32[48,1024]{1,0:T(8,128)S(1)} %get-tuple-element.30), channel_id=1, source_target_pairs={{0,4},{2,6},{4,8},{6,10},{8,12},{10,14},{12,0},{14,2},{1,5},{3,7},... | collective-permute-start | bytes 589832 | tf_op jit(solution)/shard_map/ppermute | solution.py:351
  37.2 44.7 %collective-permute-start.2 = (f32[48,1024]{1,0:T(8,128)S(1)}, f32[48,1024]{1,0:T(8,128)S(1)}, u32[]{:S(2)}, u32[]{:S(2)}) collective-permute-start(f32[48,1024]{1,0:T(8,128)S(1)} %get-tuple-element.32), channel_id=1, source_target_pairs={{0,8},{2,10},{4,12},{6,14},{8,0},{10,2},{12,4},{14,6},{1,9},{3,11}... | collective-permute-start | bytes 589832 | tf_op jit(solution)/shard_map/ppermute | solution.py:351
  38.3 43.7 %collective-permute-start.3 = (f32[48,1024]{1,0:T(8,128)S(1)}, f32[48,1024]{1,0:T(8,128)S(1)}, u32[]{:S(2)}, u32[]{:S(2)}) collective-permute-start(f32[48,1024]{1,0:T(8,128)S(1)} %get-tuple-element.31), channel_id=1, source_target_pairs={{0,12},{2,14},{4,0},{6,2},{8,4},{10,6},{12,8},{14,10},{1,13},{3,15... | collective-permute-start | bytes 589832 | tf_op jit(solution)/shard_map/ppermute | solution.py:351
  82.0 3.7 %copy-start.1 = (f32[1536,256]{1,0:T(8,128)S(1)}, f32[1536,256]{1,0:T(8,128)}, u32[]{:S(2)}) copy-start(f32[1536,256]{1,0:T(8,128)} %response.1) | copy-start | bytes 4718596
  83.3 2.4 %collective-permute-start.4 = (f32[4,192,256]{2,1,0:T(8,128)S(1)}, f32[4,192,256]{2,1,0:T(8,128)S(1)}, u32[]{:S(2)}, u32[]{:S(2)}) collective-permute-start(f32[4,192,256]{2,1,0:T(8,128)S(1)} %dynamic-slice_bitcast_fusion), channel_id=1, source_target_pairs={{0,2},{2,0},{4,6},{6,4},{8,10},{10,8},{12,14},{14,12},{1,3},{3,1},... | collective-permute-start | bytes 2359304 | tf_op jit(solution)/shard_map/ppermute | solution.py:346
  85.9 7.0 %collective-permute-start.8 = (f32[48,1024]{1,0:T(8,128)S(1)}, f32[48,1024]{1,0:T(8,128)S(1)}, u32[]{:S(2)}, u32[]{:S(2)}) collective-permute-start(f32[48,1024]{1,0:T(8,128)S(1)} %broadcast_multiply_fusion), channel_id=1, source_target_pairs={{0,1},{1,0},{2,3},{3,2},{4,5},{5,4},{6,7},{7,6},{8,9},{9,8},{10,11... | collective-permute-start | bytes 589832 | tf_op jit(solution)/shard_map/ppermute | solution.py:361
  87.6 7.8 %collective-permute-start.5 = (f32[192,256]{1,0:T(8,128)S(1)}, f32[192,256]{1,0:T(8,128)S(1)}, u32[]{:S(2)}, u32[]{:S(2)}) collective-permute-start(f32[192,256]{1,0:T(8,128)S(1)} %get-tuple-element.27), channel_id=1, source_target_pairs={{0,4},{2,6},{4,8},{6,10},{8,12},{10,14},{12,0},{14,2},{1,5},{3,7},... | collective-permute-start | bytes 589832 | tf_op jit(solution)/shard_map/ppermute | solution.py:351
  87.8 16.9 %collective-permute-start.6 = (f32[192,256]{1,0:T(8,128)S(1)}, f32[192,256]{1,0:T(8,128)S(1)}, u32[]{:S(2)}, u32[]{:S(2)}) collective-permute-start(f32[192,256]{1,0:T(8,128)S(1)} %get-tuple-element.29), channel_id=1, source_target_pairs={{0,8},{2,10},{4,12},{6,14},{8,0},{10,2},{12,4},{14,6},{1,9},{3,11}... | collective-permute-start | bytes 589832 | tf_op jit(solution)/shard_map/ppermute | solution.py:351
  91.3 16.8 %collective-permute-start.7 = (f32[192,256]{1,0:T(8,128)S(1)}, f32[192,256]{1,0:T(8,128)S(1)}, u32[]{:S(2)}, u32[]{:S(2)}) collective-permute-start(f32[192,256]{1,0:T(8,128)S(1)} %get-tuple-element.28), channel_id=1, source_target_pairs={{0,12},{2,14},{4,0},{6,2},{8,4},{10,6},{12,8},{14,10},{1,13},{3,15... | collective-permute-start | bytes 589832 | tf_op jit(solution)/shard_map/ppermute | solution.py:351
  93.0 15.3 %collective-permute-start.9 = (f32[2,48,1024]{2,1,0:T(8,128)S(1)}, f32[2,48,1024]{2,1,0:T(8,128)S(1)}, u32[]{:S(2)}, u32[]{:S(2)}) collective-permute-start(f32[2,48,1024]{2,1,0:T(8,128)S(1)} %reverse_select_fusion.1), channel_id=1, source_target_pairs={{0,16},{16,0},{1,17},{17,1},{2,18},{18,2},{3,19},{19,3},{4,20},{20... | collective-permute-start | bytes 1179656 | tf_op jit(solution)/shard_map/ppermute | solution.py:364
  109.4 13.5 %copy-start.3 = (s32[1024]{0:T(1024)S(1)}, s32[1024]{0:T(1024)}, u32[]{:S(2)}) copy-start(s32[1024]{0:T(1024)} %param.12) | copy-start | bytes 12292
  109.4 13.5 %copy-start.4 = (f32[16]{0:T(128)S(1)}, f32[16]{0:T(128)}, u32[]{:S(2)}) copy-start(f32[16]{0:T(128)} %param.13) | copy-start | bytes 196
  109.5 13.6 %collective-permute-start.10 = (f32[4,128,256]{2,1,0:T(8,128)S(1)}, f32[4,128,256]{2,1,0:T(8,128)S(1)}, u32[]{:S(2)}, u32[]{:S(2)}) collective-permute-start(f32[4,128,256]{2,1,0:T(8,128)S(1)} %dynamic-slice_bitcast_fusion.2), channel_id=1, source_target_pairs={{0,2},{2,0},{4,6},{6,4},{8,10},{10,8},{12,14},{14,12},{1,3},{3,1},... | collective-permute-start | bytes 1572872 | tf_op jit(solution)/shard_map/ppermute | solution.py:346
  109.6 6.3 %collective-permute-start.14 = (f32[32,1024]{1,0:T(8,128)S(1)}, f32[32,1024]{1,0:T(8,128)S(1)}, u32[]{:S(2)}, u32[]{:S(2)}) collective-permute-start(f32[32,1024]{1,0:T(8,128)S(1)} %slice.39), channel_id=1, source_target_pairs={{0,4},{2,6},{4,8},{6,10},{8,12},{10,14},{12,0},{14,2},{1,5},{3,7},... | collective-permute-start | bytes 393224 | tf_op jit(solution)/shard_map/ppermute | solution.py:393
  109.7 12.1 %collective-permute-start.15 = (f32[32,1024]{1,0:T(8,128)S(1)}, f32[32,1024]{1,0:T(8,128)S(1)}, u32[]{:S(2)}, u32[]{:S(2)}) collective-permute-start(f32[32,1024]{1,0:T(8,128)S(1)} %slice.39), channel_id=1, source_target_pairs={{0,8},{2,10},{4,12},{6,14},{8,0},{10,2},{12,4},{14,6},{1,9},{3,11}... | collective-permute-start | bytes 393224 | tf_op jit(solution)/shard_map/ppermute | solution.py:393
  109.9 12.2 %collective-permute-start.16 = (f32[32,1024]{1,0:T(8,128)S(1)}, f32[32,1024]{1,0:T(8,128)S(1)}, u32[]{:S(2)}, u32[]{:S(2)}) collective-permute-start(f32[32,1024]{1,0:T(8,128)S(1)} %slice.39), channel_id=1, source_target_pairs={{0,12},{2,14},{4,0},{6,2},{8,4},{10,6},{12,8},{14,10},{1,13},{3,15... | collective-permute-start | bytes 393224 | tf_op jit(solution)/shard_map/ppermute | solution.py:393
  122.8 5.5 %collective-permute-start.17 = (f32[4,32,1024]{2,1,0:T(8,128)S(1)}, f32[4,32,1024]{2,1,0:T(8,128)S(1)}, u32[]{:S(2)}, u32[]{:S(2)}) collective-permute-start(f32[4,32,1024]{2,1,0:T(8,128)S(1)} %gather_fusion), channel_id=1, source_target_pairs={{0,2},{2,0},{4,6},{6,4},{8,10},{10,8},{12,14},{14,12},{1,3},{3,1},... | collective-permute-start | bytes 1572872 | tf_op jit(solution)/shard_map/ppermute | solution.py:402
  123.2 6.0 %collective-permute-start.11 = (f32[128,256]{1,0:T(8,128)S(1)}, f32[128,256]{1,0:T(8,128)S(1)}, u32[]{:S(2)}, u32[]{:S(2)}) collective-permute-start(f32[128,256]{1,0:T(8,128)S(1)} %get-tuple-element.37), channel_id=1, source_target_pairs={{0,4},{2,6},{4,8},{6,10},{8,12},{10,14},{12,0},{14,2},{1,5},{3,7},... | collective-permute-start | bytes 393224 | tf_op jit(solution)/shard_map/ppermute | solution.py:351
  123.3 12.1 %collective-permute-start.12 = (f32[128,256]{1,0:T(8,128)S(1)}, f32[128,256]{1,0:T(8,128)S(1)}, u32[]{:S(2)}, u32[]{:S(2)}) collective-permute-start(f32[128,256]{1,0:T(8,128)S(1)} %get-tuple-element.39), channel_id=1, source_target_pairs={{0,8},{2,10},{4,12},{6,14},{8,0},{10,2},{12,4},{14,6},{1,9},{3,11}... | collective-permute-start | bytes 393224 | tf_op jit(solution)/shard_map/ppermute | solution.py:351
  126.3 12.4 %collective-permute-start.13 = (f32[128,256]{1,0:T(8,128)S(1)}, f32[128,256]{1,0:T(8,128)S(1)}, u32[]{:S(2)}, u32[]{:S(2)}) collective-permute-start(f32[128,256]{1,0:T(8,128)S(1)} %get-tuple-element.38), channel_id=1, source_target_pairs={{0,12},{2,14},{4,0},{6,2},{8,4},{10,6},{12,8},{14,10},{1,13},{3,15... | collective-permute-start | bytes 393224 | tf_op jit(solution)/shard_map/ppermute | solution.py:351
  140.2 5.5 %collective-permute-start.18 = (f32[64,512]{1,0:T(8,128)S(1)}, f32[64,512]{1,0:T(8,128)S(1)}, u32[]{:S(2)}, u32[]{:S(2)}) collective-permute-start(f32[64,512]{1,0:T(8,128)S(1)} %bitcast.113), channel_id=1, source_target_pairs={{0,1},{1,0},{16,17},{17,16},{2,3},{3,2},{18,19},{19,18},{4,5},{5,4... | collective-permute-start | bytes 393224 | tf_op jit(solution)/shard_map/ppermute | solution.py:430
  140.8 5.8 %collective-permute-start.19 = (f32[64,512]{1,0:T(8,128)S(1)}, f32[64,512]{1,0:T(8,128)S(1)}, u32[]{:S(2)}, u32[]{:S(2)}) collective-permute-start(f32[64,512]{1,0:T(8,128)S(1)} %bitcast.114), channel_id=1, source_target_pairs={{0,16},{1,17},{16,0},{17,1},{2,18},{3,19},{18,2},{19,3},{4,20},{5,... | collective-permute-start | bytes 393224 | tf_op jit(solution)/shard_map/ppermute | solution.py:430
  142.3 7.4 %collective-permute-start.20 = (f32[64,512]{1,0:T(8,128)S(1)}, f32[64,512]{1,0:T(8,128)S(1)}, u32[]{:S(2)}, u32[]{:S(2)}) collective-permute-start(f32[64,512]{1,0:T(8,128)S(1)} %bitcast.115), channel_id=1, source_target_pairs={{0,17},{1,16},{16,1},{17,0},{2,19},{3,18},{18,3},{19,2},{4,21},{5,... | collective-permute-start | bytes 393224 | tf_op jit(solution)/shard_map/ppermute | solution.py:430
  (2 other events, 5.2 us)
